TPU v7x, 512 devices: a whole 4x4x16 slice. The times are simulated.
512 devices in a mesh: gx: 64 (over x_hi, z, core), gy: 8 (over y, x_lo).
Axes of the slice: x: 4 (x_hi: 2, x_lo: 2; x = x_hi * 2 + x_lo), y: 4, z: 16, core: 2. Of those that a mesh axis runs over, the one named last changes fastest.
Arguments:
- flow_populations: float32 [19, 128, 16, 1024], P(None, 'gx', None, 'gy'), as said below
- heat_populations: float32 [7, 128, 16, 1024], P(None, 'gx', None, 'gy'), as said below
- flow_weight: float32 [3, 128, 16, 1024], P(None, 'gx', None, 'gy'), may hold values from -48 to 48
- heat_weight: float32 [128, 16, 1024], P('gx', None, 'gy'), may hold values from -192 to 192
- resistance: float32 [128, 16, 1024], P('gx', None, 'gy'), may hold values from 0.05 to 2
- conductivity: float32 [128, 16, 1024], P('gx', None, 'gy'), may hold values from 0.5 to 2
- solid_mask: int32 [128, 16, 1024], P('gx', None, 'gy'), may hold values 0 or 1
Outputs:
- resistance_sensitivity: float32 [128, 16, 1024], P('gx', None, 'gy')
- conductivity_sensitivity: float32 [128, 16, 1024], P('gx', None, 'gy')
Inputs may be any that keep to these rules, and one draw needn't show every extreme that they name: `solid_mask`: 1 marks a solid voxel, 0 a fluid one. `flow_populations`: positive. `heat_populations`: positive.
All inputs are finite; a program needn't handle non-finite values. No bound on the sum of `solid_mask` on one device may be relied on, other than what follows from the above.
Results may differ from a plain program's by a relative error of at most 0.0003.
Values sent between devices are 32-bit elements; how exact they have to be, the bound alone decides.
No kernel may reach another device: no remote copies, remote signals or barrier semaphores. Data moves between devices by JAX's collectives and lax.ppermute only.
A program may use at most 64 MiB of HBM per device.

v0:
```python
import jax
import jax.numpy as jnp
import numpy as np
from jax import lax
from jax.sharding import PartitionSpec as P

STEPS = 3


GHOST_RATE = 1.2
HEAT_RATE = 1.4


def with_halo(block, sides, width):
    for axis, dim in sides:
        count = lax.axis_size(axis)
        forward = [(i, i + 1) for i in range(count - 1)]
        forward.append((count - 1, 0))
        backward = [(target, source) for source, target in forward]
        low = lax.ppermute(
            lax.slice_in_dim(block, block.shape[dim] - width, None, axis=dim), axis, forward
        )
        high = lax.ppermute(lax.slice_in_dim(block, 0, width, axis=dim), axis, backward)
        block = jnp.concatenate([low, block, high], axis=dim)
    return block


def lattice_tables():
    velocity = np.array(
        [
            [0, 0, 0],
            [1, 0, 0],
            [-1, 0, 0],
            [0, 1, 0],
            [0, -1, 0],
            [0, 0, 1],
            [0, 0, -1],
            [1, 1, 0],
            [-1, -1, 0],
            [1, -1, 0],
            [-1, 1, 0],
            [1, 0, 1],
            [-1, 0, -1],
            [1, 0, -1],
            [-1, 0, 1],
            [0, 1, 1],
            [0, -1, -1],
            [0, 1, -1],
            [0, -1, 1],
        ],
        np.int64,
    )
    weights = np.array([1.0 / 3.0] + [1.0 / 18.0] * 6 + [1.0 / 36.0] * 12, np.float32)
    energy_stencil_factors = np.array([0.25] + [0.125] * 6, np.float32)
    dot_table = (velocity @ velocity.T).astype(np.float32)
    lengths = np.sum(velocity * velocity, axis=1).astype(np.float32)
    stress_map = (4.5 * weights[:, None] * (dot_table * dot_table - lengths[None, :] / 3.0)).astype(
        np.float32
    )
    flux_map = (4.0 * energy_stencil_factors[:, None] * dot_table[:7, :7]).astype(np.float32)
    opposite = np.array([0, 2, 1, 4, 3, 6, 5, 8, 7, 10, 9, 12, 11, 14, 13, 16, 15, 18, 17])
    return (velocity, weights, energy_stencil_factors, stress_map, flux_map, opposite)


def full_velocity():
    velocity = lattice_tables()[0]
    return np.concatenate([velocity, velocity[:7]], axis=0)


def collide(flow_part, energy_share, resistance, conductivity, solid_cells):
    velocity, weights, energy_stencil_factors, stress_map, flux_map, opposite = lattice_tables()
    highest = lax.Precision.HIGHEST
    vel_float = velocity.astype(np.float32)
    momentum = jnp.einsum("qa,qxzy->axzy", vel_float, flow_part, precision=highest)
    density = jnp.sum(flow_part, axis=0)
    warmth_grid = jnp.sum(energy_share, axis=0)
    fluid_cells = 1.0 - solid_cells
    velocity_field = momentum * (fluid_cells / (1.0 + resistance))
    chosen_heading = jnp.einsum("qa,axzy->qxzy", vel_float, velocity_field, precision=highest)
    kinetic = jnp.sum(velocity_field * velocity_field, axis=0)
    equilibrium = weights[:, None, None, None] * (
        density + 3.0 * chosen_heading + 4.5 * chosen_heading * chosen_heading - 1.5 * kinetic
    )
    excess = flow_part - equilibrium
    stress = jnp.einsum("iq,qxzy->ixzy", stress_map, excess, precision=highest)
    momentum_diffusivity = 0.1 * jnp.exp(-2.0 * (warmth_grid - 1.0))
    shear_rate = 1.0 / (0.5 + 3.0 * momentum_diffusivity)
    relaxed = equilibrium + (1.0 - shear_rate) * stress + (1.0 - GHOST_RATE) * (excess - stress)
    bounced = flow_part[opposite]
    flow_post = solid_cells * bounced + fluid_cells * relaxed
    energy_balanced_populations = (
        energy_stencil_factors[:, None, None, None] * warmth_grid * (1.0 + 4.0 * chosen_heading[:7])
    )
    heat_excess = energy_share - energy_balanced_populations
    heat_flux = jnp.einsum("iq,qxzy->ixzy", flux_map, heat_excess, precision=highest)
    flux_rate = 1.0 / (0.5 + 0.4 * conductivity)
    heat_post = (
        energy_balanced_populations
        + (1.0 - flux_rate) * heat_flux
        + (1.0 - HEAT_RATE) * (heat_excess - heat_flux)
    )
    return (flow_post, heat_post)


def stream_rims(lattice_state, velocity_table):
    members_total = velocity_table.shape[0]
    padded = with_halo(lattice_state, (("gx", 1), ("gy", 3)), 1)
    width_x = lattice_state.shape[1]
    width_y = lattice_state.shape[3]
    shifted = []
    for member in range(members_total):
        step_x, step_y, step_z = (int(entry_value) for entry_value in velocity_table[member])
        window_cells = padded[
            member, 1 - step_x : 1 - step_x + width_x, :, 1 - step_y : 1 - step_y + width_y
        ]
        shifted.append(jnp.roll(window_cells, step_z, axis=1))
    return jnp.stack(shifted)


def stream_table(lattice_state, velocity_table):
    result_state = stream_rims(lattice_state, velocity_table)
    return result_state


def stream(lattice_state, direction):
    return stream_table(lattice_state, full_velocity() * direction)


def objective_seed(flow_weight, heat_weight):
    vel_float = lattice_tables()[0].astype(np.float32)
    flow_seed = jnp.einsum("qa,axzy->qxzy", vel_float, flow_weight, precision=lax.Precision.HIGHEST)
    heat_seed = jnp.broadcast_to(heat_weight[None], (7,) + heat_weight.shape)
    return jnp.concatenate([flow_seed, heat_seed], axis=0)


def on_device(
    flow_populations,
    heat_populations,
    flow_weight,
    heat_weight,
    resistance,
    conductivity,
    solid_mask,
):
    solid_cells = solid_mask.astype(jnp.float32)
    initial = jnp.concatenate([flow_populations, heat_populations], axis=0)

    def local_step(flow_part, energy_share, resist_field, conduct_field):
        return collide(flow_part, energy_share, resist_field, conduct_field, solid_cells)

    adjoint = objective_seed(flow_weight, heat_weight)
    resistance_sensitivity = jnp.zeros_like(resistance)
    conductivity_sensitivity = jnp.zeros_like(conductivity)
    history = [initial]
    for section_index in range(STEPS - 1):
        lattice_state = history[-1]
        flow_post, heat_post = collide(
            lattice_state[:19], lattice_state[19:], resistance, conductivity, solid_cells
        )
        history.append(stream(jnp.concatenate([flow_post, heat_post], axis=0), 1))
    for section_index in reversed(range(STEPS)):
        arrived = stream(adjoint, -1)
        saved_state = history[section_index]
        unused, pullback = jax.vjp(
            local_step, saved_state[:19], saved_state[19:], resistance, conductivity
        )
        flow_back, heat_back, resist_back, conduct_back = pullback((arrived[:19], arrived[19:]))
        adjoint, resist_back, conduct_back = (
            jnp.concatenate([flow_back, heat_back], axis=0),
            resist_back,
            conduct_back,
        )
        resistance_sensitivity = resistance_sensitivity + resist_back
        conductivity_sensitivity = conductivity_sensitivity + conduct_back
    return (resistance_sensitivity, conductivity_sensitivity)


def solution(mesh):
    placed = (
        P(None, "gx", None, "gy"),
        P(None, "gx", None, "gy"),
        P(None, "gx", None, "gy"),
        P("gx", None, "gy"),
        P("gx", None, "gy"),
        P("gx", None, "gy"),
        P("gx", None, "gy"),
    )
    return jax.shard_map(
        on_device,
        mesh=mesh,
        in_specs=placed,
        out_specs=(P("gx", None, "gy"), P("gx", None, "gy")),
        check_vma=False,
    )
```

profile of v0, /device:TPU:4, one launch (start us, length us, event | category | flops | bytes accessed | tf_op | source)
XLA Modules:
  0.0 216.2 jit_solution(4477928601921407214)
XLA Ops:
  2.8 2.1 collective-permute-start.9
  4.9 10.8 %collective-permute-start.8 = (f32[26,1,16,128]{3,2,1,0:T(8,128)S(1)}, f32[26,1,16,128]{3,2,1,0:T(8,128)S(1)}, u32[]{:S(2)}, u32[]{:S(2)}) collective-permute-start(f32[26,1,16,128]{3,2,1,0:T(8,128)S(1)} %get-tuple-element.147), channel_id=1, source_target_pairs={{8,0},{16,8},{24,16},{32,24},{40,32},{48,40},{56,48},{64,56},{72,6... | collective-permute-start | bytes 638984 | tf_op jit(solution)/shard_map/ppermute | solution.py:23
  24.3 1.9 collective-permute-start
  26.2 7.3 %collective-permute-start.1 = (f32[26,1,16,128]{3,2,1,0:T(8,128)}, f32[26,1,16,128]{3,2,1,0:T(8,128)S(1)}, u32[]{:S(2)}, u32[]{:S(2)}) collective-permute-start(f32[26,1,16,128]{3,2,1,0:T(8,128)} %get-tuple-element.145), channel_id=1, source_target_pairs={{8,0},{16,8},{24,16},{32,24},{40,32},{48,40},{56,48},{64,56},{72,6... | collective-permute-start | bytes 638984 | tf_op jit(solution)/shard_map/ppermute | solution.py:23
  36.2 1.3 copy.793
  37.5 1.3 copy.791
  38.8 6.4 %collective-permute-start.10 = (f32[26,4,16,1]{0,2,3,1:T(8,128)}, f32[26,4,16,1]{0,2,3,1:T(8,128)}, u32[]{:S(2)}, u32[]{:S(2)}) collective-permute-start(f32[26,4,16,1]{0,2,3,1:T(8,128)} %copy.791), channel_id=1, source_target_pairs={{1,0},{2,1},{3,2},{4,3},{5,4},{6,5},{7,6},{0,7},{9,8},{10,9},{11,1... | collective-permute-start | bytes 19976 | tf_op jit(solution)/shard_map/ppermute | solution.py:23
  45.2 1.9 collective-permute-start.11
  47.5 1.3 copy.766
  48.8 1.3 copy.768
  50.1 6.0 %collective-permute-start.3 = (f32[26,4,16,1]{0,2,3,1:T(8,128)}, f32[26,4,16,1]{0,2,3,1:T(8,128)}, u32[]{:S(2)}, u32[]{:S(2)}) collective-permute-start(f32[26,4,16,1]{0,2,3,1:T(8,128)} %copy.768), channel_id=1, source_target_pairs={{1,0},{2,1},{3,2},{4,3},{5,4},{6,5},{7,6},{0,7},{9,8},{10,9},{11,1... | collective-permute-start | bytes 19976 | tf_op jit(solution)/shard_map/ppermute | solution.py:23
  56.1 2.1 collective-permute-start.2
  59.4 1.6 copy.794
  61.1 1.6 copy.792
  67.4 1.6 copy.767
  75.5 1.7 copy.769
  80.4 1.2 multiply_reduce_fusion.3
  82.2 1.3 fusion.102
  93.3 2.1 collective-permute-start.4
  95.4 7.3 %collective-permute-start.5 = (f32[26,1,16,128]{3,2,1,0:T(8,128)S(1)}, f32[26,1,16,128]{3,2,1,0:T(8,128)S(1)}, u32[]{:S(2)}, u32[]{:S(2)}) collective-permute-start(f32[26,1,16,128]{3,2,1,0:T(8,128)S(1)} %get-tuple-element.143), channel_id=1, source_target_pairs={{8,0},{16,8},{24,16},{32,24},{40,32},{48,40},{56,48},{64,56},{72,6... | collective-permute-start | bytes 638984 | tf_op jit(solution)/shard_map/ppermute | solution.py:23
  106.4 1.3 copy.783
  107.6 1.9 collective-permute-start.6
  111.0 6.2 %collective-permute-start.7 = (f32[26,4,16,1]{0,2,3,1:T(8,128)S(1)}, f32[26,4,16,1]{0,2,3,1:T(8,128)}, u32[]{:S(2)}, u32[]{:S(2)}) collective-permute-start(f32[26,4,16,1]{0,2,3,1:T(8,128)S(1)} %copy.785), channel_id=1, source_target_pairs={{1,0},{2,1},{3,2},{4,3},{5,4},{6,5},{7,6},{0,7},{9,8},{10,9},{11,1... | collective-permute-start | bytes 19976 | tf_op jit(solution)/shard_map/ppermute | solution.py:23
  117.2 0.9 copy.784
  124.7 1.6 copy.786
  130.5 0.8 copy-done.8
  136.9 1.1 multiply_reduce_fusion.5
  139.3 1.9 scatter_fusion
  141.3 1.9 collective-permute-start.13
  143.2 7.3 %collective-permute-start.12 = (f32[26,1,16,128]{3,2,1,0:T(8,128)S(1)}, f32[26,1,16,128]{3,2,1,0:T(8,128)S(1)}, u32[]{:S(2)}, u32[]{:S(2)}) collective-permute-start(f32[26,1,16,128]{3,2,1,0:T(8,128)S(1)} %get-tuple-element.141), channel_id=1, source_target_pairs={{8,0},{16,8},{24,16},{32,24},{40,32},{48,40},{56,48},{64,56},{72,6... | collective-permute-start | bytes 638984 | tf_op jit(solution)/shard_map/ppermute | solution.py:23
  150.5 1.6 collective-permute-done.13
  152.1 1.8 collective-permute-done.12
  155.5 3.9 %collective-permute-start.14 = (f32[26,4,16,1]{0,2,3,1:T(8,128)S(1)}, f32[26,4,16,1]{0,2,3,1:T(8,128)S(1)}, u32[]{:S(2)}, u32[]{:S(2)}) collective-permute-start(f32[26,4,16,1]{0,2,3,1:T(8,128)S(1)} %copy.818), channel_id=1, source_target_pairs={{1,0},{2,1},{3,2},{4,3},{5,4},{6,5},{7,6},{0,7},{9,8},{10,9},{11,1... | collective-permute-start | bytes 19976 | tf_op jit(solution)/shard_map/ppermute | solution.py:23
  159.4 2.2 %collective-permute-start.15 = (f32[26,4,16,1]{0,2,3,1:T(8,128)S(1)}, f32[26,4,16,1]{0,2,3,1:T(8,128)S(1)}, u32[]{:S(2)}, u32[]{:S(2)}) collective-permute-start(f32[26,4,16,1]{0,2,3,1:T(8,128)S(1)} %copy.820), channel_id=1, source_target_pairs={{0,1},{1,2},{2,3},{3,4},{4,5},{5,6},{6,7},{7,0},{8,9},{9,10},{10,1... | collective-permute-start | bytes 19976 | tf_op jit(solution)/shard_map/ppermute | solution.py:20
  161.7 5.7 %collective-permute-done.15 = f32[26,4,16,1]{0,2,3,1:T(8,128)S(1)} collective-permute-done((f32[26,4,16,1]{0,2,3,1:T(8,128)S(1)}, f32[26,4,16,1]{0,2,3,1:T(8,128)S(1)}, u32[]{:S(2)}, u32[]{:S(2)}) %collective-permute-start.15) | collective-permute-done | bytes 6688 | tf_op jit(solution)/shard_map/ppermute | solution.py:20
  167.3 0.9 copy.821
  168.2 0.9 copy.819
  178.3 1.1 fusion.91
  180.8 1.9 scatter_fusion.1
  182.7 1.9 collective-permute-start.17
  184.6 7.3 %collective-permute-start.16 = (f32[26,1,16,128]{3,2,1,0:T(8,128)S(1)}, f32[26,1,16,128]{3,2,1,0:T(8,128)S(1)}, u32[]{:S(2)}, u32[]{:S(2)}) collective-permute-start(f32[26,1,16,128]{3,2,1,0:T(8,128)S(1)} %get-tuple-element.139), channel_id=1, source_target_pairs={{8,0},{16,8},{24,16},{32,24},{40,32},{48,40},{56,48},{64,56},{72,6... | collective-permute-start | bytes 638984 | tf_op jit(solution)/shard_map/ppermute | solution.py:23
  191.9 1.6 collective-permute-done.17
  193.5 1.8 collective-permute-done.16
  196.9 1.9 collective-permute-start.18
  198.9 3.9 %collective-permute-start.19 = (f32[26,4,16,1]{0,2,3,1:T(8,128)S(1)}, f32[26,4,16,1]{0,2,3,1:T(8,128)S(1)}, u32[]{:S(2)}, u32[]{:S(2)}) collective-permute-start(f32[26,4,16,1]{0,2,3,1:T(8,128)S(1)} %copy.841), channel_id=1, source_target_pairs={{0,1},{1,2},{2,3},{3,4},{4,5},{5,6},{6,7},{7,0},{8,9},{9,10},{10,1... | collective-permute-start | bytes 19976 | tf_op jit(solution)/shard_map/ppermute | solution.py:20
  202.8 4.0 %collective-permute-done.19 = f32[26,4,16,1]{0,2,3,1:T(8,128)S(1)} collective-permute-done((f32[26,4,16,1]{0,2,3,1:T(8,128)S(1)}, f32[26,4,16,1]{0,2,3,1:T(8,128)S(1)}, u32[]{:S(2)}, u32[]{:S(2)}) %collective-permute-start.19) | collective-permute-done | bytes 6688 | tf_op jit(solution)/shard_map/ppermute | solution.py:20
  206.8 0.9 copy.842
  207.7 0.9 copy.840
  (535 shorter events, 82.1 us)
Async XLA Ops:
  2.7 13.0 %copy-start.63 = (f32[2,16,128]{2,1,0:T(8,128)S(1)}, f32[2,16,128]{2,1,0:T(8,128)}, u32[]{:S(2)}) copy-start(f32[2,16,128]{2,1,0:T(8,128)} %param.51) | copy-start | bytes 49156
  2.7 13.7 %copy-start.19 = (f32[7,2,16,128]{3,2,1,0:T(8,128)S(1)}, f32[7,2,16,128]{3,2,1,0:T(8,128)}, u32[]{:S(2)}) copy-start(f32[7,2,16,128]{3,2,1,0:T(8,128)} %param.47) | copy-start | bytes 344068
  2.8 13.7 %copy-start.1 = (f32[19,2,16,128]{3,2,1,0:T(8,128)S(1)}, f32[19,2,16,128]{3,2,1,0:T(8,128)}, u32[]{:S(2)}) copy-start(f32[19,2,16,128]{3,2,1,0:T(8,128)} %param.46) | copy-start | bytes 933892
  2.8 12.9 %copy-start.95 = (s32[19]{0:T(128)S(1)}, s32[19]{0:T(128)}, u32[]{:S(2)}) copy-start(s32[19]{0:T(128)} %constant.75) | copy-start | bytes 232
  2.8 33.0 %collective-permute-start.9 = (f32[26,1,16,128]{3,2,1,0:T(8,128)S(1)}, f32[26,1,16,128]{3,2,1,0:T(8,128)S(1)}, u32[]{:S(2)}, u32[]{:S(2)}) collective-permute-start(f32[26,1,16,128]{3,2,1,0:T(8,128)S(1)} %get-tuple-element.146), channel_id=1, source_target_pairs={{0,8},{8,16},{16,24},{24,32},{32,40},{40,48},{48,56},{56,64},{64,7... | collective-permute-start | bytes 638984 | tf_op jit(solution)/shard_map/ppermute | solution.py:20
  4.9 31.0 %collective-permute-start.8 = (f32[26,1,16,128]{3,2,1,0:T(8,128)S(1)}, f32[26,1,16,128]{3,2,1,0:T(8,128)S(1)}, u32[]{:S(2)}, u32[]{:S(2)}) collective-permute-start(f32[26,1,16,128]{3,2,1,0:T(8,128)S(1)} %get-tuple-element.147), channel_id=1, source_target_pairs={{8,0},{16,8},{24,16},{32,24},{40,32},{48,40},{56,48},{64,56},{72,6... | collective-permute-start | bytes 638984 | tf_op jit(solution)/shard_map/ppermute | solution.py:23
  15.7 2.0 copy-start.94
  16.4 6.2 %copy-start.22 = (f32[2,16,128]{2,1,0:T(8,128)}, f32[2,16,128]{2,1,0:T(8,128)S(1)}, u32[]{:S(2)}) copy-start(f32[2,16,128]{2,1,0:T(8,128)S(1)} %divide_subtract_fusion) | copy-start | bytes 49156
  16.5 6.1 %copy-start.20 = (f32[2,16,128]{2,1,0:T(8,128)}, f32[2,16,128]{2,1,0:T(8,128)S(1)}, u32[]{:S(2)}) copy-start(f32[2,16,128]{2,1,0:T(8,128)S(1)} %reduce_sum.445) | copy-start | bytes 49156
  18.9 4.3 %copy-start.43 = (f32[2,16,128]{2,1,0:T(8,128)}, f32[2,16,128]{2,1,0:T(8,128)S(1)}, u32[]{:S(2)}) copy-start(f32[2,16,128]{2,1,0:T(8,128)S(1)} %get-tuple-element.211) | copy-start | bytes 49156
  19.7 3.5 %copy-start.5 = (f32[19,2,16,128]{3,2,1,0:T(8,128)}, f32[19,2,16,128]{3,2,1,0:T(8,128)S(1)}, u32[]{:S(2)}) copy-start(f32[19,2,16,128]{3,2,1,0:T(8,128)S(1)} %get-tuple-element.49) | copy-start | bytes 933892
  24.3 22.9 %collective-permute-start = (f32[26,1,16,128]{3,2,1,0:T(8,128)}, f32[26,1,16,128]{3,2,1,0:T(8,128)S(1)}, u32[]{:S(2)}, u32[]{:S(2)}) collective-permute-start(f32[26,1,16,128]{3,2,1,0:T(8,128)} %get-tuple-element.144), channel_id=1, source_target_pairs={{0,8},{8,16},{16,24},{24,32},{32,40},{40,48},{48,56},{56,64},{64,7... | collective-permute-start | bytes 638984 | tf_op jit(solution)/shard_map/ppermute | solution.py:20
  26.2 20.9 %collective-permute-start.1 = (f32[26,1,16,128]{3,2,1,0:T(8,128)}, f32[26,1,16,128]{3,2,1,0:T(8,128)S(1)}, u32[]{:S(2)}, u32[]{:S(2)}) collective-permute-start(f32[26,1,16,128]{3,2,1,0:T(8,128)} %get-tuple-element.145), channel_id=1, source_target_pairs={{8,0},{16,8},{24,16},{32,24},{40,32},{48,40},{56,48},{64,56},{72,6... | collective-permute-start | bytes 638984 | tf_op jit(solution)/shard_map/ppermute | solution.py:23
  38.8 22.3 %collective-permute-start.10 = (f32[26,4,16,1]{0,2,3,1:T(8,128)}, f32[26,4,16,1]{0,2,3,1:T(8,128)}, u32[]{:S(2)}, u32[]{:S(2)}) collective-permute-start(f32[26,4,16,1]{0,2,3,1:T(8,128)} %copy.791), channel_id=1, source_target_pairs={{1,0},{2,1},{3,2},{4,3},{5,4},{6,5},{7,6},{0,7},{9,8},{10,9},{11,1... | collective-permute-start | bytes 19976 | tf_op jit(solution)/shard_map/ppermute | solution.py:23
  45.2 14.2 %collective-permute-start.11 = (f32[26,4,16,1]{0,2,3,1:T(8,128)}, f32[26,4,16,1]{0,2,3,1:T(8,128)}, u32[]{:S(2)}, u32[]{:S(2)}) collective-permute-start(f32[26,4,16,1]{0,2,3,1:T(8,128)} %copy.793), channel_id=1, source_target_pairs={{0,1},{1,2},{2,3},{3,4},{4,5},{5,6},{6,7},{7,0},{8,9},{9,10},{10,1... | collective-permute-start | bytes 19976 | tf_op jit(solution)/shard_map/ppermute | solution.py:20
  47.2 21.9 %copy-start.2 = (f32[26,1,16,128]{3,2,1,0:T(8,128)}, f32[26,1,16,128]{3,2,1,0:T(8,128)S(1)}, u32[]{:S(2)}) copy-start(f32[26,1,16,128]{3,2,1,0:T(8,128)S(1)} %collective-permute-done.1) | copy-start | bytes 638980
  50.1 25.4 %collective-permute-start.3 = (f32[26,4,16,1]{0,2,3,1:T(8,128)}, f32[26,4,16,1]{0,2,3,1:T(8,128)}, u32[]{:S(2)}, u32[]{:S(2)}) collective-permute-start(f32[26,4,16,1]{0,2,3,1:T(8,128)} %copy.768), channel_id=1, source_target_pairs={{1,0},{2,1},{3,2},{4,3},{5,4},{6,5},{7,6},{0,7},{9,8},{10,9},{11,1... | collective-permute-start | bytes 19976 | tf_op jit(solution)/shard_map/ppermute | solution.py:23
  56.1 11.3 %collective-permute-start.2 = (f32[26,4,16,1]{0,2,3,1:T(8,128)}, f32[26,4,16,1]{0,2,3,1:T(8,128)}, u32[]{:S(2)}, u32[]{:S(2)}) collective-permute-start(f32[26,4,16,1]{0,2,3,1:T(8,128)} %copy.766), channel_id=1, source_target_pairs={{0,1},{1,2},{2,3},{3,4},{4,5},{5,6},{6,7},{7,0},{8,9},{9,10},{10,1... | collective-permute-start | bytes 19976 | tf_op jit(solution)/shard_map/ppermute | solution.py:20
  69.7 9.6 %copy-start.36 = (f32[2,16,128]{2,1,0:T(8,128)}, f32[2,16,128]{2,1,0:T(8,128)S(1)}, u32[]{:S(2)}) copy-start(f32[2,16,128]{2,1,0:T(8,128)S(1)} %get-tuple-element.135) | copy-start | bytes 49156
  75.4 1.7 copy-start.3
  80.1 7.0 %copy-start.27 = (f32[2,16,128]{2,1,0:T(8,128)}, f32[2,16,128]{2,1,0:T(8,128)S(1)}, u32[]{:S(2)}) copy-start(f32[2,16,128]{2,1,0:T(8,128)S(1)} %get-tuple-element.39) | copy-start | bytes 49156
  81.5 2.0 copy-start.12
  85.1 7.6 %copy-start.41 = (f32[2,16,128]{2,1,0:T(8,128)}, f32[2,16,128]{2,1,0:T(8,128)S(1)}, u32[]{:S(2)}) copy-start(f32[2,16,128]{2,1,0:T(8,128)S(1)} %get-tuple-element.31) | copy-start | bytes 49156
  86.4 2.1 copy-start.17
  89.2 1.0 copy-start.73
  93.3 9.4 %copy-start.4 = (f32[19,2,16,128]{3,2,1,0:T(8,128)S(1)}, f32[19,2,16,128]{3,2,1,0:T(8,128)}, u32[]{:S(2)}) copy-start(f32[19,2,16,128]{3,2,1,0:T(8,128)} %get-tuple-element.79) | copy-start | bytes 933892
  93.3 9.4 %copy-start.71 = (f32[2,15,128]{2,1,0:T(8,128)S(1)}, f32[2,15,128]{2,1,0:T(8,128)}, u32[]{:S(2)}) copy-start(f32[2,15,128]{2,1,0:T(8,128)} %slice.1297) | copy-start | bytes 46084
  93.3 12.2 %collective-permute-start.4 = (f32[26,1,16,128]{3,2,1,0:T(8,128)S(1)}, f32[26,1,16,128]{3,2,1,0:T(8,128)S(1)}, u32[]{:S(2)}, u32[]{:S(2)}) collective-permute-start(f32[26,1,16,128]{3,2,1,0:T(8,128)S(1)} %get-tuple-element.142), channel_id=1, source_target_pairs={{0,8},{8,16},{16,24},{24,32},{32,40},{40,48},{48,56},{56,64},{64,7... | collective-permute-start | bytes 638984 | tf_op jit(solution)/shard_map/ppermute | solution.py:20
  95.4 7.3 %copy-start.103 = (f32[2,1,128]{2,1,0:T(1,128)S(1)}, f32[2,1,128]{2,1,0:T(1,128)}, u32[]{:S(2)}) copy-start(f32[2,1,128]{2,1,0:T(1,128)} %slice.1298) | copy-start | bytes 3076
  95.4 10.6 %collective-permute-start.5 = (f32[26,1,16,128]{3,2,1,0:T(8,128)S(1)}, f32[26,1,16,128]{3,2,1,0:T(8,128)S(1)}, u32[]{:S(2)}, u32[]{:S(2)}) collective-permute-start(f32[26,1,16,128]{3,2,1,0:T(8,128)S(1)} %get-tuple-element.143), channel_id=1, source_target_pairs={{8,0},{16,8},{24,16},{32,24},{40,32},{48,40},{56,48},{64,56},{72,6... | collective-permute-start | bytes 638984 | tf_op jit(solution)/shard_map/ppermute | solution.py:23
  107.6 9.6 %collective-permute-start.6 = (f32[26,4,16,1]{0,2,3,1:T(8,128)}, f32[26,4,16,1]{0,2,3,1:T(8,128)S(1)}, u32[]{:S(2)}, u32[]{:S(2)}) collective-permute-start(f32[26,4,16,1]{0,2,3,1:T(8,128)} %copy.783), channel_id=1, source_target_pairs={{0,1},{1,2},{2,3},{3,4},{4,5},{5,6},{6,7},{7,0},{8,9},{9,10},{10,1... | collective-permute-start | bytes 19976 | tf_op jit(solution)/shard_map/ppermute | solution.py:20
  111.0 13.7 %collective-permute-start.7 = (f32[26,4,16,1]{0,2,3,1:T(8,128)S(1)}, f32[26,4,16,1]{0,2,3,1:T(8,128)}, u32[]{:S(2)}, u32[]{:S(2)}) collective-permute-start(f32[26,4,16,1]{0,2,3,1:T(8,128)S(1)} %copy.785), channel_id=1, source_target_pairs={{1,0},{2,1},{3,2},{4,3},{5,4},{6,5},{7,6},{0,7},{9,8},{10,9},{11,1... | collective-permute-start | bytes 19976 | tf_op jit(solution)/shard_map/ppermute | solution.py:23
  130.3 1.0 copy-start.8
  141.3 10.8 %collective-permute-start.13 = (f32[26,1,16,128]{3,2,1,0:T(8,128)S(1)}, f32[26,1,16,128]{3,2,1,0:T(8,128)S(1)}, u32[]{:S(2)}, u32[]{:S(2)}) collective-permute-start(f32[26,1,16,128]{3,2,1,0:T(8,128)S(1)} %get-tuple-element.140), channel_id=1, source_target_pairs={{0,8},{8,16},{16,24},{24,32},{32,40},{40,48},{48,56},{56,64},{64,7... | collective-permute-start | bytes 638984 | tf_op jit(solution)/shard_map/ppermute | solution.py:20
  143.2 10.6 %collective-permute-start.12 = (f32[26,1,16,128]{3,2,1,0:T(8,128)S(1)}, f32[26,1,16,128]{3,2,1,0:T(8,128)S(1)}, u32[]{:S(2)}, u32[]{:S(2)}) collective-permute-start(f32[26,1,16,128]{3,2,1,0:T(8,128)S(1)} %get-tuple-element.141), channel_id=1, source_target_pairs={{8,0},{16,8},{24,16},{32,24},{40,32},{48,40},{56,48},{64,56},{72,6... | collective-permute-start | bytes 638984 | tf_op jit(solution)/shard_map/ppermute | solution.py:23
  155.5 12.7 %collective-permute-start.14 = (f32[26,4,16,1]{0,2,3,1:T(8,128)S(1)}, f32[26,4,16,1]{0,2,3,1:T(8,128)S(1)}, u32[]{:S(2)}, u32[]{:S(2)}) collective-permute-start(f32[26,4,16,1]{0,2,3,1:T(8,128)S(1)} %copy.818), channel_id=1, source_target_pairs={{1,0},{2,1},{3,2},{4,3},{5,4},{6,5},{7,6},{0,7},{9,8},{10,9},{11,1... | collective-permute-start | bytes 19976 | tf_op jit(solution)/shard_map/ppermute | solution.py:23
  159.4 7.9 %collective-permute-start.15 = (f32[26,4,16,1]{0,2,3,1:T(8,128)S(1)}, f32[26,4,16,1]{0,2,3,1:T(8,128)S(1)}, u32[]{:S(2)}, u32[]{:S(2)}) collective-permute-start(f32[26,4,16,1]{0,2,3,1:T(8,128)S(1)} %copy.820), channel_id=1, source_target_pairs={{0,1},{1,2},{2,3},{3,4},{4,5},{5,6},{6,7},{7,0},{8,9},{9,10},{10,1... | collective-permute-start | bytes 19976 | tf_op jit(solution)/shard_map/ppermute | solution.py:20
  172.9 1.0 copy-start.9
  172.9 1.0 copy-start.79
  182.7 10.8 %collective-permute-start.17 = (f32[26,1,16,128]{3,2,1,0:T(8,128)S(1)}, f32[26,1,16,128]{3,2,1,0:T(8,128)S(1)}, u32[]{:S(2)}, u32[]{:S(2)}) collective-permute-start(f32[26,1,16,128]{3,2,1,0:T(8,128)S(1)} %get-tuple-element.138), channel_id=1, source_target_pairs={{0,8},{8,16},{16,24},{24,32},{32,40},{40,48},{48,56},{56,64},{64,7... | collective-permute-start | bytes 638984 | tf_op jit(solution)/shard_map/ppermute | solution.py:20
  184.6 10.6 %collective-permute-start.16 = (f32[26,1,16,128]{3,2,1,0:T(8,128)S(1)}, f32[26,1,16,128]{3,2,1,0:T(8,128)S(1)}, u32[]{:S(2)}, u32[]{:S(2)}) collective-permute-start(f32[26,1,16,128]{3,2,1,0:T(8,128)S(1)} %get-tuple-element.139), channel_id=1, source_target_pairs={{8,0},{16,8},{24,16},{32,24},{40,32},{48,40},{56,48},{64,56},{72,6... | collective-permute-start | bytes 638984 | tf_op jit(solution)/shard_map/ppermute | solution.py:23
  196.9 10.7 %collective-permute-start.18 = (f32[26,4,16,1]{0,2,3,1:T(8,128)S(1)}, f32[26,4,16,1]{0,2,3,1:T(8,128)S(1)}, u32[]{:S(2)}, u32[]{:S(2)}) collective-permute-start(f32[26,4,16,1]{0,2,3,1:T(8,128)S(1)} %copy.839), channel_id=1, source_target_pairs={{1,0},{2,1},{3,2},{4,3},{5,4},{6,5},{7,6},{0,7},{9,8},{10,9},{11,1... | collective-permute-start | bytes 19976 | tf_op jit(solution)/shard_map/ppermute | solution.py:23
  198.9 7.9 %collective-permute-start.19 = (f32[26,4,16,1]{0,2,3,1:T(8,128)S(1)}, f32[26,4,16,1]{0,2,3,1:T(8,128)S(1)}, u32[]{:S(2)}, u32[]{:S(2)}) collective-permute-start(f32[26,4,16,1]{0,2,3,1:T(8,128)S(1)} %copy.841), channel_id=1, source_target_pairs={{0,1},{1,2},{2,3},{3,4},{4,5},{5,6},{6,7},{7,0},{8,9},{9,10},{10,1... | collective-permute-start | bytes 19976 | tf_op jit(solution)/shard_map/ppermute | solution.py:20
  210.0 0.9 copy-start.21
  210.0 0.9 copy-start.85
  211.9 1.0 copy-start.6
  213.2 1.4 copy-start.61
  213.2 1.4 copy-start.64
  (78 other events, 56.2 us)
where the time goes:
time: 220 us; the launch traced here: 216 us
  starting transfers between devices  86.2 us (39%)
  local copies, waits for them, and re-layouts  71.7 us (33%)
  other arithmetic  22.1 us (10%)
  waiting for transfers between devices  16.8 us (8%)
  matrix products  16.1 us (7%)
  between operations  3.23 us (1%)
    ppermute x10, starting transfers between devices, with_halo(): lax.ppermute(lax.slice_in_dim(block, 0, width, axis=dim), axis, backward)  64.3 us
    unnamed x242, local copies, waits for them, and re-layouts  32.8 us
    ppermute x10, starting transfers between devices, with_halo(): lax.ppermute(lax.slice_in_dim(block, block.shape[dim] - width, None, axis...  21.9 us
    slice x91, local copies, waits for them, and re-layouts, stream_rims(): shifted.append(jnp.roll(window_cells, step_z, axis=1))  13.8 us
    ppermute x10, waiting for transfers between devices, with_halo(): lax.ppermute(lax.slice_in_dim(block, block.shape[dim] - width, None, axis...  12.8 us
    ppermute x5, local copies, waits for them, and re-layouts, with_halo(): lax.ppermute(lax.slice_in_dim(block, 0, width, axis=dim), axis, backward)  6.71 us
    slice x10, local copies, waits for them, and re-layouts, with_halo(): lax.slice_in_dim(block, block.shape[dim] - width, None, axis=dim)  6.68 us
    ppermute x5, local copies, waits for them, and re-layouts, with_halo(): lax.ppermute(lax.slice_in_dim(block, block.shape[dim] - width, None, axis...  5.91 us
  transfers between devices with their start and end apart: 20, of which 7 were waited for; matrix products, arithmetic and copies ran while one was open for 19% of the time, Pallas kernels for 0%

commit v1 on v0

v1 whole, which is shorter than its diff:
```python
import jax
import jax.numpy as jnp
import numpy as np
from jax import lax
from jax.experimental import pallas as pl
from jax.experimental.pallas import tpu as pltpu
from jax.sharding import PartitionSpec as P

ZED = 16
LANES = 128
WIDE = 2 * LANES
EDGE = 4

FLOW_VELOCITY = [
    (0, 0, 0),
    (1, 0, 0),
    (-1, 0, 0),
    (0, 1, 0),
    (0, -1, 0),
    (0, 0, 1),
    (0, 0, -1),
    (1, 1, 0),
    (-1, -1, 0),
    (1, -1, 0),
    (-1, 1, 0),
    (1, 0, 1),
    (-1, 0, -1),
    (1, 0, -1),
    (-1, 0, 1),
    (0, 1, 1),
    (0, -1, -1),
    (0, 1, -1),
    (0, -1, 1),
]
VELOCITY = FLOW_VELOCITY + FLOW_VELOCITY[:7]
MEMBERS = len(VELOCITY)
RIGHTWARD = [q for q in range(MEMBERS) if VELOCITY[q][0] == 1]
LEFTWARD = [q for q in range(MEMBERS) if VELOCITY[q][0] == -1]
LEVEL = [q for q in range(MEMBERS) if VELOCITY[q][0] == 0]

MOBILITY, RATE, WEIGHT = MEMBERS, MEMBERS + 1, MEMBERS + 2
FIELDS = MEMBERS + 6

SLOTS = LANES // (2 * EDGE)
STRIP_ROWS = 2 * FIELDS // SLOTS
ADJ_ROWS = -(-MEMBERS // SLOTS)


def rows_of(entries):
    return {entry: row for row, entry in enumerate(entries)}


SIDE_FIELDS = list(range(MEMBERS, FIELDS))
TO_RIGHT = rows_of(
    [(q, 0) for q in RIGHTWARD] + [(q, 1) for q in RIGHTWARD + LEVEL] + [(k, 1) for k in SIDE_FIELDS]
)
TO_LEFT = rows_of(
    [(q, 1) for q in LEFTWARD] + [(q, 0) for q in LEFTWARD + LEVEL] + [(k, 0) for k in SIDE_FIELDS]
)
ADJ_TO_RIGHT = rows_of([(q, 0) for q in LEFTWARD] + [(q, 1) for q in LEFTWARD + LEVEL])
ADJ_TO_LEFT = rows_of([(q, 1) for q in RIGHTWARD] + [(q, 0) for q in RIGHTWARD + LEVEL])
BULK_ROWS = len(TO_RIGHT)
ADJ_BULK = len(ADJ_TO_RIGHT)


def pair_sums(f):
    total = [f[2 * k + 1] + f[2 * k + 2] for k in range(9)]
    gap = [f[2 * k + 1] - f[2 * k + 2] for k in range(9)]
    return total, gap


def flow_moments(f):
    s, d = pair_sums(f)
    xy, xz, yz = s[3] + s[4], s[5] + s[6], s[7] + s[8]
    rho = f[0] + (s[0] + s[1] + s[2]) + (xy + xz + yz)
    j = (
        d[0] + (d[3] + d[4]) + (d[5] + d[6]),
        d[1] + (d[3] - d[4]) + (d[7] + d[8]),
        d[2] + (d[5] - d[6]) + (d[7] - d[8]),
    )
    second = (s[0] + xy + xz, s[1] + xy + yz, s[2] + xz + yz, s[3] - s[4], s[5] - s[6], s[7] - s[8])
    return rho, j, second


def heat_moments(g):
    temperature = g[0] + (g[1] + g[2]) + (g[3] + g[4]) + (g[5] + g[6])
    return temperature, (g[1] - g[2], g[3] - g[4], g[5] - g[6])


def common(f, g, mobility):
    rho, j, second = flow_moments(f)
    temperature, flux = heat_moments(g)
    u = tuple(mobility * jk for jk in j)
    square = (u[0] * u[0], u[1] * u[1], u[2] * u[2])
    third = rho * (1.0 / 3.0)
    stress = (
        second[0] - third - square[0],
        second[1] - third - square[1],
        second[2] - third - square[2],
        second[3] - u[0] * u[1],
        second[4] - u[0] * u[2],
        second[5] - u[1] * u[2],
    )
    decay = jnp.exp(-2.0 * (temperature - 1.0))
    omega = 1.0 / (0.5 + 0.3 * decay)
    return rho, j, u, square, stress, temperature, flux, decay, omega


def collide(f, g, mobility, rate):
    rho, _, u, square, stress, temperature, flux, _, omega = common(f, g, mobility)
    solid = mobility == 0.0
    lam = 1.2 - omega
    trace = stress[0] + stress[1] + stress[2]
    base = 1.2 * rho - 1.8 * (square[0] + square[1] + square[2]) - (1.5 * lam) * trace
    scale = 4.5 * lam
    mxx = 5.4 * square[0] + scale * stress[0]
    myy = 5.4 * square[1] + scale * stress[1]
    mzz = 5.4 * square[2] + scale * stress[2]
    mxy = 2.0 * (5.4 * (u[0] * u[1]) + scale * stress[3])
    mxz = 2.0 * (5.4 * (u[0] * u[2]) + scale * stress[4])
    myz = 2.0 * (5.4 * (u[1] * u[2]) + scale * stress[5])
    bx, by, bz = base + mxx, base + myy, base + mzz
    sxy, sxz, syz = bx + myy, bx + mzz, by + mzz
    even = [bx, by, bz, sxy + mxy, sxy - mxy, sxz + mxz, sxz - mxz, syz + myz, syz - myz]
    odd = [u[0], u[1], u[2], u[0] + u[1], u[0] - u[1], u[0] + u[2], u[0] - u[2], u[1] + u[2], u[1] - u[2]]
    flow = [None] * 19
    flow[0] = jnp.where(solid, f[0], (1.0 / 3.0) * base - 0.2 * f[0])
    for k in range(9):
        a, b = 2 * k + 1, 2 * k + 2
        w = 1.0 / 18.0 if k < 3 else 1.0 / 36.0
        e, o = w * even[k], (3.6 * w) * odd[k]
        flow[a] = jnp.where(solid, f[b], (e + o) - 0.2 * f[a])
        flow[b] = jnp.where(solid, f[a], (e - o) - 0.2 * f[b])
    keep = 0.5 * (1.4 - rate)
    push = (0.5 * rate) * temperature
    warm = 0.175 * temperature
    heat = [0.35 * temperature - 0.4 * g[0]]
    for k in range(3):
        along = keep * flux[k] + push * u[k]
        heat.append((warm + along) - 0.4 * g[2 * k + 1])
        heat.append((warm - along) - 0.4 * g[2 * k + 2])
    return flow + heat


def pull_back(f, g, fa, ga, mobility, rate, wanted, sensitivity):
    rho, j, u, square, stress, temperature, flux, decay, omega = common(f, g, mobility)
    solid = mobility == 0.0
    lam = 1.2 - omega
    s, d = pair_sums(fa)
    w = 1.0 / 36.0
    xy, xz, yz = s[3] + s[4], s[5] + s[6], s[7] + s[8]
    s2 = (s[0] + s[0], s[1] + s[1], s[2] + s[2])
    mass = w * (12.0 * fa[0] + (s2[0] + s2[1] + s2[2]) + (xy + xz + yz))
    px = w * ((d[0] + d[0]) + (d[3] + d[4]) + (d[5] + d[6]))
    py = w * ((d[1] + d[1]) + (d[3] - d[4]) + (d[7] + d[8]))
    pz = w * ((d[2] + d[2]) + (d[5] - d[6]) + (d[7] - d[8]))
    rxx, ryy, rzz = w * (s2[0] + xy + xz), w * (s2[1] + xy + yz), w * (s2[2] + xz + yz)
    rxy, rxz, ryz = w * (s[3] - s[4]), w * (s[5] - s[6]), w * (s[7] - s[8])
    shift = 1.5 * mass
    dxx, dyy, dzz = 4.5 * rxx - shift, 4.5 * ryy - shift, 4.5 * rzz - shift
    dxy, dxz, dyz = 4.5 * rxy, 4.5 * rxz, 4.5 * ryz
    lam_bar = (
        dxx * stress[0]
        + dyy * stress[1]
        + dzz * stress[2]
        + 2.0 * (dxy * stress[3] + dxz * stress[4] + dyz * stress[5])
    )
    mix = 2.4 - 2.0 * lam
    b = ((ga[1] - ga[2]) * 0.125, (ga[3] - ga[4]) * 0.125, (ga[5] - ga[6]) * 0.125)
    push = (4.0 * rate) * temperature
    ux = 3.6 * px + mix * (dxx * u[0] + dxy * u[1] + dxz * u[2]) + push * b[0]
    uy = 3.6 * py + mix * (dxy * u[0] + dyy * u[1] + dyz * u[2]) + push * b[1]
    uz = 3.6 * pz + mix * (dxz * u[0] + dyz * u[1] + dzz * u[2]) + push * b[2]
    result = {}
    if wanted:
        rho_bar = 1.2 * mass - (1.5 * lam) * ((rxx + ryy + rzz) - mass)
        jx, jy, jz = mobility * ux, mobility * uy, mobility * uz
        ex, ey, ez = lam * dxx, lam * dyy, lam * dzz
        exy, exz, eyz = (2.0 * lam) * dxy, (2.0 * lam) * dxz, (2.0 * lam) * dyz
        hx, hy, hz = rho_bar + ex, rho_bar + ey, rho_bar + ez
        gxy, gxz, gyz = hx + ey, hx + ez, hy + ez
        even = [hx, hy, hz, gxy + exy, gxy - exy, gxz + exz, gxz - exz, gyz + eyz, gyz - eyz]
        odd = [jx, jy, jz, jx + jy, jx - jy, jx + jz, jx - jz, jy + jz, jy - jz]
        if 0 in wanted:
            result[0] = jnp.where(solid, fa[0], rho_bar - 0.2 * fa[0])
        for k in range(9):
            p, m = 2 * k + 1, 2 * k + 2
            if p in wanted:
                result[p] = jnp.where(solid, fa[m], (even[k] + odd[k]) - 0.2 * fa[p])
            if m in wanted:
                result[m] = jnp.where(solid, fa[p], (even[k] - odd[k]) - 0.2 * fa[m])
        warm = (
            0.35 * ga[0]
            + 0.175 * ((ga[1] + ga[2]) + (ga[3] + ga[4]) + (ga[5] + ga[6]))
            + (4.0 * rate) * (b[0] * u[0] + b[1] * u[1] + b[2] * u[2])
            - jnp.where(solid, 0.0, lam_bar * (0.6 * decay) * (omega * omega))
        )
        keep = 5.6 - 4.0 * rate
        if 19 in wanted:
            result[19] = warm - 0.4 * ga[0]
        for k in range(3):
            along = keep * b[k]
            p, m = 2 * k + 1, 2 * k + 2
            if 19 + p in wanted:
                result[19 + p] = (warm + along) - 0.4 * ga[p]
            if 19 + m in wanted:
                result[19 + m] = (warm - along) - 0.4 * ga[m]
    if sensitivity:
        by_resistance = -(mobility * mobility) * (ux * j[0] + uy * j[1] + uz * j[2])
        bent = (
            b[0] * (temperature * u[0] - flux[0])
            + b[1] * (temperature * u[1] - flux[1])
            + b[2] * (temperature * u[2] - flux[2])
        )
        by_conductivity = (-1.6 * (rate * rate)) * bent
        result["by"] = (by_resistance, by_conductivity)
    return result


def turn(value, by, axis):
    count = value.shape[axis]
    by %= count
    return pltpu.roll(value, by, axis) if by else value


def pack(value, slot):
    return turn(value, 2 * EDGE * slot + EDGE, 1)


def unpack(row, slot):
    return turn(row, -EDGE - 2 * EDGE * slot, 1)


def pack_rows(values):
    lane = lax.broadcasted_iota(jnp.int32, (ZED, LANES), 1)
    rows = []
    for start in range(0, len(values), SLOTS):
        row = None
        for slot, value in enumerate(values[start : start + SLOTS]):
            part = pack(value, slot)
            row = part if row is None else jnp.where(lane >= 2 * EDGE * slot, part, row)
        rows.append(row)
    return rows


def halves():
    return [pl.ds(0, 8), pl.ds(8, 8)]


def first_kernel(flow, heat, flow_weight, heat_weight, resistance, conductivity, solid, own, sides, right, left, strip):
    for c in range(2):
        for z in halves():
            mobility = jnp.where(solid[c, z, :] != 0, 0.0, 1.0 / (1.0 + resistance[c, z, :]))
            rate = 1.0 / (0.5 + 0.4 * conductivity[c, z, :])
            f = [flow[q, c, z, :] for q in range(19)]
            g = [heat[q, c, z, :] for q in range(7)]
            after = collide(f, g, mobility, rate)
            sides[0, c, z, :] = mobility
            sides[1, c, z, :] = rate
            more = [mobility, rate] + [flow_weight[k, c, z, :] for k in range(3)] + [heat_weight[c, z, :]]
            for k, value in enumerate(after + more):
                if k < MEMBERS:
                    own[k, c, z, :] = value
                if (k, c) in TO_RIGHT:
                    right[TO_RIGHT[k, c], z, :] = value
                if (k, c) in TO_LEFT:
                    left[TO_LEFT[k, c], z, :] = value
    values = []
    for c in range(2):
        values += [own[q, c] for q in range(MEMBERS)]
        values += [sides[0, c], sides[1, c]]
        values += [flow_weight[k, c] for k in range(3)] + [heat_weight[c]]
    for row, value in enumerate(pack_rows(values)):
        strip[row] = value


def merge_kernel(from_left, from_right, right_in, left_in, right, left, strip):
    del right_in, left_in
    lane = lax.broadcasted_iota(jnp.int32, (ZED, LANES), 1)
    low = lane % (2 * EDGE) < EDGE
    for row in range(STRIP_ROWS):
        value = jnp.where(low, from_left[row], from_right[row])
        right[row] = value
        left[row] = value
        strip[row] = value


def wide_field(k, column, own_value, strip, from_left, from_right):
    if column < 0:
        c, bulk, rows = column + 2, from_left, TO_RIGHT
        strips, start = from_left, BULK_ROWS
    elif column > 1:
        c, bulk, rows = column - 2, from_right, TO_LEFT
        strips, start = from_right, BULK_ROWS
    else:
        c, bulk, rows = column, None, None
        strips, start = strip, 0
    main = own_value(k, c) if bulk is None else bulk[rows[k, c]]
    place = c * FIELDS + k
    beside = unpack(strips[start + place // SLOTS], place % SLOTS)
    return jnp.concatenate([main, beside], axis=1)


def moved(value, velocity, way):
    _, step_y, step_z = velocity
    return turn(turn(value, way * step_z, 0), way * step_y, 1)


def tiles(lanes):
    return [(z, pl.ds(t, LANES)) for z in halves() for t in range(0, lanes, LANES)]


def second_kernel(
    own, sides, flow_weight, heat_weight, strip, from_left, from_right,
    state, wide_sides, adjoint, by_resistance, by_conductivity, right, left,
    after, later, seed,
):
    def own_value(k, c):
        if k < MEMBERS:
            return own[k, c]
        if k < WEIGHT:
            return sides[k - MOBILITY, c]
        return flow_weight[k - WEIGHT, c] if k < WEIGHT + 3 else heat_weight[c]

    def wide(k, column):
        return wide_field(k, column, own_value, strip, from_left, from_right)

    for column in range(-1, 3):
        i = column + 1
        wide_sides[0, i] = wide(MOBILITY, column)
        wide_sides[1, i] = wide(RATE, column)
        for q in range(MEMBERS):
            state[q, i] = moved(wide(q, column - VELOCITY[q][0]), VELOCITY[q], 1)
    for i in range(4):
        for z, y in tiles(WIDE):
            f = [state[q, i, z, y] for q in range(19)]
            g = [state[19 + q, i, z, y] for q in range(7)]
            result = collide(f, g, wide_sides[0, i, z, y], wide_sides[1, i, z, y])
            for q in range(MEMBERS):
                if 0 <= i - 1 + VELOCITY[q][0] <= 1:
                    after[q, i, z, y] = result[q]
    for c in range(2):
        for q in range(MEMBERS):
            later[q, c] = moved(after[q, c + 1 - VELOCITY[q][0]], VELOCITY[q], 1)
    for column in range(-1, 3):
        weights = [wide(WEIGHT + k, column) for k in range(4)]
        for q in range(1, MEMBERS):
            velocity = VELOCITY[q]
            c = column - velocity[0]
            if not 0 <= c <= 1:
                continue
            if q < 19:
                parts = [weights[k] if velocity[k] > 0 else -weights[k] for k in range(3) if velocity[k]]
                value = parts[0] if len(parts) == 1 else parts[0] + parts[1]
            else:
                value = weights[3]
            seed[q, c] = moved(value, velocity, -1)
    for c in range(2):
        for z, y in tiles(WIDE):
            f = [later[q, c, z, y] for q in range(19)]
            g = [later[19 + q, c, z, y] for q in range(7)]
            fa = [jnp.zeros((8, LANES), jnp.float32)] + [seed[q, c, z, y] for q in range(1, 19)]
            ga = [seed[19 + q, c, z, y] for q in range(7)]
            inner = y.start == 0
            result = pull_back(
                f, g, fa, ga, wide_sides[0, c + 1, z, y], wide_sides[1, c + 1, z, y], range(MEMBERS), inner
            )
            if inner:
                by_resistance[c, z, :], by_conductivity[c, z, :] = result["by"]
            for q in range(MEMBERS):
                adjoint[q, c, z, y] = result[q]
                if inner and (q, c) in ADJ_TO_RIGHT:
                    right[ADJ_TO_RIGHT[q, c], z, :] = result[q]
                if inner and (q, c) in ADJ_TO_LEFT:
                    left[ADJ_TO_LEFT[q, c], z, :] = result[q]
    for side, rows in ((right, ADJ_TO_RIGHT), (left, ADJ_TO_LEFT)):
        values = [adjoint[q, c, :, LANES:] for q, c in rows]
        for row, value in enumerate(pack_rows(values)):
            side[ADJ_BULK + row] = value


def third_kernel(
    flow, heat, state, wide_sides, adjoint, part_resistance, part_conductivity, from_left, from_right,
    by_resistance, by_conductivity,
    arrived, earlier, last,
):
    def wide(q, column):
        if 0 <= column <= 1:
            return adjoint[q, column]
        c, bulk, rows = (column + 2, from_left, ADJ_TO_RIGHT) if column < 0 else (column - 2, from_right, ADJ_TO_LEFT)
        place = rows[q, c]
        beside = unpack(bulk[ADJ_BULK + place // SLOTS], place % SLOTS)
        return jnp.concatenate([bulk[place], beside], axis=1)

    for column in range(-1, 3):
        for q in range(MEMBERS):
            arrived[q, column + 1] = moved(wide(q, column + VELOCITY[q][0]), VELOCITY[q], -1)
    for column in range(-1, 3):
        i = column + 1
        for z, y in tiles(WIDE):
            inner = y.start == 0
            own = 0 <= column <= 1
            wanted = [
                q
                for q in range(MEMBERS)
                if 0 <= column - VELOCITY[q][0] <= 1 and (inner or VELOCITY[q][1])
            ]
            f = [state[q, i, z, y] for q in range(19)]
            g = [state[19 + q, i, z, y] for q in range(7)]
            fa = [arrived[q, i, z, y] for q in range(19)]
            ga = [arrived[19 + q, i, z, y] for q in range(7)]
            result = pull_back(
                f, g, fa, ga, wide_sides[0, i, z, y], wide_sides[1, i, z, y], wanted, inner and own
            )
            for q in wanted:
                earlier[q, i, z, y] = result[q]
            if inner and own:
                by_resistance[column, z, :] = part_resistance[column, z, :] + result["by"][0]
                by_conductivity[column, z, :] = part_conductivity[column, z, :] + result["by"][1]
    for c in range(2):
        for q in range(MEMBERS):
            velocity = VELOCITY[q]
            source = earlier[q, c + 1 + velocity[0]] if velocity[1] else earlier[q, c + 1 + velocity[0], :, :LANES]
            last[q, c] = moved(source, velocity, -1)[:, :LANES]
    for c in range(2):
        for z in halves():
            f = [flow[q, c, z, :] for q in range(19)]
            g = [heat[q, c, z, :] for q in range(7)]
            fa = [last[q, c, z, :] for q in range(19)]
            ga = [last[19 + q, c, z, :] for q in range(7)]
            narrow = pl.ds(0, LANES)
            result = pull_back(
                f, g, fa, ga, wide_sides[0, c + 1, z, narrow], wide_sides[1, c + 1, z, narrow], (), True
            )
            by_resistance[c, z, :] += result["by"][0]
            by_conductivity[c, z, :] += result["by"][1]


def floats(*shape):
    return jax.ShapeDtypeStruct(shape, jnp.float32)


def neighbours(value, axis):
    count = lax.axis_size(axis)
    up = [(i, (i + 1) % count) for i in range(count)]
    return up, [(target, source) for source, target in up]


PARAMS = pltpu.CompilerParams(vmem_limit_bytes=24 * 1024 * 1024)


def on_device(flow, heat, flow_weight, heat_weight, resistance, conductivity, solid):
    own, sides, right, left, strip = pl.pallas_call(
        first_kernel,
        out_shape=(
            floats(MEMBERS, 2, ZED, LANES),
            floats(2, 2, ZED, LANES),
            floats(BULK_ROWS + STRIP_ROWS, ZED, LANES),
            floats(BULK_ROWS + STRIP_ROWS, ZED, LANES),
            floats(STRIP_ROWS, ZED, LANES),
        ),
        compiler_params=PARAMS,
        name="collide_own",
    )(flow, heat, flow_weight, heat_weight, resistance, conductivity, solid)

    up, down = neighbours(strip, "gy")
    strip_left = lax.ppermute(strip, "gy", up)
    strip_right = lax.ppermute(strip, "gy", down)

    whole = pl.BlockSpec((STRIP_ROWS, ZED, LANES), lambda i: (0, 0, 0))
    tail = pl.BlockSpec((STRIP_ROWS, ZED, LANES), lambda i: (BULK_ROWS // STRIP_ROWS, 0, 0))
    anywhere = pl.BlockSpec(memory_space=pl.ANY)
    right, left, strip = pl.pallas_call(
        merge_kernel,
        grid=(1,),
        in_specs=[whole, whole, anywhere, anywhere],
        out_specs=[tail, tail, whole],
        out_shape=(
            floats(BULK_ROWS + STRIP_ROWS, ZED, LANES),
            floats(BULK_ROWS + STRIP_ROWS, ZED, LANES),
            floats(STRIP_ROWS, ZED, LANES),
        ),
        input_output_aliases={2: 0, 3: 1},
        name="merge_strips",
    )(strip_left, strip_right, right, left)

    up, down = neighbours(right, "gx")
    from_left = lax.ppermute(right, "gx", up)
    from_right = lax.ppermute(left, "gx", down)

    state, wide_sides, adjoint, part_resistance, part_conductivity, right, left = pl.pallas_call(
        second_kernel,
        out_shape=(
            floats(MEMBERS, 4, ZED, WIDE),
            floats(2, 4, ZED, WIDE),
            floats(MEMBERS, 2, ZED, WIDE),
            floats(2, ZED, LANES),
            floats(2, ZED, LANES),
            floats(ADJ_BULK + ADJ_ROWS, ZED, LANES),
            floats(ADJ_BULK + ADJ_ROWS, ZED, LANES),
        ),
        scratch_shapes=[
            pltpu.VMEM((MEMBERS, 4, ZED, WIDE), jnp.float32),
            pltpu.VMEM((MEMBERS, 2, ZED, WIDE), jnp.float32),
            pltpu.VMEM((MEMBERS, 2, ZED, WIDE), jnp.float32),
        ],
        compiler_params=PARAMS,
        name="forward_and_seed",
    )(own, sides, flow_weight, heat_weight, strip, from_left, from_right)

    from_left = lax.ppermute(right, "gx", up)
    from_right = lax.ppermute(left, "gx", down)

    return pl.pallas_call(
        third_kernel,
        out_shape=(floats(2, ZED, LANES), floats(2, ZED, LANES)),
        scratch_shapes=[
            pltpu.VMEM((MEMBERS, 4, ZED, WIDE), jnp.float32),
            pltpu.VMEM((MEMBERS, 4, ZED, WIDE), jnp.float32),
            pltpu.VMEM((MEMBERS, 2, ZED, LANES), jnp.float32),
        ],
        compiler_params=PARAMS,
        name="adjoint_steps",
    )(flow, heat, state, wide_sides, adjoint, part_resistance, part_conductivity, from_left, from_right)


def solution(mesh):
    split = P("gx", None, "gy")
    stacked = P(None, "gx", None, "gy")
    return jax.shard_map(
        on_device,
        mesh=mesh,
        in_specs=(stacked, stacked, stacked, split, split, split, split),
        out_specs=(split, split),
        check_vma=False,
    )
```

time: 220 us -> 61.4 us (0.28); the launches traced: 216 us -> 60.6 us
  local copies, waits for them, and re-layouts: 71.7 us -> 9.83 us
  starting transfers between devices: 86.2 us -> 28.3 us
  other arithmetic: 22.1 us -> 0 us
  matrix products: 16.1 us -> 0 us
  Pallas kernels: 0 us -> 7.75 us
  waiting for transfers between devices: 16.8 us -> 14 us
  between operations: 3.23 us -> 0.74 us
    ppermute x20 -> x6, starting transfers between devices: 86.2 us -> 28.3 us  [the longest x2 17 us: on_device(): from_right = lax.ppermute(left, 'gx', down)]
    slice x106 -> x0, local copies, waits for them, and re-layouts: 25 us -> none  [the longest x91 13.8 us: stream_rims(): shifted.append(jnp.roll(window_cells, step_z, axis=1))]
    unnamed x242 -> x32, local copies, waits for them, and re-layouts: 32.8 us -> 9.83 us
    dot_general x27 -> x0, matrix products: 16.1 us -> none  [the longest x7 5.72 us: collide(): jnp.einsum('qa,axzy->qxzy', vel_float, velocity_field, precision=highest)]
    ppermute x10 -> x0, local copies, waits for them, and re-layouts: 12.6 us -> none  [the longest x5 6.71 us: with_halo(): lax.ppermute(lax.slice_in_dim(block, 0, width, axis=dim), axis, backward)]
    pallas_call x0 -> x4, Pallas kernels: none -> 7.75 us  [the longest x1 4.07 us: on_device(): pl.pallas_call(second_kernel, out_shape=(floats(MEMBERS, 4, ZED, WIDE), f...]
    unnamed x65 -> x0, other arithmetic: 5.37 us -> none
    squeeze x13 -> x0, other arithmetic: 4.07 us -> none  [stream_rims(): padded[member, 1 - step_x:1 - step_x + width_x, :, 1 - step_y:1 - step_y...]
  transfers between devices with their start and end apart: 20 -> 6, of which waited for: 7 -> 5; matrix products, arithmetic and copies ran while one was open for 19% -> 0% of each run, Pallas kernels for 0% -> 0%
where the time goes in v1:
time: 61.4 us; the launch traced here: 60.6 us
  starting transfers between devices  28.3 us (46%)
  waiting for transfers between devices  14 us (23%)
  local copies, waits for them, and re-layouts  9.83 us (16%)
  Pallas kernels  7.75 us (13%)
  between operations  0.74 us (1%)
    ppermute x2, starting transfers between devices, on_device(): from_right = lax.ppermute(left, 'gx', down)  17 us
    unnamed x32, local copies, waits for them, and re-layouts  9.83 us
    ppermute x1, waiting for transfers between devices, on_device(): strip_left = lax.ppermute(strip, 'gy', up)  5.97 us
    ppermute x1, starting transfers between devices, on_device(): strip_right = lax.ppermute(strip, 'gy', down)  5.54 us
    ppermute x2, waiting for transfers between devices, on_device(): from_left = lax.ppermute(right, 'gx', up)  4.44 us
    pallas_call x1, Pallas kernels, on_device(): pl.pallas_call(second_kernel, out_shape=(floats(MEMBERS, 4, ZED, WIDE), f...  4.07 us
    ppermute x2, starting transfers between devices, on_device(): from_left = lax.ppermute(right, 'gx', up)  3.83 us
    ppermute x2, waiting for transfers between devices, on_device(): from_right = lax.ppermute(left, 'gx', down)  3.62 us
  transfers between devices with their start and end apart: 6, of which 5 were waited for; matrix products, arithmetic and copies ran while one was open for 0% of the time, Pallas kernels for 0%

profile of v1, /device:TPU:4, one launch (start us, length us, event | category | flops | bytes accessed | tf_op | source)
XLA Modules:
  0.0 60.6 jit_solution(562966611916455936)
XLA Ops:
  0.6 0.0 copy-start
  0.6 1.0 %copy-done = f32[19,2,16,128]{3,2,1,0:T(8,128)S(1)} copy-done((f32[19,2,16,128]{3,2,1,0:T(8,128)S(1)}, f32[19,2,16,128]{3,2,1,0:T(8,128)}, u32[]{:S(2)}) %copy-start) | copy-done | bytes 311320
  1.6 0.0 copy-start.2
  1.6 0.9 %copy-done.2 = f32[7,2,16,128]{3,2,1,0:T(8,128)S(1)} copy-done((f32[7,2,16,128]{3,2,1,0:T(8,128)S(1)}, f32[7,2,16,128]{3,2,1,0:T(8,128)}, u32[]{:S(2)}) %copy-start.2) | copy-done | bytes 114712
  2.5 0.0 copy-start.6
  2.5 0.8 %copy-done.6 = f32[3,2,16,128]{3,2,1,0:T(8,128)S(1)} copy-done((f32[3,2,16,128]{3,2,1,0:T(8,128)S(1)}, f32[3,2,16,128]{3,2,1,0:T(8,128)}, u32[]{:S(2)}) %copy-start.6) | copy-done | bytes 49176
  3.3 0.0 copy-start.8
  3.3 0.7 %copy-done.8 = f32[2,16,128]{2,1,0:T(8,128)S(1)} copy-done((f32[2,16,128]{2,1,0:T(8,128)S(1)}, f32[2,16,128]{2,1,0:T(8,128)}, u32[]{:S(2)}) %copy-start.8) | copy-done | bytes 16408
  4.0 0.0 copy-start.11
  4.0 0.7 %copy-done.11 = f32[2,16,128]{2,1,0:T(8,128)S(1)} copy-done((f32[2,16,128]{2,1,0:T(8,128)S(1)}, f32[2,16,128]{2,1,0:T(8,128)}, u32[]{:S(2)}) %copy-start.11) | copy-done | bytes 16408
  4.7 0.0 copy-start.12
  4.7 0.7 %copy-done.12 = f32[2,16,128]{2,1,0:T(8,128)S(1)} copy-done((f32[2,16,128]{2,1,0:T(8,128)S(1)}, f32[2,16,128]{2,1,0:T(8,128)}, u32[]{:S(2)}) %copy-start.12) | copy-done | bytes 16408
  5.5 0.0 copy-start.13
  5.5 0.7 %copy-done.13 = s32[2,16,128]{2,1,0:T(8,128)S(1)} copy-done((s32[2,16,128]{2,1,0:T(8,128)S(1)}, s32[2,16,128]{2,1,0:T(8,128)}, u32[]{:S(2)}) %copy-start.13) | copy-done | bytes 16408
  6.2 0.0 copy-start.1
  6.2 0.0 copy-start.3
  6.2 0.3 collide_own.1
  6.5 0.0 copy-start.4
  6.5 0.7 %copy-done.4 = f32[36,16,128]{2,1,0:T(8,128)} copy-done((f32[36,16,128]{2,1,0:T(8,128)}, f32[36,16,128]{2,1,0:T(8,128)S(1)}, u32[]{:S(2)}) %copy-start.4) | copy-done | bytes 294936
  7.2 0.0 copy-start.5
  7.2 0.7 %copy-done.5 = f32[36,16,128]{2,1,0:T(8,128)} copy-done((f32[36,16,128]{2,1,0:T(8,128)}, f32[36,16,128]{2,1,0:T(8,128)S(1)}, u32[]{:S(2)}) %copy-start.5) | copy-done | bytes 294936
  7.9 5.5 %collective-permute-start.1 = (f32[4,16,128]{2,1,0:T(8,128)S(1)}, f32[4,16,128]{2,1,0:T(8,128)S(1)}, u32[]{:S(2)}, u32[]{:S(2)}) collective-permute-start(f32[4,16,128]{2,1,0:T(8,128)S(1)} %get-tuple-element.19), channel_id=1, source_target_pairs={{1,0},{2,1},{3,2},{4,3},{5,4},{6,5},{7,6},{0,7},{9,8},{10,9},{11,1... | collective-permute-start | bytes 98312 | tf_op jit(solution)/shard_map/ppermute | solution.py:468
  13.4 1.9 %collective-permute-start = (f32[4,16,128]{2,1,0:T(8,128)S(1)}, f32[4,16,128]{2,1,0:T(8,128)S(1)}, u32[]{:S(2)}, u32[]{:S(2)}) collective-permute-start(f32[4,16,128]{2,1,0:T(8,128)S(1)} %get-tuple-element.19), channel_id=1, source_target_pairs={{0,1},{1,2},{2,3},{3,4},{4,5},{5,6},{6,7},{7,0},{8,9},{9,10},{10,1... | collective-permute-start | bytes 98312 | tf_op jit(solution)/shard_map/ppermute | solution.py:467
  15.4 0.0 collective-permute-done.1.from_right
  15.4 0.0 copy-start.14
  15.4 6.0 %collective-permute-done.from_left = f32[4,16,128]{2,1,0:T(8,128)S(1)} collective-permute-done((f32[4,16,128]{2,1,0:T(8,128)S(1)}, f32[4,16,128]{2,1,0:T(8,128)S(1)}, u32[]{:S(2)}, u32[]{:S(2)}) %collective-permute-start) | collective-permute-done | bytes 32800 | tf_op jit(solution)/shard_map/ppermute | solution.py:467
  21.4 0.0 copy-start.15
  21.4 0.0 copy-done.14
  21.4 0.6 %copy-done.15 = f32[4,16,128]{2,1,0:T(8,128)} copy-done((f32[4,16,128]{2,1,0:T(8,128)}, f32[4,16,128]{2,1,0:T(8,128)S(1)}, u32[]{:S(2)}) %copy-start.15) | copy-done | bytes 32792
  22.0 1.4 %merge_strips.1 = (f32[36,16,128]{2,1,0:T(8,128)}, f32[36,16,128]{2,1,0:T(8,128)}, f32[4,16,128]{2,1,0:T(8,128)}) custom-call(f32[4,16,128]{2,1,0:T(8,128)} %copy-done.15, f32[4,16,128]{2,1,0:T(8,128)} %copy-done.14, f32[36,16,128]{2,1,0:T(8,128)} %copy-done.4, f32[36,16,128]{2,1,0:T(8,128)} %copy-done.5), custom_call_target="tpu_custom_call", output_to_operand_aliasing={{0}: (2, {}), {1}: (3, {})} | custom-call | tf_op jit(solution)/shard_map/merge_strips/pallas_call | solution.py:473
  23.4 1.9 %collective-permute-start.2 = (f32[36,16,128]{2,1,0:T(8,128)}, f32[36,16,128]{2,1,0:T(8,128)S(1)}, u32[]{:S(2)}, u32[]{:S(2)}) collective-permute-start(f32[36,16,128]{2,1,0:T(8,128)} %get-tuple-element.23), channel_id=1, source_target_pairs={{0,8},{8,16},{16,24},{24,32},{32,40},{40,48},{48,56},{56,64},{64,7... | collective-permute-start | bytes 884744 | tf_op jit(solution)/shard_map/ppermute | solution.py:488
  25.3 9.6 %collective-permute-start.3 = (f32[36,16,128]{2,1,0:T(8,128)}, f32[36,16,128]{2,1,0:T(8,128)S(1)}, u32[]{:S(2)}, u32[]{:S(2)}) collective-permute-start(f32[36,16,128]{2,1,0:T(8,128)} %get-tuple-element.24), channel_id=1, source_target_pairs={{8,0},{16,8},{24,16},{32,24},{40,32},{48,40},{56,48},{64,56},{72,6... | collective-permute-start | bytes 884744 | tf_op jit(solution)/shard_map/ppermute | solution.py:489
  35.0 2.7 %collective-permute-done.2.from_left = f32[36,16,128]{2,1,0:T(8,128)S(1)} collective-permute-done((f32[36,16,128]{2,1,0:T(8,128)}, f32[36,16,128]{2,1,0:T(8,128)S(1)}, u32[]{:S(2)}, u32[]{:S(2)}) %collective-permute-start.2) | collective-permute-done | bytes 294944 | tf_op jit(solution)/shard_map/ppermute | solution.py:488
  37.7 1.9 %collective-permute-done.3.from_right = f32[36,16,128]{2,1,0:T(8,128)S(1)} collective-permute-done((f32[36,16,128]{2,1,0:T(8,128)}, f32[36,16,128]{2,1,0:T(8,128)S(1)}, u32[]{:S(2)}, u32[]{:S(2)}) %collective-permute-start.3) | collective-permute-done | bytes 294944 | tf_op jit(solution)/shard_map/ppermute | solution.py:489
  39.5 0.0 copy-start.7
  39.5 0.8 %copy-done.7 = f32[3,2,16,128]{3,2,1,0:T(8,128)S(1)} copy-done((f32[3,2,16,128]{3,2,1,0:T(8,128)S(1)}, f32[3,2,16,128]{3,2,1,0:T(8,128)}, u32[]{:S(2)}) %copy-start.7) | copy-done | bytes 49176
  40.3 0.0 copy-start.9
  40.3 0.7 %copy-done.9 = f32[2,16,128]{2,1,0:T(8,128)S(1)} copy-done((f32[2,16,128]{2,1,0:T(8,128)S(1)}, f32[2,16,128]{2,1,0:T(8,128)}, u32[]{:S(2)}) %copy-start.9) | copy-done | bytes 16408
  41.0 0.0 copy-start.10
  41.0 0.8 %copy-done.10 = f32[4,16,128]{2,1,0:T(8,128)S(1)} copy-done((f32[4,16,128]{2,1,0:T(8,128)S(1)}, f32[4,16,128]{2,1,0:T(8,128)}, u32[]{:S(2)}) %copy-start.10) | copy-done | bytes 32792
  41.8 4.1 %forward_and_seed.1 = (f32[26,4,16,256]{3,2,1,0:T(8,128)S(1)}, f32[2,4,16,256]{3,2,1,0:T(8,128)S(1)}, f32[26,2,16,256]{3,2,1,0:T(8,128)S(1)}, f32[2,16,128]{2,1,...) custom-call(f32[26,2,16,128]{3,2,1,0:T(8,128)S(1)} %get-tuple-element.17.own, ...), custom_call_target="tpu_custom_call" | custom-call | tf_op jit(solution)/shard_map/forward_and_seed/pallas_call | solution.py:491
  45.9 1.9 %collective-permute-start.4 = (f32[28,16,128]{2,1,0:T(8,128)S(1)}, f32[28,16,128]{2,1,0:T(8,128)S(1)}, u32[]{:S(2)}, u32[]{:S(2)}) collective-permute-start(f32[28,16,128]{2,1,0:T(8,128)S(1)} %get-tuple-element.30), channel_id=1, source_target_pairs={{0,8},{8,16},{16,24},{24,32},{32,40},{40,48},{48,56},{56,64},{64,7... | collective-permute-start | bytes 688136 | tf_op jit(solution)/shard_map/ppermute | solution.py:511
  47.8 7.3 %collective-permute-start.5 = (f32[28,16,128]{2,1,0:T(8,128)S(1)}, f32[28,16,128]{2,1,0:T(8,128)S(1)}, u32[]{:S(2)}, u32[]{:S(2)}) collective-permute-start(f32[28,16,128]{2,1,0:T(8,128)S(1)} %get-tuple-element.31), channel_id=1, source_target_pairs={{8,0},{16,8},{24,16},{32,24},{40,32},{48,40},{56,48},{64,56},{72,6... | collective-permute-start | bytes 688136 | tf_op jit(solution)/shard_map/ppermute | solution.py:512
  55.1 1.8 %collective-permute-done.4.from_left = f32[28,16,128]{2,1,0:T(8,128)S(1)} collective-permute-done((f32[28,16,128]{2,1,0:T(8,128)S(1)}, f32[28,16,128]{2,1,0:T(8,128)S(1)}, u32[]{:S(2)}, u32[]{:S(2)}) %collective-permute-start.4) | collective-permute-done | bytes 229408 | tf_op jit(solution)/shard_map/ppermute | solution.py:511
  56.9 1.8 %collective-permute-done.5.from_right = f32[28,16,128]{2,1,0:T(8,128)S(1)} collective-permute-done((f32[28,16,128]{2,1,0:T(8,128)S(1)}, f32[28,16,128]{2,1,0:T(8,128)S(1)}, u32[]{:S(2)}, u32[]{:S(2)}) %collective-permute-start.5) | collective-permute-done | bytes 229408 | tf_op jit(solution)/shard_map/ppermute | solution.py:512
  58.7 0.0 copy-done.1
  58.7 0.0 copy-done.3
  58.7 1.9 %adjoint_steps.1 = (f32[2,16,128]{2,1,0:T(8,128)}, f32[2,16,128]{2,1,0:T(8,128)}) custom-call(f32[19,2,16,128]{3,2,1,0:T(8,128)S(1)} %copy-done.1, f32[7,2,16,128]{3,2,1,0:T(8,128)S(1)} %copy-done.3, f32[26,4,16,256]{3,2,1,0:T(8,128)S(1)} %get-tuple-element.25.state, f32[2,4,16,256]{3,2,1,0:T(8,128)S(1)} %get-tuple-element.26.wide_sides, ...), custom_call_target="tpu_custom_call" | custom-call | tf_op jit(solution)/shard_map/adjoint_steps/pallas_call | solution.py:514
Async XLA Ops:
  0.6 1.0 %copy-start = (f32[19,2,16,128]{3,2,1,0:T(8,128)S(1)}, f32[19,2,16,128]{3,2,1,0:T(8,128)}, u32[]{:S(2)}) copy-start(f32[19,2,16,128]{3,2,1,0:T(8,128)} %flow.3) | copy-start | bytes 933892
  1.6 0.9 %copy-start.2 = (f32[7,2,16,128]{3,2,1,0:T(8,128)S(1)}, f32[7,2,16,128]{3,2,1,0:T(8,128)}, u32[]{:S(2)}) copy-start(f32[7,2,16,128]{3,2,1,0:T(8,128)} %heat.3) | copy-start | bytes 344068
  2.5 0.8 %copy-start.6 = (f32[3,2,16,128]{3,2,1,0:T(8,128)S(1)}, f32[3,2,16,128]{3,2,1,0:T(8,128)}, u32[]{:S(2)}) copy-start(f32[3,2,16,128]{3,2,1,0:T(8,128)} %flow_weight.3) | copy-start | bytes 147460
  3.3 0.7 %copy-start.8 = (f32[2,16,128]{2,1,0:T(8,128)S(1)}, f32[2,16,128]{2,1,0:T(8,128)}, u32[]{:S(2)}) copy-start(f32[2,16,128]{2,1,0:T(8,128)} %heat_weight.3) | copy-start | bytes 49156
  4.0 0.7 %copy-start.11 = (f32[2,16,128]{2,1,0:T(8,128)S(1)}, f32[2,16,128]{2,1,0:T(8,128)}, u32[]{:S(2)}) copy-start(f32[2,16,128]{2,1,0:T(8,128)} %resistance.1) | copy-start | bytes 49156
  4.7 0.7 %copy-start.12 = (f32[2,16,128]{2,1,0:T(8,128)S(1)}, f32[2,16,128]{2,1,0:T(8,128)}, u32[]{:S(2)}) copy-start(f32[2,16,128]{2,1,0:T(8,128)} %conductivity.1) | copy-start | bytes 49156
  5.5 0.7 %copy-start.13 = (s32[2,16,128]{2,1,0:T(8,128)S(1)}, s32[2,16,128]{2,1,0:T(8,128)}, u32[]{:S(2)}) copy-start(s32[2,16,128]{2,1,0:T(8,128)} %solid.1) | copy-start | bytes 49156
  6.2 52.5 %copy-start.1 = (f32[19,2,16,128]{3,2,1,0:T(8,128)S(1)}, f32[19,2,16,128]{3,2,1,0:T(8,128)}, u32[]{:S(2)}) copy-start(f32[19,2,16,128]{3,2,1,0:T(8,128)} %flow.3) | copy-start | bytes 933892
  6.2 52.5 %copy-start.3 = (f32[7,2,16,128]{3,2,1,0:T(8,128)S(1)}, f32[7,2,16,128]{3,2,1,0:T(8,128)}, u32[]{:S(2)}) copy-start(f32[7,2,16,128]{3,2,1,0:T(8,128)} %heat.3) | copy-start | bytes 344068
  6.5 0.7 %copy-start.4 = (f32[36,16,128]{2,1,0:T(8,128)}, f32[36,16,128]{2,1,0:T(8,128)S(1)}, u32[]{:S(2)}) copy-start(f32[36,16,128]{2,1,0:T(8,128)S(1)} %get-tuple-element.20.right_in) | copy-start | bytes 884740
  7.2 0.7 %copy-start.5 = (f32[36,16,128]{2,1,0:T(8,128)}, f32[36,16,128]{2,1,0:T(8,128)S(1)}, u32[]{:S(2)}) copy-start(f32[36,16,128]{2,1,0:T(8,128)S(1)} %get-tuple-element.21.left_in) | copy-start | bytes 884740
  7.9 7.5 %collective-permute-start.1 = (f32[4,16,128]{2,1,0:T(8,128)S(1)}, f32[4,16,128]{2,1,0:T(8,128)S(1)}, u32[]{:S(2)}, u32[]{:S(2)}) collective-permute-start(f32[4,16,128]{2,1,0:T(8,128)S(1)} %get-tuple-element.19), channel_id=1, source_target_pairs={{1,0},{2,1},{3,2},{4,3},{5,4},{6,5},{7,6},{0,7},{9,8},{10,9},{11,1... | collective-permute-start | bytes 98312 | tf_op jit(solution)/shard_map/ppermute | solution.py:468
  13.4 7.9 %collective-permute-start = (f32[4,16,128]{2,1,0:T(8,128)S(1)}, f32[4,16,128]{2,1,0:T(8,128)S(1)}, u32[]{:S(2)}, u32[]{:S(2)}) collective-permute-start(f32[4,16,128]{2,1,0:T(8,128)S(1)} %get-tuple-element.19), channel_id=1, source_target_pairs={{0,1},{1,2},{2,3},{3,4},{4,5},{5,6},{6,7},{7,0},{8,9},{9,10},{10,1... | collective-permute-start | bytes 98312 | tf_op jit(solution)/shard_map/ppermute | solution.py:467
  15.4 6.0 %copy-start.14 = (f32[4,16,128]{2,1,0:T(8,128)}, f32[4,16,128]{2,1,0:T(8,128)S(1)}, u32[]{:S(2)}) copy-start(f32[4,16,128]{2,1,0:T(8,128)S(1)} %collective-permute-done.1.from_right) | copy-start | bytes 98308
  21.4 0.6 %copy-start.15 = (f32[4,16,128]{2,1,0:T(8,128)}, f32[4,16,128]{2,1,0:T(8,128)S(1)}, u32[]{:S(2)}) copy-start(f32[4,16,128]{2,1,0:T(8,128)S(1)} %collective-permute-done.from_left) | copy-start | bytes 98308
  23.4 14.2 %collective-permute-start.2 = (f32[36,16,128]{2,1,0:T(8,128)}, f32[36,16,128]{2,1,0:T(8,128)S(1)}, u32[]{:S(2)}, u32[]{:S(2)}) collective-permute-start(f32[36,16,128]{2,1,0:T(8,128)} %get-tuple-element.23), channel_id=1, source_target_pairs={{0,8},{8,16},{16,24},{24,32},{32,40},{40,48},{48,56},{56,64},{64,7... | collective-permute-start | bytes 884744 | tf_op jit(solution)/shard_map/ppermute | solution.py:488
  25.3 14.2 %collective-permute-start.3 = (f32[36,16,128]{2,1,0:T(8,128)}, f32[36,16,128]{2,1,0:T(8,128)S(1)}, u32[]{:S(2)}, u32[]{:S(2)}) collective-permute-start(f32[36,16,128]{2,1,0:T(8,128)} %get-tuple-element.24), channel_id=1, source_target_pairs={{8,0},{16,8},{24,16},{32,24},{40,32},{48,40},{56,48},{64,56},{72,6... | collective-permute-start | bytes 884744 | tf_op jit(solution)/shard_map/ppermute | solution.py:489
  39.5 0.8 %copy-start.7 = (f32[3,2,16,128]{3,2,1,0:T(8,128)S(1)}, f32[3,2,16,128]{3,2,1,0:T(8,128)}, u32[]{:S(2)}) copy-start(f32[3,2,16,128]{3,2,1,0:T(8,128)} %flow_weight.3) | copy-start | bytes 147460
  40.3 0.7 %copy-start.9 = (f32[2,16,128]{2,1,0:T(8,128)S(1)}, f32[2,16,128]{2,1,0:T(8,128)}, u32[]{:S(2)}) copy-start(f32[2,16,128]{2,1,0:T(8,128)} %heat_weight.3) | copy-start | bytes 49156
  41.0 0.8 %copy-start.10 = (f32[4,16,128]{2,1,0:T(8,128)S(1)}, f32[4,16,128]{2,1,0:T(8,128)}, u32[]{:S(2)}) copy-start(f32[4,16,128]{2,1,0:T(8,128)} %get-tuple-element.22.strip) | copy-start | bytes 98308
  45.9 11.0 %collective-permute-start.4 = (f32[28,16,128]{2,1,0:T(8,128)S(1)}, f32[28,16,128]{2,1,0:T(8,128)S(1)}, u32[]{:S(2)}, u32[]{:S(2)}) collective-permute-start(f32[28,16,128]{2,1,0:T(8,128)S(1)} %get-tuple-element.30), channel_id=1, source_target_pairs={{0,8},{8,16},{16,24},{24,32},{32,40},{40,48},{48,56},{56,64},{64,7... | collective-permute-start | bytes 688136 | tf_op jit(solution)/shard_map/ppermute | solution.py:511
  47.8 10.8 %collective-permute-start.5 = (f32[28,16,128]{2,1,0:T(8,128)S(1)}, f32[28,16,128]{2,1,0:T(8,128)S(1)}, u32[]{:S(2)}, u32[]{:S(2)}) collective-permute-start(f32[28,16,128]{2,1,0:T(8,128)S(1)} %get-tuple-element.31), channel_id=1, source_target_pairs={{8,0},{16,8},{24,16},{32,24},{40,32},{48,40},{56,48},{64,56},{72,6... | collective-permute-start | bytes 688136 | tf_op jit(solution)/shard_map/ppermute | solution.py:512

commit v2 on v1

--- a/solution.py
+++ b/solution.py
@@ -43,6 +43,7 @@
 
 SLOTS = LANES // (2 * EDGE)
 STRIP_ROWS = 2 * FIELDS // SLOTS
+HALF_ROWS = STRIP_ROWS // 2
 ADJ_ROWS = -(-MEMBERS // SLOTS)
 
 
@@ -247,7 +248,47 @@
     return [pl.ds(0, 8), pl.ds(8, 8)]
 
 
-def first_kernel(flow, heat, flow_weight, heat_weight, resistance, conductivity, solid, own, sides, right, left, strip):
+def low_lanes():
+    return lax.broadcasted_iota(jnp.int32, (ZED, LANES), 1) % (2 * EDGE) < EDGE
+
+
+def ring_place(axis):
+    count = lax.axis_size(axis)
+    place = lax.axis_index(axis)
+    return lax.rem(place + count - 1, count), lax.rem(place + 1, count)
+
+
+def either_way(move):
+    first = lax.rem(lax.axis_index("gx"), 2) == 0
+    pl.when(first)(lambda: move(True))
+    pl.when(jnp.logical_not(first))(lambda: move(False))
+
+
+def copy_rows(target, source):
+    for row in range(source.shape[0]):
+        target[row] = source[row]
+
+
+def first_kernel(
+    flow_in, heat_in, flow_weight_in, heat_weight_in, resistance_in, conductivity_in, solid_in,
+    own, far, near, strips,
+    right, left, flow, heat, flow_weight, heat_weight, resistance, conductivity, solid, arrived,
+):
+    pairs = [
+        (flow_in, flow),
+        (heat_in, heat),
+        (resistance_in, resistance),
+        (conductivity_in, conductivity),
+        (solid_in, solid),
+        (flow_weight_in, flow_weight),
+        (heat_weight_in, heat_weight),
+    ]
+    copies = [pltpu.make_async_copy(a, b, arrived.at[k]) for k, (a, b) in enumerate(pairs)]
+    for copy in copies:
+        copy.start()
+    strips[...] = jnp.zeros(strips.shape, jnp.float32)
+    for copy in copies:
+        copy.wait()
     for c in range(2):
         for z in halves():
             mobility = jnp.where(solid[c, z, :] != 0, 0.0, 1.0 / (1.0 + resistance[c, z, :]))
@@ -255,48 +296,64 @@
             f = [flow[q, c, z, :] for q in range(19)]
             g = [heat[q, c, z, :] for q in range(7)]
             after = collide(f, g, mobility, rate)
-            sides[0, c, z, :] = mobility
-            sides[1, c, z, :] = rate
             more = [mobility, rate] + [flow_weight[k, c, z, :] for k in range(3)] + [heat_weight[c, z, :]]
             for k, value in enumerate(after + more):
-                if k < MEMBERS:
-                    own[k, c, z, :] = value
                 if (k, c) in TO_RIGHT:
                     right[TO_RIGHT[k, c], z, :] = value
-                if (k, c) in TO_LEFT:
+                else:
                     left[TO_LEFT[k, c], z, :] = value
-    values = []
-    for c in range(2):
-        values += [own[q, c] for q in range(MEMBERS)]
-        values += [sides[0, c], sides[1, c]]
-        values += [flow_weight[k, c] for k in range(3)] + [heat_weight[c]]
-    for row, value in enumerate(pack_rows(values)):
-        strip[row] = value
-
-
-def merge_kernel(from_left, from_right, right_in, left_in, right, left, strip):
-    del right_in, left_in
-    lane = lax.broadcasted_iota(jnp.int32, (ZED, LANES), 1)
-    low = lane % (2 * EDGE) < EDGE
-    for row in range(STRIP_ROWS):
-        value = jnp.where(low, from_left[row], from_right[row])
-        right[row] = value
-        left[row] = value
-        strip[row] = value
-
-
-def wide_field(k, column, own_value, strip, from_left, from_right):
+
+    for k in range(BULK_ROWS):
+        own[k] = right[k]
+        own[k + BULK_ROWS] = left[k]
+
+    def send(first):
+        copy_rows(far, left if first else right)
+        copy_rows(near, right if first else left)
+
+    either_way(send)
+    rows = pack_rows([right[k] for k in range(BULK_ROWS)] + [left[k] for k in range(BULK_ROWS)])
+    low = low_lanes()
+    below, above = ring_place("gy")
+    for k in range(HALF_ROWS):
+        strips[above, k] = jnp.where(low, rows[k], turn(rows[k + HALF_ROWS], EDGE, 1))
+        strips[below, k] = jnp.where(low, turn(rows[k], -EDGE, 1), rows[k + HALF_ROWS])
+
+
+def merge_kernel(strips, own_in, far_in, near_in, own, far, near, strip, sent):
+    del own_in, far_in, near_in
+    low = low_lanes()
+    below, above = ring_place("gy")
+    for k in range(HALF_ROWS):
+        under, over = strips[below, k], strips[above, k]
+        strip[k] = jnp.where(low, under, turn(over, EDGE, 1))
+        strip[k + HALF_ROWS] = jnp.where(low, turn(under, -EDGE, 1), over)
+    tail = pl.ds(BULK_ROWS, HALF_ROWS)
+    rightward = HALF_ROWS * lax.rem(lax.axis_index("gx"), 2)
+    copies = [
+        pltpu.make_async_copy(strip.at[pl.ds(HALF_ROWS - rightward, HALF_ROWS)], far.at[tail], sent.at[0]),
+        pltpu.make_async_copy(strip.at[pl.ds(rightward, HALF_ROWS)], near.at[tail], sent.at[1]),
+        pltpu.make_async_copy(strip, own.at[pl.ds(2 * BULK_ROWS, STRIP_ROWS)], sent.at[2]),
+    ]
+    for copy in copies:
+        copy.start()
+    for copy in copies:
+        copy.wait()
+
+
+def wide_field(k, column, own, from_left, from_right):
     if column < 0:
-        c, bulk, rows = column + 2, from_left, TO_RIGHT
-        strips, start = from_left, BULK_ROWS
+        place = TO_RIGHT[k, column + 2]
+        main, strips, start = from_left[place], from_left, BULK_ROWS
     elif column > 1:
-        c, bulk, rows = column - 2, from_right, TO_LEFT
-        strips, start = from_right, BULK_ROWS
+        place = TO_LEFT[k, column - 2]
+        main, strips, start = from_right[place], from_right, BULK_ROWS
+    elif (k, column) in TO_RIGHT:
+        place = TO_RIGHT[k, column]
+        main, strips, start = own[place], own, 2 * BULK_ROWS
     else:
-        c, bulk, rows = column, None, None
-        strips, start = strip, 0
-    main = own_value(k, c) if bulk is None else bulk[rows[k, c]]
-    place = c * FIELDS + k
+        place = TO_LEFT[k, column]
+        main, strips, start = own[BULK_ROWS + place], own, 2 * BULK_ROWS + HALF_ROWS
     beside = unpack(strips[start + place // SLOTS], place % SLOTS)
     return jnp.concatenate([main, beside], axis=1)
 
@@ -311,19 +368,18 @@
 
 
 def second_kernel(
-    own, sides, flow_weight, heat_weight, strip, from_left, from_right,
-    state, wide_sides, adjoint, by_resistance, by_conductivity, right, left,
-    after, later, seed,
+    own, from_far, from_near,
+    state, wide_sides, adjoint, by_resistance, by_conductivity, far, near,
+    from_left, from_right, after, later, seed, right, left,
 ):
-    def own_value(k, c):
-        if k < MEMBERS:
-            return own[k, c]
-        if k < WEIGHT:
-            return sides[k - MOBILITY, c]
-        return flow_weight[k - WEIGHT, c] if k < WEIGHT + 3 else heat_weight[c]
+    def receive(first):
+        copy_rows(from_left, from_far if first else from_near)
+        copy_rows(from_right, from_near if first else from_far)
+
+    either_way(receive)
 
     def wide(k, column):
-        return wide_field(k, column, own_value, strip, from_left, from_right)
+        return wide_field(k, column, own, from_left, from_right)
 
     for column in range(-1, 3):
         i = column + 1
@@ -378,12 +434,24 @@
         for row, value in enumerate(pack_rows(values)):
             side[ADJ_BULK + row] = value
 
+    def send(first):
+        copy_rows(far, left if first else right)
+        copy_rows(near, right if first else left)
+
+    either_way(send)
+
 
 def third_kernel(
-    flow, heat, state, wide_sides, adjoint, part_resistance, part_conductivity, from_left, from_right,
+    flow, heat, state, wide_sides, adjoint, part_resistance, part_conductivity, from_far, from_near,
     by_resistance, by_conductivity,
-    arrived, earlier, last,
+    from_left, from_right, arrived, earlier, last,
 ):
+    def receive(first):
+        copy_rows(from_left, from_far if first else from_near)
+        copy_rows(from_right, from_near if first else from_far)
+
+    either_way(receive)
+
     def wide(q, column):
         if 0 <= column <= 1:
             return adjoint[q, column]
@@ -440,55 +508,68 @@
     return jax.ShapeDtypeStruct(shape, jnp.float32)
 
 
-def neighbours(value, axis):
-    count = lax.axis_size(axis)
-    up = [(i, (i + 1) % count) for i in range(count)]
-    return up, [(target, source) for source, target in up]
-
-
+def vmem(*shape):
+    return pltpu.VMEM(shape, jnp.float32)
+
+
+def swap_along_x(far, near):
+    count = lax.axis_size("gx")
+    across = [(i, (i + (1 if i % 2 else -1)) % count) for i in range(count)]
+    within = [(i, i ^ 1) for i in range(count)]
+    return lax.ppermute(far, "gx", across), lax.ppermute(near, "gx", within)
+
+
+FIRST_PARAMS = pltpu.CompilerParams(vmem_limit_bytes=56 * 1024 * 1024)
 PARAMS = pltpu.CompilerParams(vmem_limit_bytes=24 * 1024 * 1024)
+SENT = BULK_ROWS + HALF_ROWS
+OWN_ROWS = 2 * BULK_ROWS + STRIP_ROWS
+ADJ_SENT = ADJ_BULK + ADJ_ROWS
 
 
 def on_device(flow, heat, flow_weight, heat_weight, resistance, conductivity, solid):
-    own, sides, right, left, strip = pl.pallas_call(
+    rings = lax.axis_size("gy")
+    own, far, near, strips = pl.pallas_call(
         first_kernel,
+        in_specs=[pl.BlockSpec(memory_space=pltpu.HBM)] * 7,
         out_shape=(
-            floats(MEMBERS, 2, ZED, LANES),
-            floats(2, 2, ZED, LANES),
-            floats(BULK_ROWS + STRIP_ROWS, ZED, LANES),
-            floats(BULK_ROWS + STRIP_ROWS, ZED, LANES),
-            floats(STRIP_ROWS, ZED, LANES),
+            floats(OWN_ROWS, ZED, LANES),
+            floats(SENT, ZED, LANES),
+            floats(SENT, ZED, LANES),
+            floats(rings, HALF_ROWS, ZED, LANES),
         ),
-        compiler_params=PARAMS,
+        scratch_shapes=[
+            vmem(BULK_ROWS, ZED, LANES),
+            vmem(BULK_ROWS, ZED, LANES),
+            vmem(19, 2, ZED, LANES),
+            vmem(7, 2, ZED, LANES),
+            vmem(3, 2, ZED, LANES),
+            vmem(2, ZED, LANES),
+            vmem(2, ZED, LANES),
+            vmem(2, ZED, LANES),
+            pltpu.VMEM((2, ZED, LANES), jnp.int32),
+            pltpu.SemaphoreType.DMA((7,)),
+        ],
+        compiler_params=FIRST_PARAMS,
         name="collide_own",
     )(flow, heat, flow_weight, heat_weight, resistance, conductivity, solid)
 
-    up, down = neighbours(strip, "gy")
-    strip_left = lax.ppermute(strip, "gy", up)
-    strip_right = lax.ppermute(strip, "gy", down)
-
-    whole = pl.BlockSpec((STRIP_ROWS, ZED, LANES), lambda i: (0, 0, 0))
-    tail = pl.BlockSpec((STRIP_ROWS, ZED, LANES), lambda i: (BULK_ROWS // STRIP_ROWS, 0, 0))
-    anywhere = pl.BlockSpec(memory_space=pl.ANY)
-    right, left, strip = pl.pallas_call(
+    strips = lax.all_to_all(strips, "gy", 0, 0)
+
+    in_place = pl.BlockSpec(memory_space=pltpu.HBM)
+    own, far, near = pl.pallas_call(
         merge_kernel,
-        grid=(1,),
-        in_specs=[whole, whole, anywhere, anywhere],
-        out_specs=[tail, tail, whole],
-        out_shape=(
-            floats(BULK_ROWS + STRIP_ROWS, ZED, LANES),
-            floats(BULK_ROWS + STRIP_ROWS, ZED, LANES),
-            floats(STRIP_ROWS, ZED, LANES),
-        ),
-        input_output_aliases={2: 0, 3: 1},
+        in_specs=[pl.BlockSpec(memory_space=pltpu.VMEM), in_place, in_place, in_place],
+        out_specs=[in_place, in_place, in_place],
+        out_shape=(floats(OWN_ROWS, ZED, LANES), floats(SENT, ZED, LANES), floats(SENT, ZED, LANES)),
+        scratch_shapes=[vmem(STRIP_ROWS, ZED, LANES), pltpu.SemaphoreType.DMA((3,))],
+        input_output_aliases={1: 0, 2: 1, 3: 2},
+        compiler_params=FIRST_PARAMS,
         name="merge_strips",
-    )(strip_left, strip_right, right, left)
-
-    up, down = neighbours(right, "gx")
-    from_left = lax.ppermute(right, "gx", up)
-    from_right = lax.ppermute(left, "gx", down)
-
-    state, wide_sides, adjoint, part_resistance, part_conductivity, right, left = pl.pallas_call(
+    )(strips, own, far, near)
+
+    from_far, from_near = swap_along_x(far, near)
+
+    state, wide_sides, adjoint, part_resistance, part_conductivity, far, near = pl.pallas_call(
         second_kernel,
         out_shape=(
             floats(MEMBERS, 4, ZED, WIDE),
@@ -496,32 +577,37 @@
             floats(MEMBERS, 2, ZED, WIDE),
             floats(2, ZED, LANES),
             floats(2, ZED, LANES),
-            floats(ADJ_BULK + ADJ_ROWS, ZED, LANES),
-            floats(ADJ_BULK + ADJ_ROWS, ZED, LANES),
+            floats(ADJ_SENT, ZED, LANES),
+            floats(ADJ_SENT, ZED, LANES),
         ),
         scratch_shapes=[
-            pltpu.VMEM((MEMBERS, 4, ZED, WIDE), jnp.float32),
-            pltpu.VMEM((MEMBERS, 2, ZED, WIDE), jnp.float32),
-            pltpu.VMEM((MEMBERS, 2, ZED, WIDE), jnp.float32),
+            vmem(SENT, ZED, LANES),
+            vmem(SENT, ZED, LANES),
+            vmem(MEMBERS, 4, ZED, WIDE),
+            vmem(MEMBERS, 2, ZED, WIDE),
+            vmem(MEMBERS, 2, ZED, WIDE),
+            vmem(ADJ_SENT, ZED, LANES),
+            vmem(ADJ_SENT, ZED, LANES),
         ],
         compiler_params=PARAMS,
         name="forward_and_seed",
-    )(own, sides, flow_weight, heat_weight, strip, from_left, from_right)
-
-    from_left = lax.ppermute(right, "gx", up)
-    from_right = lax.ppermute(left, "gx", down)
+    )(own, from_far, from_near)
+
+    from_far, from_near = swap_along_x(far, near)
 
     return pl.pallas_call(
         third_kernel,
         out_shape=(floats(2, ZED, LANES), floats(2, ZED, LANES)),
         scratch_shapes=[
-            pltpu.VMEM((MEMBERS, 4, ZED, WIDE), jnp.float32),
-            pltpu.VMEM((MEMBERS, 4, ZED, WIDE), jnp.float32),
-            pltpu.VMEM((MEMBERS, 2, ZED, LANES), jnp.float32),
+            vmem(ADJ_SENT, ZED, LANES),
+            vmem(ADJ_SENT, ZED, LANES),
+            vmem(MEMBERS, 4, ZED, WIDE),
+            vmem(MEMBERS, 4, ZED, WIDE),
+            vmem(MEMBERS, 2, ZED, LANES),
         ],
         compiler_params=PARAMS,
         name="adjoint_steps",
-    )(flow, heat, state, wide_sides, adjoint, part_resistance, part_conductivity, from_left, from_right)
+    )(flow, heat, state, wide_sides, adjoint, part_resistance, part_conductivity, from_far, from_near)
 
 
 def solution(mesh):

time: 61.4 us -> 52.3 us (0.85)
  the two profiles are of different devices: /device:TPU:4 before, /device:TPU:1 now
where the time goes in v2:
time: 52.3 us; the launch traced here: 51.9 us
  starting transfers between devices  25.9 us (50%)
  blocking collectives  11.6 us (22%)
  Pallas kernels  10.1 us (19%)
  waiting for transfers between devices  2.45 us (5%)
  local copies, waits for them, and re-layouts  1.06 us (2%)
  between operations  0.72 us (1%)
    ppermute x4, starting transfers between devices, swap_along_x(): return (lax.ppermute(far, 'gx', across), lax.ppermute(near, 'gx', within))  25.9 us
    all_to_all x1, blocking collectives, on_device(): strips = lax.all_to_all(strips, 'gy', 0, 0)  11.6 us
    pallas_call x1, Pallas kernels, on_device(): pl.pallas_call(second_kernel, out_shape=(floats(MEMBERS, 4, ZED, WIDE), f...  4.15 us
    ppermute x4, waiting for transfers between devices, swap_along_x(): return (lax.ppermute(far, 'gx', across), lax.ppermute(near, 'gx', within))  2.45 us
    pallas_call x1, Pallas kernels, on_device(): pl.pallas_call(first_kernel, in_specs=[pl.BlockSpec(memory_space=pltpu.HB...  2.37 us
    pallas_call x1, Pallas kernels, on_device(): pl.pallas_call(third_kernel, out_shape=(floats(2, ZED, LANES), floats(2,...  1.97 us
    pallas_call x1, Pallas kernels, on_device(): pl.pallas_call(merge_kernel, in_specs=[pl.BlockSpec(memory_space=pltpu.VM...  1.63 us
    unnamed x6, local copies, waits for them, and re-layouts  1.06 us
  transfers between devices with their start and end apart: 4, of which 2 were waited for; matrix products, arithmetic and copies ran while one was open for 0% of the time, Pallas kernels for 0%

profile of v2, /device:TPU:1, one launch (start us, length us, event | category | flops | bytes accessed | tf_op | source)
XLA Modules:
  0.0 51.9 jit_solution(17035559501626295296)
XLA Ops:
  0.6 0.0 copy-start.2
  0.6 0.0 copy-start.1
  0.7 2.4 %collide_own.1 = (f32[68,16,128]{2,1,0:T(8,128)}, f32[34,16,128]{2,1,0:T(8,128)}, f32[34,16,128]{2,1,0:T(8,128)}, f32[8,2,16,128]{3,2,1,0:T(8,128)}) custom-call(f32[19,2,16,128]{3,2,1,0:T(8,128)} %flow.1, f32[7,2,16,128]{3,2,1,0:T(8,128)} %heat.1, f32[3,2,16,128]{3,2,1,0:T(8,128)} %flow_weight_in.1, f32[2,16,128]{2,1,0:T(8,128)} %heat_weight_in.1, ...), custom_call_target="tpu_custom_call" | custom-call | tf_op jit(solution)/shard_map/collide_own/pallas_call | solution.py:531
  3.0 11.6 %all_to_all.5.strips = f32[8,2,16,128]{3,2,1,0:T(8,128)} all-to-all(f32[8,2,16,128]{3,2,1,0:T(8,128)} %get-tuple-element.16), channel_id=1, replica_groups=mesh['gx'=64,'gy'=8] {'gy'}, dimensions={0} | all-to-all | bytes 262144 | tf_op jit(solution)/shard_map/all_to_all | solution.py:556
  14.6 1.6 %merge_strips.1 = (f32[68,16,128]{2,1,0:T(8,128)}, f32[34,16,128]{2,1,0:T(8,128)}, f32[34,16,128]{2,1,0:T(8,128)}) custom-call(f32[8,2,16,128]{3,2,1,0:T(8,128)} %all_to_all.5.strips, f32[68,16,128]{2,1,0:T(8,128)} %get-tuple-element.17.own_in, f32[34,16,128]{2,1,0:T(8,128)} %get-tuple-element.18.far_in, ...), custom_call_target="tpu_custom_call", output_to_operand_aliasing={{0}: (1, {}), {1}: (2, {}), {2}: (3, {})} | custom-call | tf_op jit(solution)/shard_map/merge_strips/pallas_call | solution.py:559
  16.3 5.5 %collective-permute-start = (f32[34,16,128]{2,1,0:T(8,128)}, f32[34,16,128]{2,1,0:T(8,128)S(1)}, u32[]{:S(2)}, u32[]{:S(2)}) collective-permute-start(f32[34,16,128]{2,1,0:T(8,128)} %get-tuple-element.21), channel_id=1, source_target_pairs={{0,504},{8,16},{16,8},{24,32},{32,24},{40,48},{48,40},{56,64},{64,... | collective-permute-start | bytes 835592 | tf_op jit(solution)/shard_map/ppermute | solution.py:519
  21.8 10.1 %collective-permute-start.1 = (f32[34,16,128]{2,1,0:T(8,128)}, f32[34,16,128]{2,1,0:T(8,128)S(1)}, u32[]{:S(2)}, u32[]{:S(2)}) collective-permute-start(f32[34,16,128]{2,1,0:T(8,128)} %get-tuple-element.22), channel_id=1, source_target_pairs={{0,8},{8,0},{16,24},{24,16},{32,40},{40,32},{48,56},{56,48},{64,72... | collective-permute-start | bytes 835592 | tf_op jit(solution)/shard_map/ppermute | solution.py:519
  31.9 0.0 collective-permute-done.from_far
  31.9 1.4 %collective-permute-done.1.from_near = f32[34,16,128]{2,1,0:T(8,128)S(1)} collective-permute-done((f32[34,16,128]{2,1,0:T(8,128)}, f32[34,16,128]{2,1,0:T(8,128)S(1)}, u32[]{:S(2)}, u32[]{:S(2)}) %collective-permute-start.1) | collective-permute-done | bytes 278560 | tf_op jit(solution)/shard_map/ppermute | solution.py:519
  33.3 0.0 copy-start
  33.3 1.1 %copy-done = f32[68,16,128]{2,1,0:T(8,128)S(1)} copy-done((f32[68,16,128]{2,1,0:T(8,128)S(1)}, f32[68,16,128]{2,1,0:T(8,128)}, u32[]{:S(2)}) %copy-start) | copy-done | bytes 557080
  34.3 4.1 %forward_and_seed.1 = (f32[26,4,16,256]{3,2,1,0:T(8,128)S(1)}, f32[2,4,16,256]{3,2,1,0:T(8,128)S(1)}, f32[26,2,16,256]{3,2,1,0:T(8,128)S(1)}, f32[2,16,128]{2,1,...) custom-call(f32[68,16,128]{2,1,0:T(8,128)S(1)} %copy-done, ...), custom_call_target="tpu_custom_call" | custom-call | tf_op jit(solution)/shard_map/forward_and_seed/pallas_call | solution.py:572
  38.5 1.9 %collective-permute-start.2 = (f32[28,16,128]{2,1,0:T(8,128)S(1)}, f32[28,16,128]{2,1,0:T(8,128)S(1)}, u32[]{:S(2)}, u32[]{:S(2)}) collective-permute-start(f32[28,16,128]{2,1,0:T(8,128)S(1)} %get-tuple-element.28), channel_id=1, source_target_pairs={{0,504},{8,16},{16,8},{24,32},{32,24},{40,48},{48,40},{56,64},{64,... | collective-permute-start | bytes 688136 | tf_op jit(solution)/shard_map/ppermute | solution.py:519
  40.4 8.4 %collective-permute-start.3 = (f32[28,16,128]{2,1,0:T(8,128)S(1)}, f32[28,16,128]{2,1,0:T(8,128)S(1)}, u32[]{:S(2)}, u32[]{:S(2)}) collective-permute-start(f32[28,16,128]{2,1,0:T(8,128)S(1)} %get-tuple-element.29), channel_id=1, source_target_pairs={{0,8},{8,0},{16,24},{24,16},{32,40},{40,32},{48,56},{56,48},{64,72... | collective-permute-start | bytes 688136 | tf_op jit(solution)/shard_map/ppermute | solution.py:519
  48.8 0.0 collective-permute-done.2.from_far
  48.8 1.1 %collective-permute-done.3.from_near = f32[28,16,128]{2,1,0:T(8,128)S(1)} collective-permute-done((f32[28,16,128]{2,1,0:T(8,128)S(1)}, f32[28,16,128]{2,1,0:T(8,128)S(1)}, u32[]{:S(2)}, u32[]{:S(2)}) %collective-permute-start.3) | collective-permute-done | bytes 229408 | tf_op jit(solution)/shard_map/ppermute | solution.py:519
  49.9 0.0 copy-done.2
  49.9 0.0 copy-done.1
  49.9 2.0 %adjoint_steps.1 = (f32[2,16,128]{2,1,0:T(8,128)}, f32[2,16,128]{2,1,0:T(8,128)}) custom-call(f32[19,2,16,128]{3,2,1,0:T(8,128)S(1)} %copy-done.1, f32[7,2,16,128]{3,2,1,0:T(8,128)S(1)} %copy-done.2, f32[26,4,16,256]{3,2,1,0:T(8,128)S(1)} %get-tuple-element.23.state, f32[2,4,16,256]{3,2,1,0:T(8,128)S(1)} %get-tuple-element.24.wide_sides, ...), custom_call_target="tpu_custom_call" | custom-call | tf_op jit(solution)/shard_map/adjoint_steps/pallas_call | solution.py:598
Async XLA Ops:
  0.6 49.3 %copy-start.2 = (f32[7,2,16,128]{3,2,1,0:T(8,128)S(1)}, f32[7,2,16,128]{3,2,1,0:T(8,128)}, u32[]{:S(2)}) copy-start(f32[7,2,16,128]{3,2,1,0:T(8,128)} %heat.1) | copy-start | bytes 344068
  0.6 49.3 %copy-start.1 = (f32[19,2,16,128]{3,2,1,0:T(8,128)S(1)}, f32[19,2,16,128]{3,2,1,0:T(8,128)}, u32[]{:S(2)}) copy-start(f32[19,2,16,128]{3,2,1,0:T(8,128)} %flow.1) | copy-start | bytes 933892
  16.3 15.6 %collective-permute-start = (f32[34,16,128]{2,1,0:T(8,128)}, f32[34,16,128]{2,1,0:T(8,128)S(1)}, u32[]{:S(2)}, u32[]{:S(2)}) collective-permute-start(f32[34,16,128]{2,1,0:T(8,128)} %get-tuple-element.21), channel_id=1, source_target_pairs={{0,504},{8,16},{16,8},{24,32},{32,24},{40,48},{48,40},{56,64},{64,... | collective-permute-start | bytes 835592 | tf_op jit(solution)/shard_map/ppermute | solution.py:519
  21.8 11.5 %collective-permute-start.1 = (f32[34,16,128]{2,1,0:T(8,128)}, f32[34,16,128]{2,1,0:T(8,128)S(1)}, u32[]{:S(2)}, u32[]{:S(2)}) collective-permute-start(f32[34,16,128]{2,1,0:T(8,128)} %get-tuple-element.22), channel_id=1, source_target_pairs={{0,8},{8,0},{16,24},{24,16},{32,40},{40,32},{48,56},{56,48},{64,72... | collective-permute-start | bytes 835592 | tf_op jit(solution)/shard_map/ppermute | solution.py:519
  33.3 1.1 %copy-start = (f32[68,16,128]{2,1,0:T(8,128)S(1)}, f32[68,16,128]{2,1,0:T(8,128)}, u32[]{:S(2)}) copy-start(f32[68,16,128]{2,1,0:T(8,128)} %get-tuple-element.20.own) | copy-start | bytes 1671172
  38.5 10.3 %collective-permute-start.2 = (f32[28,16,128]{2,1,0:T(8,128)S(1)}, f32[28,16,128]{2,1,0:T(8,128)S(1)}, u32[]{:S(2)}, u32[]{:S(2)}) collective-permute-start(f32[28,16,128]{2,1,0:T(8,128)S(1)} %get-tuple-element.28), channel_id=1, source_target_pairs={{0,504},{8,16},{16,8},{24,32},{32,24},{40,48},{48,40},{56,64},{64,... | collective-permute-start | bytes 688136 | tf_op jit(solution)/shard_map/ppermute | solution.py:519
  40.4 9.5 %collective-permute-start.3 = (f32[28,16,128]{2,1,0:T(8,128)S(1)}, f32[28,16,128]{2,1,0:T(8,128)S(1)}, u32[]{:S(2)}, u32[]{:S(2)}) collective-permute-start(f32[28,16,128]{2,1,0:T(8,128)S(1)} %get-tuple-element.29), channel_id=1, source_target_pairs={{0,8},{8,0},{16,24},{24,16},{32,40},{40,32},{48,56},{56,48},{64,72... | collective-permute-start | bytes 688136 | tf_op jit(solution)/shard_map/ppermute | solution.py:519

commit v3 on v2

--- a/solution.py
+++ b/solution.py
@@ -42,7 +42,7 @@
 FIELDS = MEMBERS + 6
 
 SLOTS = LANES // (2 * EDGE)
-STRIP_ROWS = 2 * FIELDS // SLOTS
+STRIP_ROWS = 4 * FIELDS // SLOTS
 HALF_ROWS = STRIP_ROWS // 2
 ADJ_ROWS = -(-MEMBERS // SLOTS)
 
@@ -228,10 +228,6 @@
     return turn(value, 2 * EDGE * slot + EDGE, 1)
 
 
-def unpack(row, slot):
-    return turn(row, -EDGE - 2 * EDGE * slot, 1)
-
-
 def pack_rows(values):
     lane = lax.broadcasted_iota(jnp.int32, (ZED, LANES), 1)
     rows = []
@@ -271,8 +267,8 @@
 
 def first_kernel(
     flow_in, heat_in, flow_weight_in, heat_weight_in, resistance_in, conductivity_in, solid_in,
-    own, far, near, strips,
-    right, left, flow, heat, flow_weight, heat_weight, resistance, conductivity, solid, arrived,
+    own, far, near,
+    both, flow, heat, flow_weight, heat_weight, resistance, conductivity, solid, arrived, sent,
 ):
     pairs = [
         (flow_in, flow),
@@ -286,7 +282,6 @@
     copies = [pltpu.make_async_copy(a, b, arrived.at[k]) for k, (a, b) in enumerate(pairs)]
     for copy in copies:
         copy.start()
-    strips[...] = jnp.zeros(strips.shape, jnp.float32)
     for copy in copies:
         copy.wait()
     for c in range(2):
@@ -298,21 +293,31 @@
             after = collide(f, g, mobility, rate)
             more = [mobility, rate] + [flow_weight[k, c, z, :] for k in range(3)] + [heat_weight[c, z, :]]
             for k, value in enumerate(after + more):
-                if (k, c) in TO_RIGHT:
-                    right[TO_RIGHT[k, c], z, :] = value
-                else:
-                    left[TO_LEFT[k, c], z, :] = value
-
-    for k in range(BULK_ROWS):
-        own[k] = right[k]
-        own[k + BULK_ROWS] = left[k]
-
-    def send(first):
-        copy_rows(far, left if first else right)
-        copy_rows(near, right if first else left)
-
-    either_way(send)
-    rows = pack_rows([right[k] for k in range(BULK_ROWS)] + [left[k] for k in range(BULK_ROWS)])
+                both[TO_RIGHT[k, c] if (k, c) in TO_RIGHT else BULK_ROWS + TO_LEFT[k, c], z, :] = value
+    odd = lax.rem(lax.axis_index("gx"), 2)
+    copies = [
+        pltpu.make_async_copy(both.at[pl.ds(BULK_ROWS * (1 - odd), BULK_ROWS)], far, sent.at[0]),
+        pltpu.make_async_copy(both.at[pl.ds(BULK_ROWS * odd, BULK_ROWS)], near, sent.at[1]),
+        pltpu.make_async_copy(both, own, sent.at[2]),
+    ]
+    for copy in copies:
+        copy.start()
+    for copy in copies:
+        copy.wait()
+
+
+def strip_kernel(own, from_far, from_near, strips, from_left, from_right):
+    def receive(first):
+        copy_rows(from_left, from_far if first else from_near)
+        copy_rows(from_right, from_near if first else from_far)
+
+    either_way(receive)
+    strips[...] = jnp.zeros(strips.shape, jnp.float32)
+    rows = pack_rows(
+        [own[k] for k in range(2 * BULK_ROWS)]
+        + [from_left[k] for k in range(BULK_ROWS)]
+        + [from_right[k] for k in range(BULK_ROWS)]
+    )
     low = low_lanes()
     below, above = ring_place("gy")
     for k in range(HALF_ROWS):
@@ -320,73 +325,71 @@
         strips[below, k] = jnp.where(low, turn(rows[k], -EDGE, 1), rows[k + HALF_ROWS])
 
 
-def merge_kernel(strips, own_in, far_in, near_in, own, far, near, strip, sent):
-    del own_in, far_in, near_in
+def split(value):
+    return value[:, :LANES], value[:, LANES:], 0
+
+
+def beside(row, slot):
+    return row, -EDGE - 2 * EDGE * slot
+
+
+def moved(pair, velocity, way):
+    main, extra, by = pair
+    _, step_y, step_z = velocity
+    step = way * step_y
+    main, extra = turn(main, way * step_z, 0), turn(extra, way * step_z, 0)
+    if not step:
+        return main, turn(extra, by, 1)
+    main, extra = turn(main, step, 1), turn(extra, by + step, 1)
+    lane = lax.broadcasted_iota(jnp.int32, (ZED, LANES), 1)
+    edge = lane == (0 if step == 1 else LANES - 1)
+    return jnp.where(edge, extra, main), jnp.where(edge, main, extra)
+
+
+def put(ref, q, i, pair):
+    ref[q, i, :, :LANES], ref[q, i, :, LANES:] = pair
+
+
+def tiles(lanes):
+    return [(z, pl.ds(t, LANES)) for z in halves() for t in range(0, lanes, LANES)]
+
+
+STILL = (0, 0, 0)
+
+
+def second_kernel(
+    own, from_left, from_right, strips,
+    state, wide_sides, adjoint, by_resistance, by_conductivity, far, near,
+    strip, after, later, seed, right, left,
+):
     low = low_lanes()
     below, above = ring_place("gy")
     for k in range(HALF_ROWS):
         under, over = strips[below, k], strips[above, k]
         strip[k] = jnp.where(low, under, turn(over, EDGE, 1))
         strip[k + HALF_ROWS] = jnp.where(low, turn(under, -EDGE, 1), over)
-    tail = pl.ds(BULK_ROWS, HALF_ROWS)
-    rightward = HALF_ROWS * lax.rem(lax.axis_index("gx"), 2)
-    copies = [
-        pltpu.make_async_copy(strip.at[pl.ds(HALF_ROWS - rightward, HALF_ROWS)], far.at[tail], sent.at[0]),
-        pltpu.make_async_copy(strip.at[pl.ds(rightward, HALF_ROWS)], near.at[tail], sent.at[1]),
-        pltpu.make_async_copy(strip, own.at[pl.ds(2 * BULK_ROWS, STRIP_ROWS)], sent.at[2]),
-    ]
-    for copy in copies:
-        copy.start()
-    for copy in copies:
-        copy.wait()
-
-
-def wide_field(k, column, own, from_left, from_right):
-    if column < 0:
-        place = TO_RIGHT[k, column + 2]
-        main, strips, start = from_left[place], from_left, BULK_ROWS
-    elif column > 1:
-        place = TO_LEFT[k, column - 2]
-        main, strips, start = from_right[place], from_right, BULK_ROWS
-    elif (k, column) in TO_RIGHT:
-        place = TO_RIGHT[k, column]
-        main, strips, start = own[place], own, 2 * BULK_ROWS
-    else:
-        place = TO_LEFT[k, column]
-        main, strips, start = own[BULK_ROWS + place], own, 2 * BULK_ROWS + HALF_ROWS
-    beside = unpack(strips[start + place // SLOTS], place % SLOTS)
-    return jnp.concatenate([main, beside], axis=1)
-
-
-def moved(value, velocity, way):
-    _, step_y, step_z = velocity
-    return turn(turn(value, way * step_z, 0), way * step_y, 1)
-
-
-def tiles(lanes):
-    return [(z, pl.ds(t, LANES)) for z in halves() for t in range(0, lanes, LANES)]
-
-
-def second_kernel(
-    own, from_far, from_near,
-    state, wide_sides, adjoint, by_resistance, by_conductivity, far, near,
-    from_left, from_right, after, later, seed, right, left,
-):
-    def receive(first):
-        copy_rows(from_left, from_far if first else from_near)
-        copy_rows(from_right, from_near if first else from_far)
-
-    either_way(receive)
 
     def wide(k, column):
-        return wide_field(k, column, own, from_left, from_right)
+        if column < 0:
+            place = TO_RIGHT[k, column + 2]
+            main, start = from_left[place], 2 * BULK_ROWS
+        elif column > 1:
+            place = TO_LEFT[k, column - 2]
+            main, start = from_right[place], 3 * BULK_ROWS
+        elif (k, column) in TO_RIGHT:
+            place, start = TO_RIGHT[k, column], 0
+            main = own[place]
+        else:
+            place, start = TO_LEFT[k, column], BULK_ROWS
+            main = own[BULK_ROWS + place]
+        return (main,) + beside(strip[(start + place) // SLOTS], place % SLOTS)
 
     for column in range(-1, 3):
         i = column + 1
-        wide_sides[0, i] = wide(MOBILITY, column)
-        wide_sides[1, i] = wide(RATE, column)
+        put(wide_sides, 0, i, moved(wide(MOBILITY, column), STILL, 1))
+        put(wide_sides, 1, i, moved(wide(RATE, column), STILL, 1))
         for q in range(MEMBERS):
-            state[q, i] = moved(wide(q, column - VELOCITY[q][0]), VELOCITY[q], 1)
+            put(state, q, i, moved(wide(q, column - VELOCITY[q][0]), VELOCITY[q], 1))
     for i in range(4):
         for z, y in tiles(WIDE):
             f = [state[q, i, z, y] for q in range(19)]
@@ -397,20 +400,24 @@
                     after[q, i, z, y] = result[q]
     for c in range(2):
         for q in range(MEMBERS):
-            later[q, c] = moved(after[q, c + 1 - VELOCITY[q][0]], VELOCITY[q], 1)
+            put(later, q, c, moved(split(after[q, c + 1 - VELOCITY[q][0]]), VELOCITY[q], 1))
     for column in range(-1, 3):
-        weights = [wide(WEIGHT + k, column) for k in range(4)]
+        weights = [wide(WEIGHT + k, column) for k in range(3)]
+        weights = [(main, turn(extra, by, 1)) for main, extra, by in weights]
         for q in range(1, MEMBERS):
             velocity = VELOCITY[q]
             c = column - velocity[0]
             if not 0 <= c <= 1:
                 continue
             if q < 19:
-                parts = [weights[k] if velocity[k] > 0 else -weights[k] for k in range(3) if velocity[k]]
-                value = parts[0] if len(parts) == 1 else parts[0] + parts[1]
+                parts = [
+                    tuple(value if velocity[k] > 0 else -value for value in weights[k]) for k in range(3) if velocity[k]
+                ]
+                pair = parts[0] if len(parts) == 1 else tuple(a + b for a, b in zip(*parts))
+                pair += (0,)
             else:
-                value = weights[3]
-            seed[q, c] = moved(value, velocity, -1)
+                pair = wide(WEIGHT + 3, column)
+            put(seed, q, c, moved(pair, velocity, -1))
     for c in range(2):
         for z, y in tiles(WIDE):
             f = [later[q, c, z, y] for q in range(19)]
@@ -454,15 +461,16 @@
 
     def wide(q, column):
         if 0 <= column <= 1:
-            return adjoint[q, column]
-        c, bulk, rows = (column + 2, from_left, ADJ_TO_RIGHT) if column < 0 else (column - 2, from_right, ADJ_TO_LEFT)
-        place = rows[q, c]
-        beside = unpack(bulk[ADJ_BULK + place // SLOTS], place % SLOTS)
-        return jnp.concatenate([bulk[place], beside], axis=1)
+            return split(adjoint[q, column])
+        if column < 0:
+            bulk, place = from_left, ADJ_TO_RIGHT[q, column + 2]
+        else:
+            bulk, place = from_right, ADJ_TO_LEFT[q, column - 2]
+        return (bulk[place],) + beside(bulk[ADJ_BULK + place // SLOTS], place % SLOTS)
 
     for column in range(-1, 3):
         for q in range(MEMBERS):
-            arrived[q, column + 1] = moved(wide(q, column + VELOCITY[q][0]), VELOCITY[q], -1)
+            put(arrived, q, column + 1, moved(wide(q, column + VELOCITY[q][0]), VELOCITY[q], -1))
     for column in range(-1, 3):
         i = column + 1
         for z, y in tiles(WIDE):
@@ -488,8 +496,11 @@
     for c in range(2):
         for q in range(MEMBERS):
             velocity = VELOCITY[q]
-            source = earlier[q, c + 1 + velocity[0]] if velocity[1] else earlier[q, c + 1 + velocity[0], :, :LANES]
-            last[q, c] = moved(source, velocity, -1)[:, :LANES]
+            i = c + 1 + velocity[0]
+            if velocity[1]:
+                last[q, c] = moved(split(earlier[q, i]), velocity, -1)[0]
+            else:
+                last[q, c] = turn(earlier[q, i, :, :LANES], -velocity[2], 0)
     for c in range(2):
         for z in halves():
             f = [flow[q, c, z, :] for q in range(19)]
@@ -521,25 +532,23 @@
 
 FIRST_PARAMS = pltpu.CompilerParams(vmem_limit_bytes=56 * 1024 * 1024)
 PARAMS = pltpu.CompilerParams(vmem_limit_bytes=24 * 1024 * 1024)
-SENT = BULK_ROWS + HALF_ROWS
-OWN_ROWS = 2 * BULK_ROWS + STRIP_ROWS
 ADJ_SENT = ADJ_BULK + ADJ_ROWS
 
 
 def on_device(flow, heat, flow_weight, heat_weight, resistance, conductivity, solid):
     rings = lax.axis_size("gy")
-    own, far, near, strips = pl.pallas_call(
+    in_hbm = pl.BlockSpec(memory_space=pltpu.HBM)
+    own, far, near = pl.pallas_call(
         first_kernel,
-        in_specs=[pl.BlockSpec(memory_space=pltpu.HBM)] * 7,
+        in_specs=[in_hbm] * 7,
+        out_specs=[in_hbm] * 3,
         out_shape=(
-            floats(OWN_ROWS, ZED, LANES),
-            floats(SENT, ZED, LANES),
-            floats(SENT, ZED, LANES),
-            floats(rings, HALF_ROWS, ZED, LANES),
+            floats(2 * BULK_ROWS, ZED, LANES),
+            floats(BULK_ROWS, ZED, LANES),
+            floats(BULK_ROWS, ZED, LANES),
         ),
         scratch_shapes=[
-            vmem(BULK_ROWS, ZED, LANES),
-            vmem(BULK_ROWS, ZED, LANES),
+            vmem(2 * BULK_ROWS, ZED, LANES),
             vmem(19, 2, ZED, LANES),
             vmem(7, 2, ZED, LANES),
             vmem(3, 2, ZED, LANES),
@@ -548,26 +557,26 @@
             vmem(2, ZED, LANES),
             pltpu.VMEM((2, ZED, LANES), jnp.int32),
             pltpu.SemaphoreType.DMA((7,)),
+            pltpu.SemaphoreType.DMA((3,)),
         ],
         compiler_params=FIRST_PARAMS,
         name="collide_own",
     )(flow, heat, flow_weight, heat_weight, resistance, conductivity, solid)
 
+    from_far, from_near = swap_along_x(far, near)
+
+    strips, from_left, from_right = pl.pallas_call(
+        strip_kernel,
+        out_shape=(
+            floats(rings, HALF_ROWS, ZED, LANES),
+            floats(BULK_ROWS, ZED, LANES),
+            floats(BULK_ROWS, ZED, LANES),
+        ),
+        compiler_params=PARAMS,
+        name="pack_strips",
+    )(own, from_far, from_near)
+
     strips = lax.all_to_all(strips, "gy", 0, 0)
-
-    in_place = pl.BlockSpec(memory_space=pltpu.HBM)
-    own, far, near = pl.pallas_call(
-        merge_kernel,
-        in_specs=[pl.BlockSpec(memory_space=pltpu.VMEM), in_place, in_place, in_place],
-        out_specs=[in_place, in_place, in_place],
-        out_shape=(floats(OWN_ROWS, ZED, LANES), floats(SENT, ZED, LANES), floats(SENT, ZED, LANES)),
-        scratch_shapes=[vmem(STRIP_ROWS, ZED, LANES), pltpu.SemaphoreType.DMA((3,))],
-        input_output_aliases={1: 0, 2: 1, 3: 2},
-        compiler_params=FIRST_PARAMS,
-        name="merge_strips",
-    )(strips, own, far, near)
-
-    from_far, from_near = swap_along_x(far, near)
 
     state, wide_sides, adjoint, part_resistance, part_conductivity, far, near = pl.pallas_call(
         second_kernel,
@@ -581,8 +590,7 @@
             floats(ADJ_SENT, ZED, LANES),
         ),
         scratch_shapes=[
-            vmem(SENT, ZED, LANES),
-            vmem(SENT, ZED, LANES),
+            vmem(STRIP_ROWS, ZED, LANES),
             vmem(MEMBERS, 4, ZED, WIDE),
             vmem(MEMBERS, 2, ZED, WIDE),
             vmem(MEMBERS, 2, ZED, WIDE),
@@ -591,7 +599,7 @@
         ],
         compiler_params=PARAMS,
         name="forward_and_seed",
-    )(own, from_far, from_near)
+    )(own, from_left, from_right, strips)
 
     from_far, from_near = swap_along_x(far, near)
 

time: 52.3 us -> 48.1 us (0.920)
  Pallas kernels: 10.1 us -> 5.92 us
  starting transfers between devices: 25.9 us -> 27.4 us
  blocking collectives: 11.6 us -> 10.2 us
    pallas_call x1, Pallas kernels: 4.15 us -> 1.65 us  [on_device(): pl.pallas_call(second_kernel, out_shape=(floats(MEMBERS, 4, ZED, WIDE), f...]
    ppermute x4, starting transfers between devices: 25.9 us -> 27.4 us  [swap_along_x(): return (lax.ppermute(far, 'gx', across), lax.ppermute(near, 'gx', within))]
    all_to_all x1, blocking collectives: 11.6 us -> 10.2 us  [on_device(): strips = lax.all_to_all(strips, 'gy', 0, 0)]
    pallas_call x2, Pallas kernels: 4 us -> 2.74 us  [the longest x1 2.3 us: on_device(): pl.pallas_call(first_kernel, in_specs=[in_hbm] * 7, out_specs=[in_hbm] *...]
where the time goes in v3:
time: 48.1 us; the launch traced here: 47.7 us
  starting transfers between devices  27.4 us (57%)
  blocking collectives  10.2 us (21%)
  Pallas kernels  5.92 us (12%)
  waiting for transfers between devices  2.43 us (5%)
  local copies, waits for them, and re-layouts  1.05 us (2%)
  between operations  0.72 us (1%)
    ppermute x4, starting transfers between devices, swap_along_x(): return (lax.ppermute(far, 'gx', across), lax.ppermute(near, 'gx', within))  27.4 us
    all_to_all x1, blocking collectives, on_device(): strips = lax.all_to_all(strips, 'gy', 0, 0)  10.2 us
    ppermute x4, waiting for transfers between devices, swap_along_x(): return (lax.ppermute(far, 'gx', across), lax.ppermute(near, 'gx', within))  2.43 us
    pallas_call x1, Pallas kernels, on_device(): pl.pallas_call(first_kernel, in_specs=[in_hbm] * 7, out_specs=[in_hbm] *...  2.3 us
    pallas_call x1, Pallas kernels, on_device(): pl.pallas_call(second_kernel, out_shape=(floats(MEMBERS, 4, ZED, WIDE), f...  1.65 us
    pallas_call x1, Pallas kernels, on_device(): pl.pallas_call(third_kernel, out_shape=(floats(2, ZED, LANES), floats(2,...  1.53 us
    unnamed x6, local copies, waits for them, and re-layouts  1.05 us
  transfers between devices with their start and end apart: 4, of which 2 were waited for; matrix products, arithmetic and copies ran while one was open for 0% of the time, Pallas kernels for 0%

profile of v3, /device:TPU:1, one launch (start us, length us, event | category | flops | bytes accessed | tf_op | source)
XLA Modules:
  0.0 47.7 jit_solution(3691971595012660791)
XLA Ops:
  0.6 0.0 copy-start.2
  0.6 0.0 copy-start.1
  0.7 2.3 %collide_own.1 = (f32[64,16,128]{2,1,0:T(8,128)}, f32[32,16,128]{2,1,0:T(8,128)}, f32[32,16,128]{2,1,0:T(8,128)}) custom-call(f32[19,2,16,128]{3,2,1,0:T(8,128)} %flow.1, f32[7,2,16,128]{3,2,1,0:T(8,128)} %heat.1, f32[3,2,16,128]{3,2,1,0:T(8,128)} %flow_weight_in.1, f32[2,16,128]{2,1,0:T(8,128)} %heat_weight_in.1, f32[2,16,128]{2,1,0:T(8,128)} %resistance_in.1, ...), custom_call_target="tpu_custom_call" | custom-call | tf_op jit(solution)/shard_map/collide_own/pallas_call | solution.py:541
  3.0 4.9 %collective-permute-start = (f32[32,16,128]{2,1,0:T(8,128)}, f32[32,16,128]{2,1,0:T(8,128)S(1)}, u32[]{:S(2)}, u32[]{:S(2)}) collective-permute-start(f32[32,16,128]{2,1,0:T(8,128)} %get-tuple-element.16), channel_id=1, source_target_pairs={{0,504},{8,16},{16,8},{24,32},{32,24},{40,48},{48,40},{56,64},{64,... | collective-permute-start | bytes 786440 | tf_op jit(solution)/shard_map/ppermute | solution.py:530
  7.9 11.8 %collective-permute-start.1 = (f32[32,16,128]{2,1,0:T(8,128)}, f32[32,16,128]{2,1,0:T(8,128)S(1)}, u32[]{:S(2)}, u32[]{:S(2)}) collective-permute-start(f32[32,16,128]{2,1,0:T(8,128)} %get-tuple-element.17), channel_id=1, source_target_pairs={{0,8},{8,0},{16,24},{24,16},{32,40},{40,32},{48,56},{56,48},{64,72... | collective-permute-start | bytes 786440 | tf_op jit(solution)/shard_map/ppermute | solution.py:530
  19.7 0.0 collective-permute-done.from_far
  19.7 1.3 %collective-permute-done.1.from_near = f32[32,16,128]{2,1,0:T(8,128)S(1)} collective-permute-done((f32[32,16,128]{2,1,0:T(8,128)}, f32[32,16,128]{2,1,0:T(8,128)S(1)}, u32[]{:S(2)}, u32[]{:S(2)}) %collective-permute-start.1) | collective-permute-done | bytes 262176 | tf_op jit(solution)/shard_map/ppermute | solution.py:530
  21.0 0.0 copy-start
  21.0 1.0 %copy-done = f32[64,16,128]{2,1,0:T(8,128)S(1)} copy-done((f32[64,16,128]{2,1,0:T(8,128)S(1)}, f32[64,16,128]{2,1,0:T(8,128)}, u32[]{:S(2)}) %copy-start) | copy-done | bytes 524312
  22.1 0.4 pack_strips.1
  22.5 10.2 %all_to_all.5.strips = f32[8,4,16,128]{3,2,1,0:T(8,128)S(1)} all-to-all(f32[8,4,16,128]{3,2,1,0:T(8,128)S(1)} %get-tuple-element.20), channel_id=1, replica_groups=mesh['gx'=64,'gy'=8] {'gy'}, dimensions={0} | all-to-all | bytes 524288 | tf_op jit(solution)/shard_map/all_to_all | solution.py:579
  32.7 1.6 %forward_and_seed.1 = (f32[26,4,16,256]{3,2,1,0:T(8,128)S(1)}, f32[2,4,16,256]{3,2,1,0:T(8,128)S(1)}, f32[26,2,16,256]{3,2,1,0:T(8,128)S(1)}, f32[2,16,128]{2,1,...) custom-call(f32[64,16,128]{2,1,0:T(8,128)S(1)} %copy-done, ...), custom_call_target="tpu_custom_call" | custom-call | tf_op jit(solution)/shard_map/forward_and_seed/pallas_call | solution.py:581
  34.4 1.9 %collective-permute-start.2 = (f32[28,16,128]{2,1,0:T(8,128)S(1)}, f32[28,16,128]{2,1,0:T(8,128)S(1)}, u32[]{:S(2)}, u32[]{:S(2)}) collective-permute-start(f32[28,16,128]{2,1,0:T(8,128)S(1)} %get-tuple-element.26), channel_id=1, source_target_pairs={{0,504},{8,16},{16,8},{24,32},{32,24},{40,48},{48,40},{56,64},{64,... | collective-permute-start | bytes 688136 | tf_op jit(solution)/shard_map/ppermute | solution.py:530
  36.3 8.8 %collective-permute-start.3 = (f32[28,16,128]{2,1,0:T(8,128)S(1)}, f32[28,16,128]{2,1,0:T(8,128)S(1)}, u32[]{:S(2)}, u32[]{:S(2)}) collective-permute-start(f32[28,16,128]{2,1,0:T(8,128)S(1)} %get-tuple-element.27), channel_id=1, source_target_pairs={{0,8},{8,0},{16,24},{24,16},{32,40},{40,32},{48,56},{56,48},{64,72... | collective-permute-start | bytes 688136 | tf_op jit(solution)/shard_map/ppermute | solution.py:530
  45.1 0.0 collective-permute-done.2.from_far
  45.1 1.1 %collective-permute-done.3.from_near = f32[28,16,128]{2,1,0:T(8,128)S(1)} collective-permute-done((f32[28,16,128]{2,1,0:T(8,128)S(1)}, f32[28,16,128]{2,1,0:T(8,128)S(1)}, u32[]{:S(2)}, u32[]{:S(2)}) %collective-permute-start.3) | collective-permute-done | bytes 229408 | tf_op jit(solution)/shard_map/ppermute | solution.py:530
  46.2 0.0 copy-done.2
  46.2 0.0 copy-done.1
  46.2 1.5 %adjoint_steps.1 = (f32[2,16,128]{2,1,0:T(8,128)}, f32[2,16,128]{2,1,0:T(8,128)}) custom-call(f32[19,2,16,128]{3,2,1,0:T(8,128)S(1)} %copy-done.1, f32[7,2,16,128]{3,2,1,0:T(8,128)S(1)} %copy-done.2, f32[26,4,16,256]{3,2,1,0:T(8,128)S(1)} %get-tuple-element.21.state, f32[2,4,16,256]{3,2,1,0:T(8,128)S(1)} %get-tuple-element.22.wide_sides, ...), custom_call_target="tpu_custom_call" | custom-call | tf_op jit(solution)/shard_map/adjoint_steps/pallas_call | solution.py:606
Async XLA Ops:
  0.6 45.6 %copy-start.2 = (f32[7,2,16,128]{3,2,1,0:T(8,128)S(1)}, f32[7,2,16,128]{3,2,1,0:T(8,128)}, u32[]{:S(2)}) copy-start(f32[7,2,16,128]{3,2,1,0:T(8,128)} %heat.1) | copy-start | bytes 344068
  0.6 45.6 %copy-start.1 = (f32[19,2,16,128]{3,2,1,0:T(8,128)S(1)}, f32[19,2,16,128]{3,2,1,0:T(8,128)}, u32[]{:S(2)}) copy-start(f32[19,2,16,128]{3,2,1,0:T(8,128)} %flow.1) | copy-start | bytes 933892
  3.0 16.7 %collective-permute-start = (f32[32,16,128]{2,1,0:T(8,128)}, f32[32,16,128]{2,1,0:T(8,128)S(1)}, u32[]{:S(2)}, u32[]{:S(2)}) collective-permute-start(f32[32,16,128]{2,1,0:T(8,128)} %get-tuple-element.16), channel_id=1, source_target_pairs={{0,504},{8,16},{16,8},{24,32},{32,24},{40,48},{48,40},{56,64},{64,... | collective-permute-start | bytes 786440 | tf_op jit(solution)/shard_map/ppermute | solution.py:530
  7.9 13.1 %collective-permute-start.1 = (f32[32,16,128]{2,1,0:T(8,128)}, f32[32,16,128]{2,1,0:T(8,128)S(1)}, u32[]{:S(2)}, u32[]{:S(2)}) collective-permute-start(f32[32,16,128]{2,1,0:T(8,128)} %get-tuple-element.17), channel_id=1, source_target_pairs={{0,8},{8,0},{16,24},{24,16},{32,40},{40,32},{48,56},{56,48},{64,72... | collective-permute-start | bytes 786440 | tf_op jit(solution)/shard_map/ppermute | solution.py:530
  21.0 1.0 %copy-start = (f32[64,16,128]{2,1,0:T(8,128)S(1)}, f32[64,16,128]{2,1,0:T(8,128)}, u32[]{:S(2)}) copy-start(f32[64,16,128]{2,1,0:T(8,128)} %get-tuple-element.15.own) | copy-start | bytes 1572868
  34.4 10.7 %collective-permute-start.2 = (f32[28,16,128]{2,1,0:T(8,128)S(1)}, f32[28,16,128]{2,1,0:T(8,128)S(1)}, u32[]{:S(2)}, u32[]{:S(2)}) collective-permute-start(f32[28,16,128]{2,1,0:T(8,128)S(1)} %get-tuple-element.26), channel_id=1, source_target_pairs={{0,504},{8,16},{16,8},{24,32},{32,24},{40,48},{48,40},{56,64},{64,... | collective-permute-start | bytes 688136 | tf_op jit(solution)/shard_map/ppermute | solution.py:530
  36.3 9.9 %collective-permute-start.3 = (f32[28,16,128]{2,1,0:T(8,128)S(1)}, f32[28,16,128]{2,1,0:T(8,128)S(1)}, u32[]{:S(2)}, u32[]{:S(2)}) collective-permute-start(f32[28,16,128]{2,1,0:T(8,128)S(1)} %get-tuple-element.27), channel_id=1, source_target_pairs={{0,8},{8,0},{16,24},{24,16},{32,40},{40,32},{48,56},{56,48},{64,72... | collective-permute-start | bytes 688136 | tf_op jit(solution)/shard_map/ppermute | solution.py:530

commit v4 on v2

v4 whole, which is shorter than its diff:
```python
import jax
import jax.numpy as jnp
from jax import lax
from jax.experimental import pallas as pl
from jax.experimental.pallas import tpu as pltpu
from jax.sharding import PartitionSpec as P

ZED = 16
LANES = 128
WIDE = 2 * LANES
EDGE = 4

FLOW_VELOCITY = [
    (0, 0, 0),
    (1, 0, 0),
    (-1, 0, 0),
    (0, 1, 0),
    (0, -1, 0),
    (0, 0, 1),
    (0, 0, -1),
    (1, 1, 0),
    (-1, -1, 0),
    (1, -1, 0),
    (-1, 1, 0),
    (1, 0, 1),
    (-1, 0, -1),
    (1, 0, -1),
    (-1, 0, 1),
    (0, 1, 1),
    (0, -1, -1),
    (0, 1, -1),
    (0, -1, 1),
]
VELOCITY = FLOW_VELOCITY + FLOW_VELOCITY[:7]
STILL = (0, 0, 0)
MEMBERS = len(VELOCITY)
RIGHTWARD = [q for q in range(MEMBERS) if VELOCITY[q][0] == 1]
LEFTWARD = [q for q in range(MEMBERS) if VELOCITY[q][0] == -1]
LEVEL = [q for q in range(MEMBERS) if VELOCITY[q][0] == 0]

MOBILITY, RATE, WEIGHT = MEMBERS, MEMBERS + 1, MEMBERS + 2
FIELDS = MEMBERS + 6
SIDE_FIELDS = list(range(MEMBERS, FIELDS))

SUMS = 9
SUM_FIELDS = [FIELDS + k for k in range(SUMS)]

SLOTS = LANES // (2 * EDGE)
STRIP_ROWS = 2 * FIELDS // SLOTS
HALF_ROWS = STRIP_ROWS // 2


def rows_of(entries):
    return {entry: row for row, entry in enumerate(entries)}


TO_RIGHT = rows_of([(q, 0) for q in RIGHTWARD] + [(k, 1) for k in RIGHTWARD + SIDE_FIELDS + SUM_FIELDS])
TO_LEFT = rows_of([(q, 1) for q in LEFTWARD] + [(k, 0) for k in LEFTWARD + SIDE_FIELDS + SUM_FIELDS])
ADJ_TO_RIGHT = rows_of([(q, 0) for q in LEFTWARD] + [(k, 1) for k in LEFTWARD + SUM_FIELDS])
ADJ_TO_LEFT = rows_of([(q, 1) for q in RIGHTWARD] + [(k, 0) for k in RIGHTWARD + SUM_FIELDS])
BULK_ROWS, ADJ_BULK = len(TO_RIGHT), len(ADJ_TO_RIGHT)


def with_strips(bulk):
    return bulk + -(-bulk // SLOTS)


SENT, ADJ_SENT = with_strips(BULK_ROWS), with_strips(ADJ_BULK)


def level_sums(p):
    s1, s2, d1, d2 = p[3] + p[4], p[5] + p[6], p[3] - p[4], p[5] - p[6]
    s7, s8, d7, d8 = p[15] + p[16], p[17] + p[18], p[15] - p[16], p[17] - p[18]
    yz = s7 + s8
    mass = p[0] + (s1 + s2) + yz
    return [
        mass, d1 + (d7 + d8), d2 + (d7 - d8), s1 + yz, s2 + yz, s7 - s8,
        p[19] + (p[22] + p[23]) + (p[24] + p[25]), p[22] - p[23], p[24] - p[25],
    ]


def level_adjoint_sums(p):
    s1, s2, d1, d2 = p[3] + p[4], p[5] + p[6], p[3] - p[4], p[5] - p[6]
    s7, s8, d7, d8 = p[15] + p[16], p[17] + p[18], p[15] - p[16], p[17] - p[18]
    yz = s7 + s8
    t1, t2 = s1 + s1, s2 + s2
    mass = 12.0 * p[0] + (t1 + t2) + yz
    return [
        mass, (d1 + d1) + (d7 + d8), (d2 + d2) + (d7 - d8), t1 + yz, t2 + yz, s7 - s8,
        0.35 * p[19] + 0.175 * ((p[22] + p[23]) + (p[24] + p[25])),
        0.125 * (p[22] - p[23]), 0.125 * (p[24] - p[25]),
    ]


def cross_sums(p):
    pairs = [(1, 2), (7, 8), (9, 10), (11, 12), (13, 14)]
    return [p[a] + p[b] for a, b in pairs], [p[a] - p[b] for a, b in pairs]


def common(p, level, mobility):
    s, d = cross_sums(p)
    xy, xz = s[1] + s[2], s[3] + s[4]
    along = s[0] + xy + xz
    rho = level[0] + along
    j = (d[0] + (d[1] + d[2]) + (d[3] + d[4]), level[1] + (d[1] - d[2]), level[2] + (d[3] - d[4]))
    temperature = level[6] + (p[20] + p[21])
    flux = (p[20] - p[21], level[7], level[8])
    u = tuple(mobility * jk for jk in j)
    square = (u[0] * u[0], u[1] * u[1], u[2] * u[2])
    third = rho * (1.0 / 3.0)
    stress = (
        along - third - square[0],
        (level[3] + xy) - third - square[1],
        (level[4] + xz) - third - square[2],
        (s[1] - s[2]) - u[0] * u[1],
        (s[3] - s[4]) - u[0] * u[2],
        level[5] - u[1] * u[2],
    )
    decay = jnp.exp(-2.0 * (temperature - 1.0))
    omega = 1.0 / (0.5 + 0.3 * decay)
    return rho, j, u, square, stress, temperature, flux, decay, omega


def collide(p, level, mobility, rate, wanted):
    rho, _, u, square, stress, temperature, flux, _, omega = common(p, level, mobility)
    solid = mobility == 0.0
    lam = 1.2 - omega
    trace = stress[0] + stress[1] + stress[2]
    base = 1.2 * rho - 1.8 * (square[0] + square[1] + square[2]) - (1.5 * lam) * trace
    scale = 4.5 * lam
    mxx = 5.4 * square[0] + scale * stress[0]
    myy = 5.4 * square[1] + scale * stress[1]
    mzz = 5.4 * square[2] + scale * stress[2]
    mxy = 2.0 * (5.4 * (u[0] * u[1]) + scale * stress[3])
    mxz = 2.0 * (5.4 * (u[0] * u[2]) + scale * stress[4])
    myz = 2.0 * (5.4 * (u[1] * u[2]) + scale * stress[5])
    bx, by, bz = base + mxx, base + myy, base + mzz
    sxy, sxz, syz = bx + myy, bx + mzz, by + mzz
    even = [bx, by, bz, sxy + mxy, sxy - mxy, sxz + mxz, sxz - mxz, syz + myz, syz - myz]
    odd = [u[0], u[1], u[2], u[0] + u[1], u[0] - u[1], u[0] + u[2], u[0] - u[2], u[1] + u[2], u[1] - u[2]]
    result = {}
    if 0 in wanted:
        result[0] = jnp.where(solid, p[0], (1.0 / 3.0) * base - 0.2 * p[0])
    for k in range(9):
        a, b = 2 * k + 1, 2 * k + 2
        w = 1.0 / 18.0 if k < 3 else 1.0 / 36.0
        e, o = w * even[k], (3.6 * w) * odd[k]
        if a in wanted:
            result[a] = jnp.where(solid, p[b], (e + o) - 0.2 * p[a])
        if b in wanted:
            result[b] = jnp.where(solid, p[a], (e - o) - 0.2 * p[b])
    keep = 0.5 * (1.4 - rate)
    push = (0.5 * rate) * temperature
    warm = 0.175 * temperature
    if 19 in wanted:
        result[19] = 0.35 * temperature - 0.4 * p[19]
    for k in range(3):
        along = keep * flux[k] + push * u[k]
        a, b = 20 + 2 * k, 21 + 2 * k
        if a in wanted:
            result[a] = (warm + along) - 0.4 * p[a]
        if b in wanted:
            result[b] = (warm - along) - 0.4 * p[b]
    return result


def pull_back(p, level, pa, adjoint_level, mobility, rate, wanted, sensitivity):
    rho, j, u, square, stress, temperature, flux, decay, omega = common(p, level, mobility)
    solid = mobility == 0.0
    lam = 1.2 - omega
    s, d = cross_sums(pa)
    w = 1.0 / 36.0
    xy, xz = s[1] + s[2], s[3] + s[4]
    along = (s[0] + s[0]) + xy + xz
    mass = w * (adjoint_level[0] + along)
    px = w * ((d[0] + d[0]) + (d[1] + d[2]) + (d[3] + d[4]))
    py = w * (adjoint_level[1] + (d[1] - d[2]))
    pz = w * (adjoint_level[2] + (d[3] - d[4]))
    rxx, ryy, rzz = w * along, w * (adjoint_level[3] + xy), w * (adjoint_level[4] + xz)
    rxy, rxz, ryz = w * (s[1] - s[2]), w * (s[3] - s[4]), w * adjoint_level[5]
    shift = 1.5 * mass
    dxx, dyy, dzz = 4.5 * rxx - shift, 4.5 * ryy - shift, 4.5 * rzz - shift
    dxy, dxz, dyz = 4.5 * rxy, 4.5 * rxz, 4.5 * ryz
    mix = 2.4 - 2.0 * lam
    b = ((pa[20] - pa[21]) * 0.125, adjoint_level[7], adjoint_level[8])
    push = (4.0 * rate) * temperature
    ux = 3.6 * px + mix * (dxx * u[0] + dxy * u[1] + dxz * u[2]) + push * b[0]
    uy = 3.6 * py + mix * (dxy * u[0] + dyy * u[1] + dyz * u[2]) + push * b[1]
    uz = 3.6 * pz + mix * (dxz * u[0] + dyz * u[1] + dzz * u[2]) + push * b[2]
    result = {}
    if wanted:
        lam_bar = (
            dxx * stress[0]
            + dyy * stress[1]
            + dzz * stress[2]
            + 2.0 * (dxy * stress[3] + dxz * stress[4] + dyz * stress[5])
        )
        rho_bar = 1.2 * mass - (1.5 * lam) * ((rxx + ryy + rzz) - mass)
        jx, jy, jz = mobility * ux, mobility * uy, mobility * uz
        ex, ey, ez = lam * dxx, lam * dyy, lam * dzz
        exy, exz, eyz = (2.0 * lam) * dxy, (2.0 * lam) * dxz, (2.0 * lam) * dyz
        hx, hy, hz = rho_bar + ex, rho_bar + ey, rho_bar + ez
        gxy, gxz, gyz = hx + ey, hx + ez, hy + ez
        even = [hx, hy, hz, gxy + exy, gxy - exy, gxz + exz, gxz - exz, gyz + eyz, gyz - eyz]
        odd = [jx, jy, jz, jx + jy, jx - jy, jx + jz, jx - jz, jy + jz, jy - jz]
        if 0 in wanted:
            result[0] = jnp.where(solid, pa[0], rho_bar - 0.2 * pa[0])
        for k in range(9):
            a, m = 2 * k + 1, 2 * k + 2
            if a in wanted:
                result[a] = jnp.where(solid, pa[m], (even[k] + odd[k]) - 0.2 * pa[a])
            if m in wanted:
                result[m] = jnp.where(solid, pa[a], (even[k] - odd[k]) - 0.2 * pa[m])
        warm = (
            adjoint_level[6]
            + 0.175 * (pa[20] + pa[21])
            + (4.0 * rate) * (b[0] * u[0] + b[1] * u[1] + b[2] * u[2])
            - jnp.where(solid, 0.0, lam_bar * (0.6 * decay) * (omega * omega))
        )
        keep = 5.6 - 4.0 * rate
        if 19 in wanted:
            result[19] = warm - 0.4 * pa[19]
        for k in range(3):
            along = keep * b[k]
            a, m = 20 + 2 * k, 21 + 2 * k
            if a in wanted:
                result[a] = (warm + along) - 0.4 * pa[a]
            if m in wanted:
                result[m] = (warm - along) - 0.4 * pa[m]
    if sensitivity:
        by_resistance = -(mobility * mobility) * (ux * j[0] + uy * j[1] + uz * j[2])
        bent = (
            b[0] * (temperature * u[0] - flux[0])
            + b[1] * (temperature * u[1] - flux[1])
            + b[2] * (temperature * u[2] - flux[2])
        )
        by_conductivity = (-1.6 * (rate * rate)) * bent
        result["by"] = (by_resistance, by_conductivity)
    return result


def turn(value, by, axis):
    count = value.shape[axis]
    by %= count
    return pltpu.roll(value, by, axis) if by else value


def side_by_side(parts):
    lane = lax.broadcasted_iota(jnp.int32, (ZED, LANES), 1)
    row = None
    for slot, part in enumerate(parts):
        row = part if row is None else jnp.where(lane >= 2 * EDGE * slot, part, row)
    return row


def packed(value, slot):
    return turn(value, 2 * EDGE * slot + EDGE, 1)


def pack_rows(parts):
    return [
        side_by_side([part(slot) for slot, part in enumerate(parts[start : start + SLOTS])])
        for start in range(0, len(parts), SLOTS)
    ]


def halves():
    return [pl.ds(0, 8), pl.ds(8, 8)]


def low_lanes():
    return lax.broadcasted_iota(jnp.int32, (ZED, LANES), 1) % (2 * EDGE) < EDGE


def ring_place(axis):
    count = lax.axis_size(axis)
    place = lax.axis_index(axis)
    return lax.rem(place + count - 1, count), lax.rem(place + 1, count)


def either_way(move):
    first = lax.rem(lax.axis_index("gx"), 2) == 0
    pl.when(first)(lambda: move(True))
    pl.when(jnp.logical_not(first))(lambda: move(False))


def copy_rows(target, source):
    for row in range(source.shape[0]):
        target[row] = source[row]


def split(value):
    return value[:, :LANES], value[:, LANES:], 0


def beside(row, slot):
    return row, -EDGE - 2 * EDGE * slot


def moved(triple, velocity, way):
    main, extra, by = triple
    _, step_y, step_z = velocity
    step = way * step_y
    main, extra = turn(main, way * step_z, 0), turn(extra, way * step_z, 0)
    if not step:
        return main, turn(extra, by, 1)
    main, extra = turn(main, step, 1), turn(extra, by + step, 1)
    lane = lax.broadcasted_iota(jnp.int32, (ZED, LANES), 1)
    edge = lane == (0 if step == 1 else LANES - 1)
    return jnp.where(edge, extra, main), jnp.where(edge, main, extra)


def put(ref, q, i, pair):
    ref[q, i, :, :LANES], ref[q, i, :, LANES:] = pair


def tiles(lanes):
    return [(z, pl.ds(t, LANES)) for z in halves() for t in range(0, lanes, LANES)]


def own_row(k, c):
    return c * FIELDS + k


def own_value(own, strip, k, c):
    place = own_row(k, c)
    return (own[place],) + beside(strip[place // SLOTS], place % SLOTS)


def halo_value(buffer, bulk, place):
    return (buffer[place],) + beside(buffer[bulk + place // SLOTS], place % SLOTS)


def send_out(far, near, right, left):
    def send(first):
        copy_rows(far, left if first else right)
        copy_rows(near, right if first else left)

    either_way(send)


def take_in(from_left, from_right, from_far, from_near):
    def receive(first):
        copy_rows(from_left, from_far if first else from_near)
        copy_rows(from_right, from_near if first else from_far)

    either_way(receive)


def first_kernel(
    flow_in, heat_in, flow_weight_in, heat_weight_in, resistance_in, conductivity_in, solid_in,
    own_out, strips_out,
    own, strips, flow, heat, flow_weight, heat_weight, resistance, conductivity, solid, arrived, sent,
):
    pairs = [
        (flow_in, flow),
        (heat_in, heat),
        (resistance_in, resistance),
        (conductivity_in, conductivity),
        (solid_in, solid),
        (flow_weight_in, flow_weight),
        (heat_weight_in, heat_weight),
    ]
    copies = [pltpu.make_async_copy(a, b, arrived.at[k]) for k, (a, b) in enumerate(pairs)]
    for copy in copies:
        copy.start()
    strips[...] = jnp.zeros(strips.shape, jnp.float32)
    for copy in copies:
        copy.wait()
    for c in range(2):
        for z in halves():
            mobility = jnp.where(solid[c, z, :] != 0, 0.0, 1.0 / (1.0 + resistance[c, z, :]))
            rate = 1.0 / (0.5 + 0.4 * conductivity[c, z, :])
            p = [flow[q, c, z, :] for q in range(19)] + [heat[q, c, z, :] for q in range(7)]
            after = collide(p, level_sums(p), mobility, rate, range(MEMBERS))
            more = [mobility, rate] + [flow_weight[k, c, z, :] for k in range(3)] + [heat_weight[c, z, :]]
            for k, value in enumerate([after[q] for q in range(MEMBERS)] + more):
                own[own_row(k, c), z, :] = value
    copy_own = pltpu.make_async_copy(own, own_out, sent.at[0])
    copy_own.start()
    rows = pack_rows([lambda slot, k=k: packed(own[k], slot) for k in range(2 * FIELDS)])
    low = low_lanes()
    below, above = ring_place("gy")
    for k in range(HALF_ROWS):
        strips[above, k] = jnp.where(low, rows[k], turn(rows[k + HALF_ROWS], EDGE, 1))
        strips[below, k] = jnp.where(low, turn(rows[k], -EDGE, 1), rows[k + HALF_ROWS])
    copy_strips = pltpu.make_async_copy(strips, strips_out, sent.at[1])
    copy_strips.start()
    copy_own.wait()
    copy_strips.wait()


def halo_kernel(own, strips, far, near, strip, right, left):
    low = low_lanes()
    below, above = ring_place("gy")
    for k in range(HALF_ROWS):
        under, over = strips[below, k], strips[above, k]
        strip[k] = jnp.where(low, under, turn(over, EDGE, 1))
        strip[k + HALF_ROWS] = jnp.where(low, turn(under, -EDGE, 1), over)
    for side, rows, c in ((right, TO_RIGHT, 1), (left, TO_LEFT, 0)):
        level = {q: moved(own_value(own, strip, q, c), VELOCITY[q], 1) for q in LEVEL}
        sums = [level_sums({q: level[q][t] for q in LEVEL}) for t in range(2)]
        parts = []
        for (k, column), row in rows.items():
            if k >= FIELDS:
                side[row] = sums[0][k - FIELDS]
                parts.append(lambda slot, k=k: packed(sums[1][k - FIELDS], slot))
            else:
                place = own_row(k, column)
                side[row] = own[place]
                parts.append(
                    lambda slot, place=place: turn(
                        strip[place // SLOTS], 2 * EDGE * (slot - place % SLOTS), 1
                    )
                )
        for k, row in enumerate(pack_rows(parts)):
            side[BULK_ROWS + k] = row
    send_out(far, near, right, left)


def level_of(p, column, sums):
    return sums(p) if 0 <= column <= 1 else [p[q] for q in LEVEL[:SUMS]]


def second_kernel(
    own, strip, from_far, from_near,
    state, wide_sides, adjoint, by_resistance, by_conductivity, far, near,
    from_left, from_right, after, later, seed, right, left,
):
    take_in(from_left, from_right, from_far, from_near)

    def wide(k, column):
        if column < 0:
            return halo_value(from_left, BULK_ROWS, TO_RIGHT[k, column + 2])
        if column > 1:
            return halo_value(from_right, BULK_ROWS, TO_LEFT[k, column - 2])
        return own_value(own, strip, k, column)

    for column in range(-1, 3):
        i = column + 1
        put(wide_sides, 0, i, moved(wide(MOBILITY, column), STILL, 1))
        put(wide_sides, 1, i, moved(wide(RATE, column), STILL, 1))
        for q in range(MEMBERS):
            if 0 <= column <= 1 or q not in LEVEL:
                put(state, q, i, moved(wide(q, column - VELOCITY[q][0]), VELOCITY[q], 1))
            elif q in LEVEL[:SUMS]:
                put(state, q, i, moved(wide(SUM_FIELDS[LEVEL.index(q)], column), STILL, 1))
    for column in range(-1, 3):
        i = column + 1
        wanted = [q for q in range(MEMBERS) if 0 <= column + VELOCITY[q][0] <= 1]
        for z, y in tiles(WIDE):
            p = [state[q, i, z, y] for q in range(MEMBERS)]
            level = level_of(p, column, level_sums)
            result = collide(p, level, wide_sides[0, i, z, y], wide_sides[1, i, z, y], wanted)
            for q in wanted:
                after[q, i, z, y] = result[q]
    for c in range(2):
        for q in range(MEMBERS):
            put(later, q, c, moved(split(after[q, c + 1 - VELOCITY[q][0]]), VELOCITY[q], 1))
    for column in range(-1, 3):
        weights = [wide(WEIGHT + k, column) for k in range(3)]
        weights = [(main, turn(extra, by, 1)) for main, extra, by in weights]
        for q in range(1, MEMBERS):
            velocity = VELOCITY[q]
            c = column - velocity[0]
            if not 0 <= c <= 1:
                continue
            if q < 19:
                parts = [
                    tuple(value if velocity[k] > 0 else -value for value in weights[k]) for k in range(3) if velocity[k]
                ]
                pair = parts[0] if len(parts) == 1 else tuple(a + b for a, b in zip(*parts))
                pair += (0,)
            else:
                pair = wide(WEIGHT + 3, column)
            put(seed, q, c, moved(pair, velocity, -1))
    for c in range(2):
        for z, y in tiles(WIDE):
            p = [later[q, c, z, y] for q in range(MEMBERS)]
            pa = [jnp.zeros((8, LANES), jnp.float32)] + [seed[q, c, z, y] for q in range(1, MEMBERS)]
            inner = y.start == 0
            result = pull_back(
                p, level_sums(p), pa, level_adjoint_sums(pa),
                wide_sides[0, c + 1, z, y], wide_sides[1, c + 1, z, y], range(MEMBERS), inner,
            )
            if inner:
                by_resistance[c, z, :], by_conductivity[c, z, :] = result["by"]
            for q in range(MEMBERS):
                adjoint[q, c, z, y] = result[q]
    for side, rows, c in ((right, ADJ_TO_RIGHT, 1), (left, ADJ_TO_LEFT, 0)):
        level = {q: moved(split(adjoint[q, c]), VELOCITY[q], -1) for q in LEVEL}
        sums = [level_adjoint_sums({q: level[q][t] for q in LEVEL}) for t in range(2)]
        parts = []
        for (k, column), row in rows.items():
            if k >= FIELDS:
                side[row] = sums[0][k - FIELDS]
                parts.append(lambda slot, k=k: packed(sums[1][k - FIELDS], slot))
            else:
                side[row] = adjoint[k, column, :, :LANES]
                parts.append(lambda slot, k=k, column=column: packed(adjoint[k, column, :, LANES:], slot))
        for k, row in enumerate(pack_rows(parts)):
            side[ADJ_BULK + k] = row
    send_out(far, near, right, left)


def third_kernel(
    flow, heat, state, wide_sides, adjoint, part_resistance, part_conductivity, from_far, from_near,
    by_resistance, by_conductivity,
    from_left, from_right, arrived, earlier, last,
):
    take_in(from_left, from_right, from_far, from_near)

    def wide(k, column):
        if column < 0:
            return halo_value(from_left, ADJ_BULK, ADJ_TO_RIGHT[k, column + 2])
        if column > 1:
            return halo_value(from_right, ADJ_BULK, ADJ_TO_LEFT[k, column - 2])
        return split(adjoint[k, column])

    for column in range(-1, 3):
        i = column + 1
        for q in range(MEMBERS):
            if 0 <= column <= 1 or q not in LEVEL:
                put(arrived, q, i, moved(wide(q, column + VELOCITY[q][0]), VELOCITY[q], -1))
            elif q in LEVEL[:SUMS]:
                put(arrived, q, i, moved(wide(SUM_FIELDS[LEVEL.index(q)], column), STILL, 1))
    for column in range(-1, 3):
        i = column + 1
        own = 0 <= column <= 1
        for z, y in tiles(WIDE):
            inner = y.start == 0
            wanted = [
                q
                for q in range(MEMBERS)
                if 0 <= column - VELOCITY[q][0] <= 1 and (inner or VELOCITY[q][1])
            ]
            p = [state[q, i, z, y] for q in range(MEMBERS)]
            pa = [arrived[q, i, z, y] for q in range(MEMBERS)]
            result = pull_back(
                p, level_of(p, column, level_sums), pa, level_of(pa, column, level_adjoint_sums),
                wide_sides[0, i, z, y], wide_sides[1, i, z, y], wanted, inner and own,
            )
            for q in wanted:
                earlier[q, i, z, y] = result[q]
            if inner and own:
                by_resistance[column, z, :] = part_resistance[column, z, :] + result["by"][0]
                by_conductivity[column, z, :] = part_conductivity[column, z, :] + result["by"][1]
    for c in range(2):
        for q in range(MEMBERS):
            velocity = VELOCITY[q]
            i = c + 1 + velocity[0]
            if velocity[1]:
                last[q, c] = moved(split(earlier[q, i]), velocity, -1)[0]
            else:
                last[q, c] = turn(earlier[q, i, :, :LANES], -velocity[2], 0)
    narrow = pl.ds(0, LANES)
    for c in range(2):
        for z in halves():
            p = [flow[q, c, z, :] for q in range(19)] + [heat[q, c, z, :] for q in range(7)]
            pa = [last[q, c, z, :] for q in range(MEMBERS)]
            result = pull_back(
                p, level_sums(p), pa, level_adjoint_sums(pa),
                wide_sides[0, c + 1, z, narrow], wide_sides[1, c + 1, z, narrow], (), True,
            )
            by_resistance[c, z, :] += result["by"][0]
            by_conductivity[c, z, :] += result["by"][1]


def floats(*shape):
    return jax.ShapeDtypeStruct(shape, jnp.float32)


def vmem(*shape):
    return pltpu.VMEM(shape, jnp.float32)


def swap_along_x(far, near):
    count = lax.axis_size("gx")
    across = [(i, (i + (1 if i % 2 else -1)) % count) for i in range(count)]
    within = [(i, i ^ 1) for i in range(count)]
    return lax.ppermute(far, "gx", across), lax.ppermute(near, "gx", within)


FIRST_PARAMS = pltpu.CompilerParams(vmem_limit_bytes=56 * 1024 * 1024)
PARAMS = pltpu.CompilerParams(vmem_limit_bytes=24 * 1024 * 1024)


def on_device(flow, heat, flow_weight, heat_weight, resistance, conductivity, solid):
    rings = lax.axis_size("gy")
    in_hbm = pl.BlockSpec(memory_space=pltpu.HBM)
    own, strips = pl.pallas_call(
        first_kernel,
        in_specs=[in_hbm] * 7,
        out_specs=[in_hbm] * 2,
        out_shape=(floats(2 * FIELDS, ZED, LANES), floats(rings, HALF_ROWS, ZED, LANES)),
        scratch_shapes=[
            vmem(2 * FIELDS, ZED, LANES),
            vmem(rings, HALF_ROWS, ZED, LANES),
            vmem(19, 2, ZED, LANES),
            vmem(7, 2, ZED, LANES),
            vmem(3, 2, ZED, LANES),
            vmem(2, ZED, LANES),
            vmem(2, ZED, LANES),
            vmem(2, ZED, LANES),
            pltpu.VMEM((2, ZED, LANES), jnp.int32),
            pltpu.SemaphoreType.DMA((7,)),
            pltpu.SemaphoreType.DMA((2,)),
        ],
        compiler_params=FIRST_PARAMS,
        name="collide_own",
    )(flow, heat, flow_weight, heat_weight, resistance, conductivity, solid)

    strips = lax.all_to_all(strips, "gy", 0, 0)

    far, near, strip = pl.pallas_call(
        halo_kernel,
        out_shape=(floats(SENT, ZED, LANES), floats(SENT, ZED, LANES), floats(STRIP_ROWS, ZED, LANES)),
        scratch_shapes=[vmem(SENT, ZED, LANES), vmem(SENT, ZED, LANES)],
        compiler_params=PARAMS,
        name="halo_buffers",
    )(own, strips)

    from_far, from_near = swap_along_x(far, near)

    state, wide_sides, adjoint, part_resistance, part_conductivity, far, near = pl.pallas_call(
        second_kernel,
        out_shape=(
            floats(MEMBERS, 4, ZED, WIDE),
            floats(2, 4, ZED, WIDE),
            floats(MEMBERS, 2, ZED, WIDE),
            floats(2, ZED, LANES),
            floats(2, ZED, LANES),
            floats(ADJ_SENT, ZED, LANES),
            floats(ADJ_SENT, ZED, LANES),
        ),
        scratch_shapes=[
            vmem(SENT, ZED, LANES),
            vmem(SENT, ZED, LANES),
            vmem(MEMBERS, 4, ZED, WIDE),
            vmem(MEMBERS, 2, ZED, WIDE),
            vmem(MEMBERS, 2, ZED, WIDE),
            vmem(ADJ_SENT, ZED, LANES),
            vmem(ADJ_SENT, ZED, LANES),
        ],
        compiler_params=PARAMS,
        name="forward_and_seed",
    )(own, strip, from_far, from_near)

    from_far, from_near = swap_along_x(far, near)

    return pl.pallas_call(
        third_kernel,
        out_shape=(floats(2, ZED, LANES), floats(2, ZED, LANES)),
        scratch_shapes=[
            vmem(ADJ_SENT, ZED, LANES),
            vmem(ADJ_SENT, ZED, LANES),
            vmem(MEMBERS, 4, ZED, WIDE),
            vmem(MEMBERS, 4, ZED, WIDE),
            vmem(MEMBERS, 2, ZED, LANES),
        ],
        compiler_params=PARAMS,
        name="adjoint_steps",
    )(flow, heat, state, wide_sides, adjoint, part_resistance, part_conductivity, from_far, from_near)


def solution(mesh):
    split = P("gx", None, "gy")
    stacked = P(None, "gx", None, "gy")
    return jax.shard_map(
        on_device,
        mesh=mesh,
        in_specs=(stacked, stacked, stacked, split, split, split, split),
        out_specs=(split, split),
        check_vma=False,
    )
```

time: 52.3 us -> 47 us (0.90)
  Pallas kernels: 10.1 us -> 5.59 us
    pallas_call x1, Pallas kernels: 4.15 us -> 1.64 us  [on_device(): pl.pallas_call(second_kernel, out_shape=(floats(MEMBERS, 4, ZED, WIDE), f...]
    pallas_call x2, Pallas kernels: 4 us -> 2.48 us  [the longest x1 2.13 us: on_device(): pl.pallas_call(first_kernel, in_specs=[in_hbm] * 7, out_specs=[in_hbm] *...]
where the time goes in v4:
time: 47 us; the launch traced here: 46.5 us
  starting transfers between devices  25.5 us (54%)
  blocking collectives  11.5 us (24%)
  Pallas kernels  5.59 us (12%)
  waiting for transfers between devices  2.13 us (5%)
  local copies, waits for them, and re-layouts  1.05 us (2%)
  between operations  0.72 us (2%)
    ppermute x4, starting transfers between devices, swap_along_x(): return (lax.ppermute(far, 'gx', across), lax.ppermute(near, 'gx', within))  25.5 us
    all_to_all x1, blocking collectives, on_device(): strips = lax.all_to_all(strips, 'gy', 0, 0)  11.5 us
    pallas_call x1, Pallas kernels, on_device(): pl.pallas_call(first_kernel, in_specs=[in_hbm] * 7, out_specs=[in_hbm] *...  2.13 us
    ppermute x4, waiting for transfers between devices, swap_along_x(): return (lax.ppermute(far, 'gx', across), lax.ppermute(near, 'gx', within))  2.13 us
    pallas_call x1, Pallas kernels, on_device(): pl.pallas_call(second_kernel, out_shape=(floats(MEMBERS, 4, ZED, WIDE), f...  1.64 us
    pallas_call x1, Pallas kernels, on_device(): pl.pallas_call(third_kernel, out_shape=(floats(2, ZED, LANES), floats(2,...  1.47 us
    unnamed x6, local copies, waits for them, and re-layouts  1.05 us
  transfers between devices with their start and end apart: 4, of which 2 were waited for; matrix products, arithmetic and copies ran while one was open for 0% of the time, Pallas kernels for 0%

profile of v4, /device:TPU:1, one launch (start us, length us, event | category | flops | bytes accessed | tf_op | source)
XLA Modules:
  0.0 46.5 jit_solution(1398636806069773281)
XLA Ops:
  0.6 0.0 copy-start.2
  0.6 0.0 copy-start.1
  0.7 2.1 %collide_own.1 = (f32[64,16,128]{2,1,0:T(8,128)}, f32[8,2,16,128]{3,2,1,0:T(8,128)}) custom-call(f32[19,2,16,128]{3,2,1,0:T(8,128)} %flow.1, f32[7,2,16,128]{3,2,1,0:T(8,128)} %heat.1, f32[3,2,16,128]{3,2,1,0:T(8,128)} %flow_weight_in.1, f32[2,16,128]{2,1,0:T(8,128)} %heat_weight_in.1, f32[2,16,128]{2,1,0:T(8,128)} %resistance_in.1, ...), custom_call_target="tpu_custom_call" | custom-call | tf_op jit(solution)/shard_map/collide_own/pallas_call | solution.py:591
  2.8 11.5 %all_to_all.5.strips = f32[8,2,16,128]{3,2,1,0:T(8,128)S(1)} all-to-all(f32[8,2,16,128]{3,2,1,0:T(8,128)} %get-tuple-element.15), channel_id=1, replica_groups=mesh['gx'=64,'gy'=8] {'gy'}, dimensions={0} | all-to-all | bytes 262144 | tf_op jit(solution)/shard_map/all_to_all | solution.py:613
  14.3 0.0 copy-start
  14.3 1.0 %copy-done = f32[64,16,128]{2,1,0:T(8,128)S(1)} copy-done((f32[64,16,128]{2,1,0:T(8,128)S(1)}, f32[64,16,128]{2,1,0:T(8,128)}, u32[]{:S(2)}) %copy-start) | copy-done | bytes 524312
  15.3 0.4 halo_buffers.1
  15.7 5.5 %collective-permute-start = (f32[29,16,128]{2,1,0:T(8,128)S(1)}, f32[29,16,128]{2,1,0:T(8,128)S(1)}, u32[]{:S(2)}, u32[]{:S(2)}) collective-permute-start(f32[29,16,128]{2,1,0:T(8,128)S(1)} %get-tuple-element.17), channel_id=1, source_target_pairs={{0,504},{8,16},{16,8},{24,32},{32,24},{40,48},{48,40},{56,64},{64,... | collective-permute-start | bytes 712712 | tf_op jit(solution)/shard_map/ppermute | solution.py:581
  21.2 10.1 %collective-permute-start.1 = (f32[29,16,128]{2,1,0:T(8,128)S(1)}, f32[29,16,128]{2,1,0:T(8,128)S(1)}, u32[]{:S(2)}, u32[]{:S(2)}) collective-permute-start(f32[29,16,128]{2,1,0:T(8,128)S(1)} %get-tuple-element.18), channel_id=1, source_target_pairs={{0,8},{8,0},{16,24},{24,16},{32,40},{40,32},{48,56},{56,48},{64,72... | collective-permute-start | bytes 712712 | tf_op jit(solution)/shard_map/ppermute | solution.py:581
  31.3 0.0 collective-permute-done.from_far
  31.3 1.1 %collective-permute-done.1.from_near = f32[29,16,128]{2,1,0:T(8,128)S(1)} collective-permute-done((f32[29,16,128]{2,1,0:T(8,128)S(1)}, f32[29,16,128]{2,1,0:T(8,128)S(1)}, u32[]{:S(2)}, u32[]{:S(2)}) %collective-permute-start.1) | collective-permute-done | bytes 237600 | tf_op jit(solution)/shard_map/ppermute | solution.py:581
  32.4 1.6 %forward_and_seed.1 = (f32[26,4,16,256]{3,2,1,0:T(8,128)S(1)}, f32[2,4,16,256]{3,2,1,0:T(8,128)S(1)}, f32[26,2,16,256]{3,2,1,0:T(8,128)S(1)}, f32[2,16,128]{2,1,...) custom-call(f32[64,16,128]{2,1,0:T(8,128)S(1)} %copy-done, ...), custom_call_target="tpu_custom_call" | custom-call | tf_op jit(solution)/shard_map/forward_and_seed/pallas_call | solution.py:625
  34.1 1.9 %collective-permute-start.2 = (f32[23,16,128]{2,1,0:T(8,128)S(1)}, f32[23,16,128]{2,1,0:T(8,128)S(1)}, u32[]{:S(2)}, u32[]{:S(2)}) collective-permute-start(f32[23,16,128]{2,1,0:T(8,128)S(1)} %get-tuple-element.24), channel_id=1, source_target_pairs={{0,504},{8,16},{16,8},{24,32},{32,24},{40,48},{48,40},{56,64},{64,... | collective-permute-start | bytes 565256 | tf_op jit(solution)/shard_map/ppermute | solution.py:581
  36.0 8.0 %collective-permute-start.3 = (f32[23,16,128]{2,1,0:T(8,128)S(1)}, f32[23,16,128]{2,1,0:T(8,128)S(1)}, u32[]{:S(2)}, u32[]{:S(2)}) collective-permute-start(f32[23,16,128]{2,1,0:T(8,128)S(1)} %get-tuple-element.25), channel_id=1, source_target_pairs={{0,8},{8,0},{16,24},{24,16},{32,40},{40,32},{48,56},{56,48},{64,72... | collective-permute-start | bytes 565256 | tf_op jit(solution)/shard_map/ppermute | solution.py:581
  44.0 0.0 collective-permute-done.2.from_far
  44.0 1.0 %collective-permute-done.3.from_near = f32[23,16,128]{2,1,0:T(8,128)S(1)} collective-permute-done((f32[23,16,128]{2,1,0:T(8,128)S(1)}, f32[23,16,128]{2,1,0:T(8,128)S(1)}, u32[]{:S(2)}, u32[]{:S(2)}) %collective-permute-start.3) | collective-permute-done | bytes 188448 | tf_op jit(solution)/shard_map/ppermute | solution.py:581
  45.1 0.0 copy-done.2
  45.1 0.0 copy-done.1
  45.1 1.5 %adjoint_steps.1 = (f32[2,16,128]{2,1,0:T(8,128)}, f32[2,16,128]{2,1,0:T(8,128)}) custom-call(f32[19,2,16,128]{3,2,1,0:T(8,128)S(1)} %copy-done.1, f32[7,2,16,128]{3,2,1,0:T(8,128)S(1)} %copy-done.2, f32[26,4,16,256]{3,2,1,0:T(8,128)S(1)} %get-tuple-element.19.state, f32[2,4,16,256]{3,2,1,0:T(8,128)S(1)} %get-tuple-element.20.wide_sides, ...), custom_call_target="tpu_custom_call" | custom-call | tf_op jit(solution)/shard_map/adjoint_steps/pallas_call | solution.py:651
Async XLA Ops:
  0.6 44.4 %copy-start.2 = (f32[7,2,16,128]{3,2,1,0:T(8,128)S(1)}, f32[7,2,16,128]{3,2,1,0:T(8,128)}, u32[]{:S(2)}) copy-start(f32[7,2,16,128]{3,2,1,0:T(8,128)} %heat.1) | copy-start | bytes 344068
  0.6 44.4 %copy-start.1 = (f32[19,2,16,128]{3,2,1,0:T(8,128)S(1)}, f32[19,2,16,128]{3,2,1,0:T(8,128)}, u32[]{:S(2)}) copy-start(f32[19,2,16,128]{3,2,1,0:T(8,128)} %flow.1) | copy-start | bytes 933892
  14.3 1.0 %copy-start = (f32[64,16,128]{2,1,0:T(8,128)S(1)}, f32[64,16,128]{2,1,0:T(8,128)}, u32[]{:S(2)}) copy-start(f32[64,16,128]{2,1,0:T(8,128)} %get-tuple-element.14.own) | copy-start | bytes 1572868
  15.7 15.6 %collective-permute-start = (f32[29,16,128]{2,1,0:T(8,128)S(1)}, f32[29,16,128]{2,1,0:T(8,128)S(1)}, u32[]{:S(2)}, u32[]{:S(2)}) collective-permute-start(f32[29,16,128]{2,1,0:T(8,128)S(1)} %get-tuple-element.17), channel_id=1, source_target_pairs={{0,504},{8,16},{16,8},{24,32},{32,24},{40,48},{48,40},{56,64},{64,... | collective-permute-start | bytes 712712 | tf_op jit(solution)/shard_map/ppermute | solution.py:581
  21.2 11.2 %collective-permute-start.1 = (f32[29,16,128]{2,1,0:T(8,128)S(1)}, f32[29,16,128]{2,1,0:T(8,128)S(1)}, u32[]{:S(2)}, u32[]{:S(2)}) collective-permute-start(f32[29,16,128]{2,1,0:T(8,128)S(1)} %get-tuple-element.18), channel_id=1, source_target_pairs={{0,8},{8,0},{16,24},{24,16},{32,40},{40,32},{48,56},{56,48},{64,72... | collective-permute-start | bytes 712712 | tf_op jit(solution)/shard_map/ppermute | solution.py:581
  34.1 9.9 %collective-permute-start.2 = (f32[23,16,128]{2,1,0:T(8,128)S(1)}, f32[23,16,128]{2,1,0:T(8,128)S(1)}, u32[]{:S(2)}, u32[]{:S(2)}) collective-permute-start(f32[23,16,128]{2,1,0:T(8,128)S(1)} %get-tuple-element.24), channel_id=1, source_target_pairs={{0,504},{8,16},{16,8},{24,32},{32,24},{40,48},{48,40},{56,64},{64,... | collective-permute-start | bytes 565256 | tf_op jit(solution)/shard_map/ppermute | solution.py:581
  36.0 9.1 %collective-permute-start.3 = (f32[23,16,128]{2,1,0:T(8,128)S(1)}, f32[23,16,128]{2,1,0:T(8,128)S(1)}, u32[]{:S(2)}, u32[]{:S(2)}) collective-permute-start(f32[23,16,128]{2,1,0:T(8,128)S(1)} %get-tuple-element.25), channel_id=1, source_target_pairs={{0,8},{8,0},{16,24},{24,16},{32,40},{40,32},{48,56},{56,48},{64,72... | collective-permute-start | bytes 565256 | tf_op jit(solution)/shard_map/ppermute | solution.py:581

commit v5 on v4

--- a/solution.py
+++ b/solution.py
@@ -272,12 +272,6 @@
     return lax.broadcasted_iota(jnp.int32, (ZED, LANES), 1) % (2 * EDGE) < EDGE
 
 
-def ring_place(axis):
-    count = lax.axis_size(axis)
-    place = lax.axis_index(axis)
-    return lax.rem(place + count - 1, count), lax.rem(place + 1, count)
-
-
 def either_way(move):
     first = lax.rem(lax.axis_index("gx"), 2) == 0
     pl.when(first)(lambda: move(True))
@@ -349,8 +343,8 @@
 
 def first_kernel(
     flow_in, heat_in, flow_weight_in, heat_weight_in, resistance_in, conductivity_in, solid_in,
-    own_out, strips_out,
-    own, strips, flow, heat, flow_weight, heat_weight, resistance, conductivity, solid, arrived, sent,
+    own_out, up_out, down_out,
+    own, up, down, flow, heat, flow_weight, heat_weight, resistance, conductivity, solid, arrived, sent,
 ):
     pairs = [
         (flow_in, flow),
@@ -364,7 +358,6 @@
     copies = [pltpu.make_async_copy(a, b, arrived.at[k]) for k, (a, b) in enumerate(pairs)]
     for copy in copies:
         copy.start()
-    strips[...] = jnp.zeros(strips.shape, jnp.float32)
     for copy in copies:
         copy.wait()
     for c in range(2):
@@ -380,21 +373,28 @@
     copy_own.start()
     rows = pack_rows([lambda slot, k=k: packed(own[k], slot) for k in range(2 * FIELDS)])
     low = low_lanes()
-    below, above = ring_place("gy")
     for k in range(HALF_ROWS):
-        strips[above, k] = jnp.where(low, rows[k], turn(rows[k + HALF_ROWS], EDGE, 1))
-        strips[below, k] = jnp.where(low, turn(rows[k], -EDGE, 1), rows[k + HALF_ROWS])
-    copy_strips = pltpu.make_async_copy(strips, strips_out, sent.at[1])
-    copy_strips.start()
+        up[k] = jnp.where(low, rows[k], turn(rows[k + HALF_ROWS], EDGE, 1))
+        down[k] = jnp.where(low, turn(rows[k], -EDGE, 1), rows[k + HALF_ROWS])
+    copies = [
+        pltpu.make_async_copy(up, up_out, sent.at[1]),
+        pltpu.make_async_copy(down, down_out, sent.at[2]),
+    ]
+    for copy in copies:
+        copy.start()
     copy_own.wait()
-    copy_strips.wait()
-
-
-def halo_kernel(own, strips, far, near, strip, right, left):
+    for copy in copies:
+        copy.wait()
+
+
+def stage_kernel(own, staged):
+    copy_rows(staged, own)
+
+
+def halo_kernel(own, from_below, from_above, far, near, strip, right, left):
     low = low_lanes()
-    below, above = ring_place("gy")
     for k in range(HALF_ROWS):
-        under, over = strips[below, k], strips[above, k]
+        under, over = from_below[k], from_above[k]
         strip[k] = jnp.where(low, under, turn(over, EDGE, 1))
         strip[k + HALF_ROWS] = jnp.where(low, turn(under, -EDGE, 1), over)
     for side, rows, c in ((right, TO_RIGHT, 1), (left, TO_LEFT, 0)):
@@ -586,16 +586,20 @@
 
 
 def on_device(flow, heat, flow_weight, heat_weight, resistance, conductivity, solid):
-    rings = lax.axis_size("gy")
     in_hbm = pl.BlockSpec(memory_space=pltpu.HBM)
-    own, strips = pl.pallas_call(
+    own, up, down = pl.pallas_call(
         first_kernel,
         in_specs=[in_hbm] * 7,
-        out_specs=[in_hbm] * 2,
-        out_shape=(floats(2 * FIELDS, ZED, LANES), floats(rings, HALF_ROWS, ZED, LANES)),
+        out_specs=[in_hbm] * 3,
+        out_shape=(
+            floats(2 * FIELDS, ZED, LANES),
+            floats(HALF_ROWS, ZED, LANES),
+            floats(HALF_ROWS, ZED, LANES),
+        ),
         scratch_shapes=[
             vmem(2 * FIELDS, ZED, LANES),
-            vmem(rings, HALF_ROWS, ZED, LANES),
+            vmem(HALF_ROWS, ZED, LANES),
+            vmem(HALF_ROWS, ZED, LANES),
             vmem(19, 2, ZED, LANES),
             vmem(7, 2, ZED, LANES),
             vmem(3, 2, ZED, LANES),
@@ -604,13 +608,24 @@
             vmem(2, ZED, LANES),
             pltpu.VMEM((2, ZED, LANES), jnp.int32),
             pltpu.SemaphoreType.DMA((7,)),
-            pltpu.SemaphoreType.DMA((2,)),
+            pltpu.SemaphoreType.DMA((3,)),
         ],
         compiler_params=FIRST_PARAMS,
         name="collide_own",
     )(flow, heat, flow_weight, heat_weight, resistance, conductivity, solid)
 
-    strips = lax.all_to_all(strips, "gy", 0, 0)
+    count = lax.axis_size("gy")
+    upward = [(i, (i + 1) % count) for i in range(count)]
+    from_below = lax.ppermute(up, "gy", upward)
+    from_above = lax.ppermute(down, "gy", [(target, source) for source, target in upward])
+
+    own = pl.pallas_call(
+        stage_kernel,
+        out_shape=floats(2 * FIELDS, ZED, LANES),
+        compiler_params=PARAMS,
+        cost_estimate=pl.CostEstimate(flops=10**7, bytes_accessed=10**6, transcendentals=0),
+        name="stage_own",
+    )(own)
 
     far, near, strip = pl.pallas_call(
         halo_kernel,
@@ -618,7 +633,7 @@
         scratch_shapes=[vmem(SENT, ZED, LANES), vmem(SENT, ZED, LANES)],
         compiler_params=PARAMS,
         name="halo_buffers",
-    )(own, strips)
+    )(own, from_below, from_above)
 
     from_far, from_near = swap_along_x(far, near)
 

time: 47 us -> 43.9 us (0.934)
  blocking collectives: 11.5 us -> 0 us
  starting transfers between devices: 25.5 us -> 34 us
    all_to_all x1 -> x0, blocking collectives: 11.5 us -> none  [on_device(): strips = lax.all_to_all(strips, 'gy', 0, 0)]
    ppermute x0 -> x2, starting transfers between devices: none -> 8.32 us  [the longest x1 4.37 us: on_device(): lax.ppermute(down, 'gy', [(target, source) for source, target in upward])]
  transfers between devices with their start and end apart: 4 -> 6, of which waited for: 2 -> 2; matrix products, arithmetic and copies ran while one was open for 0% -> 0% of each run, Pallas kernels for 0% -> 0%
where the time goes in v5:
time: 43.9 us; the launch traced here: 43.6 us
  starting transfers between devices  34 us (77%)
  Pallas kernels  5.59 us (13%)
  waiting for transfers between devices  2.13 us (5%)
  local copies, waits for them, and re-layouts  1.04 us (2%)
  between operations  0.76 us (2%)
    ppermute x4, starting transfers between devices, swap_along_x(): return (lax.ppermute(far, 'gx', across), lax.ppermute(near, 'gx', within))  25.7 us
    ppermute x1, starting transfers between devices, on_device(): lax.ppermute(down, 'gy', [(target, source) for source, target in upward])  4.37 us
    ppermute x1, starting transfers between devices, on_device(): from_below = lax.ppermute(up, 'gy', upward)  3.95 us
    ppermute x4, waiting for transfers between devices, swap_along_x(): return (lax.ppermute(far, 'gx', across), lax.ppermute(near, 'gx', within))  2.13 us
    pallas_call x1, Pallas kernels, on_device(): pl.pallas_call(first_kernel, in_specs=[in_hbm] * 7, out_specs=[in_hbm] *...  2.1 us
    pallas_call x1, Pallas kernels, on_device(): pl.pallas_call(second_kernel, out_shape=(floats(MEMBERS, 4, ZED, WIDE), f...  1.64 us
    pallas_call x1, Pallas kernels, on_device(): pl.pallas_call(third_kernel, out_shape=(floats(2, ZED, LANES), floats(2,...  1.47 us
    unnamed x6, local copies, waits for them, and re-layouts  1.04 us
  transfers between devices with their start and end apart: 6, of which 2 were waited for; matrix products, arithmetic and copies ran while one was open for 0% of the time, Pallas kernels for 0%

profile of v5, /device:TPU:1, one launch (start us, length us, event | category | flops | bytes accessed | tf_op | source)
XLA Modules:
  0.0 43.6 jit_solution(10673665509378344932)
XLA Ops:
  0.6 0.0 copy-start.2
  0.6 0.0 copy-start
  0.7 2.1 %collide_own.1 = (f32[64,16,128]{2,1,0:T(8,128)}, f32[2,16,128]{2,1,0:T(8,128)}, f32[2,16,128]{2,1,0:T(8,128)}) custom-call(f32[19,2,16,128]{3,2,1,0:T(8,128)} %flow.1, f32[7,2,16,128]{3,2,1,0:T(8,128)} %heat.1, f32[3,2,16,128]{3,2,1,0:T(8,128)} %flow_weight_in.1, f32[2,16,128]{2,1,0:T(8,128)} %heat_weight_in.1, f32[2,16,128]{2,1,0:T(8,128)} %resistance_in.1, ...), custom_call_target="tpu_custom_call" | custom-call | tf_op jit(solution)/shard_map/collide_own/pallas_call | solution.py:590
  2.8 3.9 %collective-permute-start = (f32[2,16,128]{2,1,0:T(8,128)}, f32[2,16,128]{2,1,0:T(8,128)S(1)}, u32[]{:S(2)}, u32[]{:S(2)}) collective-permute-start(f32[2,16,128]{2,1,0:T(8,128)} %get-tuple-element.16), channel_id=1, source_target_pairs={{0,1},{1,2},{2,3},{3,4},{4,5},{5,6},{6,7},{7,0},{8,9},{9,10},{10,1... | collective-permute-start | bytes 49160 | tf_op jit(solution)/shard_map/ppermute | solution.py:619
  6.7 4.4 %collective-permute-start.1 = (f32[2,16,128]{2,1,0:T(8,128)}, f32[2,16,128]{2,1,0:T(8,128)S(1)}, u32[]{:S(2)}, u32[]{:S(2)}) collective-permute-start(f32[2,16,128]{2,1,0:T(8,128)} %get-tuple-element.17), channel_id=1, source_target_pairs={{1,0},{2,1},{3,2},{4,3},{5,4},{6,5},{7,6},{0,7},{9,8},{10,9},{11,1... | collective-permute-start | bytes 49160 | tf_op jit(solution)/shard_map/ppermute | solution.py:620
  11.1 0.0 copy-start.1
  11.1 1.0 %copy-done.1 = f32[64,16,128]{2,1,0:T(8,128)S(1)} copy-done((f32[64,16,128]{2,1,0:T(8,128)S(1)}, f32[64,16,128]{2,1,0:T(8,128)}, u32[]{:S(2)}) %copy-start.1) | copy-done | bytes 524312
  12.2 0.0 collective-permute-done.from_below
  12.2 0.0 collective-permute-done.1.from_above
  12.2 0.4 halo_buffers.1
  12.6 5.1 %collective-permute-start.2 = (f32[29,16,128]{2,1,0:T(8,128)S(1)}, f32[29,16,128]{2,1,0:T(8,128)S(1)}, u32[]{:S(2)}, u32[]{:S(2)}) collective-permute-start(f32[29,16,128]{2,1,0:T(8,128)S(1)} %get-tuple-element.19), channel_id=1, source_target_pairs={{0,504},{8,16},{16,8},{24,32},{32,24},{40,48},{48,40},{56,64},{64,... | collective-permute-start | bytes 712712 | tf_op jit(solution)/shard_map/ppermute | solution.py:581
  17.6 10.7 %collective-permute-start.3 = (f32[29,16,128]{2,1,0:T(8,128)S(1)}, f32[29,16,128]{2,1,0:T(8,128)S(1)}, u32[]{:S(2)}, u32[]{:S(2)}) collective-permute-start(f32[29,16,128]{2,1,0:T(8,128)S(1)} %get-tuple-element.20), channel_id=1, source_target_pairs={{0,8},{8,0},{16,24},{24,16},{32,40},{40,32},{48,56},{56,48},{64,72... | collective-permute-start | bytes 712712 | tf_op jit(solution)/shard_map/ppermute | solution.py:581
  28.4 0.0 collective-permute-done.2.from_far
  28.4 1.1 %collective-permute-done.3.from_near = f32[29,16,128]{2,1,0:T(8,128)S(1)} collective-permute-done((f32[29,16,128]{2,1,0:T(8,128)S(1)}, f32[29,16,128]{2,1,0:T(8,128)S(1)}, u32[]{:S(2)}, u32[]{:S(2)}) %collective-permute-start.3) | collective-permute-done | bytes 237600 | tf_op jit(solution)/shard_map/ppermute | solution.py:581
  29.5 1.6 %forward_and_seed.1 = (f32[26,4,16,256]{3,2,1,0:T(8,128)S(1)}, f32[2,4,16,256]{3,2,1,0:T(8,128)S(1)}, f32[26,2,16,256]{3,2,1,0:T(8,128)S(1)}, f32[2,16,128]{2,1,...) custom-call(f32[64,16,128]{2,1,0:T(8,128)S(1)} %stage_own.1.own, ...), custom_call_target="tpu_custom_call" | custom-call | tf_op jit(solution)/shard_map/forward_and_seed/pallas_call | solution.py:640
  31.1 1.9 %collective-permute-start.4 = (f32[23,16,128]{2,1,0:T(8,128)S(1)}, f32[23,16,128]{2,1,0:T(8,128)S(1)}, u32[]{:S(2)}, u32[]{:S(2)}) collective-permute-start(f32[23,16,128]{2,1,0:T(8,128)S(1)} %get-tuple-element.26), channel_id=1, source_target_pairs={{0,504},{8,16},{16,8},{24,32},{32,24},{40,48},{48,40},{56,64},{64,... | collective-permute-start | bytes 565256 | tf_op jit(solution)/shard_map/ppermute | solution.py:581
  33.0 8.0 %collective-permute-start.5 = (f32[23,16,128]{2,1,0:T(8,128)S(1)}, f32[23,16,128]{2,1,0:T(8,128)S(1)}, u32[]{:S(2)}, u32[]{:S(2)}) collective-permute-start(f32[23,16,128]{2,1,0:T(8,128)S(1)} %get-tuple-element.27), channel_id=1, source_target_pairs={{0,8},{8,0},{16,24},{24,16},{32,40},{40,32},{48,56},{56,48},{64,72... | collective-permute-start | bytes 565256 | tf_op jit(solution)/shard_map/ppermute | solution.py:581
  41.1 0.0 collective-permute-done.4.from_far
  41.1 1.0 %collective-permute-done.5.from_near = f32[23,16,128]{2,1,0:T(8,128)S(1)} collective-permute-done((f32[23,16,128]{2,1,0:T(8,128)S(1)}, f32[23,16,128]{2,1,0:T(8,128)S(1)}, u32[]{:S(2)}, u32[]{:S(2)}) %collective-permute-start.5) | collective-permute-done | bytes 188448 | tf_op jit(solution)/shard_map/ppermute | solution.py:581
  42.1 0.0 copy-done.2
  42.1 0.0 copy-done
  42.1 1.5 %adjoint_steps.1 = (f32[2,16,128]{2,1,0:T(8,128)}, f32[2,16,128]{2,1,0:T(8,128)}) custom-call(f32[19,2,16,128]{3,2,1,0:T(8,128)S(1)} %copy-done, f32[7,2,16,128]{3,2,1,0:T(8,128)S(1)} %copy-done.2, f32[26,4,16,256]{3,2,1,0:T(8,128)S(1)} %get-tuple-element.21.state, f32[2,4,16,256]{3,2,1,0:T(8,128)S(1)} %get-tuple-element.22.wide_sides, ...), custom_call_target="tpu_custom_call" | custom-call | tf_op jit(solution)/shard_map/adjoint_steps/pallas_call | solution.py:666
  (1 shorter events, 0.0 us)
Async XLA Ops:
  0.6 41.5 %copy-start.2 = (f32[7,2,16,128]{3,2,1,0:T(8,128)S(1)}, f32[7,2,16,128]{3,2,1,0:T(8,128)}, u32[]{:S(2)}) copy-start(f32[7,2,16,128]{3,2,1,0:T(8,128)} %heat.1) | copy-start | bytes 344068
  0.6 41.5 %copy-start = (f32[19,2,16,128]{3,2,1,0:T(8,128)S(1)}, f32[19,2,16,128]{3,2,1,0:T(8,128)}, u32[]{:S(2)}) copy-start(f32[19,2,16,128]{3,2,1,0:T(8,128)} %flow.1) | copy-start | bytes 933892
  2.8 9.4 %collective-permute-start = (f32[2,16,128]{2,1,0:T(8,128)}, f32[2,16,128]{2,1,0:T(8,128)S(1)}, u32[]{:S(2)}, u32[]{:S(2)}) collective-permute-start(f32[2,16,128]{2,1,0:T(8,128)} %get-tuple-element.16), channel_id=1, source_target_pairs={{0,1},{1,2},{2,3},{3,4},{4,5},{5,6},{6,7},{7,0},{8,9},{9,10},{10,1... | collective-permute-start | bytes 49160 | tf_op jit(solution)/shard_map/ppermute | solution.py:619
  6.7 5.5 %collective-permute-start.1 = (f32[2,16,128]{2,1,0:T(8,128)}, f32[2,16,128]{2,1,0:T(8,128)S(1)}, u32[]{:S(2)}, u32[]{:S(2)}) collective-permute-start(f32[2,16,128]{2,1,0:T(8,128)} %get-tuple-element.17), channel_id=1, source_target_pairs={{1,0},{2,1},{3,2},{4,3},{5,4},{6,5},{7,6},{0,7},{9,8},{10,9},{11,1... | collective-permute-start | bytes 49160 | tf_op jit(solution)/shard_map/ppermute | solution.py:620
  11.1 1.0 %copy-start.1 = (f32[64,16,128]{2,1,0:T(8,128)S(1)}, f32[64,16,128]{2,1,0:T(8,128)}, u32[]{:S(2)}) copy-start(f32[64,16,128]{2,1,0:T(8,128)} %get-tuple-element.15.own) | copy-start | bytes 1572868
  12.6 15.8 %collective-permute-start.2 = (f32[29,16,128]{2,1,0:T(8,128)S(1)}, f32[29,16,128]{2,1,0:T(8,128)S(1)}, u32[]{:S(2)}, u32[]{:S(2)}) collective-permute-start(f32[29,16,128]{2,1,0:T(8,128)S(1)} %get-tuple-element.19), channel_id=1, source_target_pairs={{0,504},{8,16},{16,8},{24,32},{32,24},{40,48},{48,40},{56,64},{64,... | collective-permute-start | bytes 712712 | tf_op jit(solution)/shard_map/ppermute | solution.py:581
  17.6 11.8 %collective-permute-start.3 = (f32[29,16,128]{2,1,0:T(8,128)S(1)}, f32[29,16,128]{2,1,0:T(8,128)S(1)}, u32[]{:S(2)}, u32[]{:S(2)}) collective-permute-start(f32[29,16,128]{2,1,0:T(8,128)S(1)} %get-tuple-element.20), channel_id=1, source_target_pairs={{0,8},{8,0},{16,24},{24,16},{32,40},{40,32},{48,56},{56,48},{64,72... | collective-permute-start | bytes 712712 | tf_op jit(solution)/shard_map/ppermute | solution.py:581
  31.1 9.9 %collective-permute-start.4 = (f32[23,16,128]{2,1,0:T(8,128)S(1)}, f32[23,16,128]{2,1,0:T(8,128)S(1)}, u32[]{:S(2)}, u32[]{:S(2)}) collective-permute-start(f32[23,16,128]{2,1,0:T(8,128)S(1)} %get-tuple-element.26), channel_id=1, source_target_pairs={{0,504},{8,16},{16,8},{24,32},{32,24},{40,48},{48,40},{56,64},{64,... | collective-permute-start | bytes 565256 | tf_op jit(solution)/shard_map/ppermute | solution.py:581
  33.0 9.1 %collective-permute-start.5 = (f32[23,16,128]{2,1,0:T(8,128)S(1)}, f32[23,16,128]{2,1,0:T(8,128)S(1)}, u32[]{:S(2)}, u32[]{:S(2)}) collective-permute-start(f32[23,16,128]{2,1,0:T(8,128)S(1)} %get-tuple-element.27), channel_id=1, source_target_pairs={{0,8},{8,0},{16,24},{24,16},{32,40},{40,32},{48,56},{56,48},{64,72... | collective-permute-start | bytes 565256 | tf_op jit(solution)/shard_map/ppermute | solution.py:581

commit v6 on v5

--- a/solution.py
+++ b/solution.py
@@ -424,8 +424,8 @@
 
 def second_kernel(
     own, strip, from_far, from_near,
-    state, wide_sides, adjoint, by_resistance, by_conductivity, far, near,
-    from_left, from_right, after, later, seed, right, left,
+    state, wide_sides, adjoint, by_resistance, by_conductivity, right, left,
+    from_left, from_right, after, later, seed,
 ):
     take_in(from_left, from_right, from_far, from_near)
 
@@ -500,16 +500,13 @@
                 parts.append(lambda slot, k=k, column=column: packed(adjoint[k, column, :, LANES:], slot))
         for k, row in enumerate(pack_rows(parts)):
             side[ADJ_BULK + k] = row
-    send_out(far, near, right, left)
 
 
 def third_kernel(
-    flow, heat, state, wide_sides, adjoint, part_resistance, part_conductivity, from_far, from_near,
+    flow, heat, state, wide_sides, adjoint, part_resistance, part_conductivity, from_left, from_right,
     by_resistance, by_conductivity,
-    from_left, from_right, arrived, earlier, last,
+    arrived, earlier, last,
 ):
-    take_in(from_left, from_right, from_far, from_near)
-
     def wide(k, column):
         if column < 0:
             return halo_value(from_left, ADJ_BULK, ADJ_TO_RIGHT[k, column + 2])
@@ -637,7 +634,7 @@
 
     from_far, from_near = swap_along_x(far, near)
 
-    state, wide_sides, adjoint, part_resistance, part_conductivity, far, near = pl.pallas_call(
+    state, wide_sides, adjoint, part_resistance, part_conductivity, right, left = pl.pallas_call(
         second_kernel,
         out_shape=(
             floats(MEMBERS, 4, ZED, WIDE),
@@ -654,28 +651,27 @@
             vmem(MEMBERS, 4, ZED, WIDE),
             vmem(MEMBERS, 2, ZED, WIDE),
             vmem(MEMBERS, 2, ZED, WIDE),
-            vmem(ADJ_SENT, ZED, LANES),
-            vmem(ADJ_SENT, ZED, LANES),
         ],
         compiler_params=PARAMS,
         name="forward_and_seed",
     )(own, strip, from_far, from_near)
 
-    from_far, from_near = swap_along_x(far, near)
+    count = lax.axis_size("gx")
+    rightward = [(i, (i + 1) % count) for i in range(count)]
+    from_left = lax.ppermute(right, "gx", rightward)
+    from_right = lax.ppermute(left, "gx", [(target, source) for source, target in rightward])
 
     return pl.pallas_call(
         third_kernel,
         out_shape=(floats(2, ZED, LANES), floats(2, ZED, LANES)),
         scratch_shapes=[
-            vmem(ADJ_SENT, ZED, LANES),
-            vmem(ADJ_SENT, ZED, LANES),
             vmem(MEMBERS, 4, ZED, WIDE),
             vmem(MEMBERS, 4, ZED, WIDE),
             vmem(MEMBERS, 2, ZED, LANES),
         ],
         compiler_params=PARAMS,
         name="adjoint_steps",
-    )(flow, heat, state, wide_sides, adjoint, part_resistance, part_conductivity, from_far, from_near)
+    )(flow, heat, state, wide_sides, adjoint, part_resistance, part_conductivity, from_left, from_right)
 
 
 def solution(mesh):

time: 43.9 us -> 45.2 us (1.030)
  the two profiles are of different devices: /device:TPU:1 before, /device:TPU:26 now
where the time goes in v6:
time: 45.2 us; the launch traced here: 44.9 us
  starting transfers between devices  26.4 us (58%)
  waiting for transfers between devices  11.2 us (25%)
  Pallas kernels  5.51 us (12%)
  local copies, waits for them, and re-layouts  1.04 us (2%)
  between operations  0.74 us (2%)
    ppermute x2, starting transfers between devices, swap_along_x(): return (lax.ppermute(far, 'gx', across), lax.ppermute(near, 'gx', within))  7.83 us
    ppermute x1, starting transfers between devices, on_device(): from_below = lax.ppermute(up, 'gy', upward)  7.48 us
    ppermute x1, starting transfers between devices, on_device(): lax.ppermute(left, 'gx', [(target, source) for source, target in rightward])  7.26 us
    ppermute x1, waiting for transfers between devices, on_device(): lax.ppermute(down, 'gy', [(target, source) for source, target in upward])  4.93 us
    ppermute x2, waiting for transfers between devices, swap_along_x(): return (lax.ppermute(far, 'gx', across), lax.ppermute(near, 'gx', within))  3.2 us
    pallas_call x1, Pallas kernels, on_device(): pl.pallas_call(first_kernel, in_specs=[in_hbm] * 7, out_specs=[in_hbm] *...  2.1 us
    ppermute x1, starting transfers between devices, on_device(): from_left = lax.ppermute(right, 'gx', rightward)  1.92 us
    ppermute x1, starting transfers between devices, on_device(): lax.ppermute(down, 'gy', [(target, source) for source, target in upward])  1.92 us
  transfers between devices with their start and end apart: 6, of which 4 were waited for; matrix products, arithmetic and copies ran while one was open for 0% of the time, Pallas kernels for 0%

profile of v6, /device:TPU:26, one launch (start us, length us, event | category | flops | bytes accessed | tf_op | source)
XLA Modules:
  0.0 44.9 jit_solution(9162553975505478413)
XLA Ops:
  0.6 0.0 copy-start.2
  0.6 0.0 copy-start
  0.7 2.1 %collide_own.1 = (f32[64,16,128]{2,1,0:T(8,128)}, f32[2,16,128]{2,1,0:T(8,128)}, f32[2,16,128]{2,1,0:T(8,128)}) custom-call(f32[19,2,16,128]{3,2,1,0:T(8,128)} %flow.1, f32[7,2,16,128]{3,2,1,0:T(8,128)} %heat.1, f32[3,2,16,128]{3,2,1,0:T(8,128)} %flow_weight_in.1, f32[2,16,128]{2,1,0:T(8,128)} %heat_weight_in.1, f32[2,16,128]{2,1,0:T(8,128)} %resistance_in.1, ...), custom_call_target="tpu_custom_call" | custom-call | tf_op jit(solution)/shard_map/collide_own/pallas_call | solution.py:587
  2.8 7.5 %collective-permute-start = (f32[2,16,128]{2,1,0:T(8,128)}, f32[2,16,128]{2,1,0:T(8,128)S(1)}, u32[]{:S(2)}, u32[]{:S(2)}) collective-permute-start(f32[2,16,128]{2,1,0:T(8,128)} %get-tuple-element.16), channel_id=1, source_target_pairs={{0,1},{1,2},{2,3},{3,4},{4,5},{5,6},{6,7},{7,0},{8,9},{9,10},{10,1... | collective-permute-start | bytes 49160 | tf_op jit(solution)/shard_map/ppermute | solution.py:616
  10.2 1.9 %collective-permute-start.1 = (f32[2,16,128]{2,1,0:T(8,128)}, f32[2,16,128]{2,1,0:T(8,128)S(1)}, u32[]{:S(2)}, u32[]{:S(2)}) collective-permute-start(f32[2,16,128]{2,1,0:T(8,128)} %get-tuple-element.17), channel_id=1, source_target_pairs={{1,0},{2,1},{3,2},{4,3},{5,4},{6,5},{7,6},{0,7},{9,8},{10,9},{11,1... | collective-permute-start | bytes 49160 | tf_op jit(solution)/shard_map/ppermute | solution.py:617
  12.2 0.0 copy-start.1
  12.2 1.0 %copy-done.1 = f32[64,16,128]{2,1,0:T(8,128)S(1)} copy-done((f32[64,16,128]{2,1,0:T(8,128)S(1)}, f32[64,16,128]{2,1,0:T(8,128)}, u32[]{:S(2)}) %copy-start.1) | copy-done | bytes 524312
  13.2 0.0 collective-permute-done.from_below
  13.3 4.9 %collective-permute-done.1.from_above = f32[2,16,128]{2,1,0:T(8,128)S(1)} collective-permute-done((f32[2,16,128]{2,1,0:T(8,128)}, f32[2,16,128]{2,1,0:T(8,128)S(1)}, u32[]{:S(2)}, u32[]{:S(2)}) %collective-permute-start.1) | collective-permute-done | bytes 16416 | tf_op jit(solution)/shard_map/ppermute | solution.py:617
  18.2 0.3 halo_buffers.1
  18.5 5.9 %collective-permute-start.2 = (f32[29,16,128]{2,1,0:T(8,128)S(1)}, f32[29,16,128]{2,1,0:T(8,128)S(1)}, u32[]{:S(2)}, u32[]{:S(2)}) collective-permute-start(f32[29,16,128]{2,1,0:T(8,128)S(1)} %get-tuple-element.19), channel_id=1, source_target_pairs={{0,504},{8,16},{16,8},{24,32},{32,24},{40,48},{48,40},{56,64},{64,... | collective-permute-start | bytes 712712 | tf_op jit(solution)/shard_map/ppermute | solution.py:578
  24.5 1.9 %collective-permute-start.3 = (f32[29,16,128]{2,1,0:T(8,128)S(1)}, f32[29,16,128]{2,1,0:T(8,128)S(1)}, u32[]{:S(2)}, u32[]{:S(2)}) collective-permute-start(f32[29,16,128]{2,1,0:T(8,128)S(1)} %get-tuple-element.20), channel_id=1, source_target_pairs={{0,8},{8,0},{16,24},{24,16},{32,40},{40,32},{48,56},{56,48},{64,72... | collective-permute-start | bytes 712712 | tf_op jit(solution)/shard_map/ppermute | solution.py:578
  26.4 3.2 %collective-permute-done.2.from_far = f32[29,16,128]{2,1,0:T(8,128)S(1)} collective-permute-done((f32[29,16,128]{2,1,0:T(8,128)S(1)}, f32[29,16,128]{2,1,0:T(8,128)S(1)}, u32[]{:S(2)}, u32[]{:S(2)}) %collective-permute-start.2) | collective-permute-done | bytes 237600 | tf_op jit(solution)/shard_map/ppermute | solution.py:578
  29.6 0.0 collective-permute-done.3.from_near
  29.6 1.6 %forward_and_seed.1 = (f32[26,4,16,256]{3,2,1,0:T(8,128)S(1)}, f32[2,4,16,256]{3,2,1,0:T(8,128)S(1)}, f32[26,2,16,256]{3,2,1,0:T(8,128)S(1)}, f32[2,16,128]{2,1,...) custom-call(f32[64,16,128]{2,1,0:T(8,128)S(1)} %stage_own.1.own, ...), custom_call_target="tpu_custom_call" | custom-call | tf_op jit(solution)/shard_map/forward_and_seed/pallas_call | solution.py:637
  31.2 1.9 %collective-permute-start.4 = (f32[23,16,128]{2,1,0:T(8,128)S(1)}, f32[23,16,128]{2,1,0:T(8,128)S(1)}, u32[]{:S(2)}, u32[]{:S(2)}) collective-permute-start(f32[23,16,128]{2,1,0:T(8,128)S(1)} %get-tuple-element.26), channel_id=1, source_target_pairs={{0,8},{8,16},{16,24},{24,32},{32,40},{40,48},{48,56},{56,64},{64,7... | collective-permute-start | bytes 565256 | tf_op jit(solution)/shard_map/ppermute | solution.py:661
  33.1 7.3 %collective-permute-start.5 = (f32[23,16,128]{2,1,0:T(8,128)S(1)}, f32[23,16,128]{2,1,0:T(8,128)S(1)}, u32[]{:S(2)}, u32[]{:S(2)}) collective-permute-start(f32[23,16,128]{2,1,0:T(8,128)S(1)} %get-tuple-element.27), channel_id=1, source_target_pairs={{8,0},{16,8},{24,16},{32,24},{40,32},{48,40},{56,48},{64,56},{72,6... | collective-permute-start | bytes 565256 | tf_op jit(solution)/shard_map/ppermute | solution.py:662
  40.4 1.3 %collective-permute-done.4.from_left = f32[23,16,128]{2,1,0:T(8,128)S(1)} collective-permute-done((f32[23,16,128]{2,1,0:T(8,128)S(1)}, f32[23,16,128]{2,1,0:T(8,128)S(1)}, u32[]{:S(2)}, u32[]{:S(2)}) %collective-permute-start.4) | collective-permute-done | bytes 188448 | tf_op jit(solution)/shard_map/ppermute | solution.py:661
  41.7 1.8 %collective-permute-done.5.from_right = f32[23,16,128]{2,1,0:T(8,128)S(1)} collective-permute-done((f32[23,16,128]{2,1,0:T(8,128)S(1)}, f32[23,16,128]{2,1,0:T(8,128)S(1)}, u32[]{:S(2)}, u32[]{:S(2)}) %collective-permute-start.5) | collective-permute-done | bytes 188448 | tf_op jit(solution)/shard_map/ppermute | solution.py:662
  43.5 0.0 copy-done.2
  43.5 0.0 copy-done
  43.5 1.4 %adjoint_steps.1 = (f32[2,16,128]{2,1,0:T(8,128)}, f32[2,16,128]{2,1,0:T(8,128)}) custom-call(f32[19,2,16,128]{3,2,1,0:T(8,128)S(1)} %copy-done, f32[7,2,16,128]{3,2,1,0:T(8,128)S(1)} %copy-done.2, f32[26,4,16,256]{3,2,1,0:T(8,128)S(1)} %get-tuple-element.21.state, f32[2,4,16,256]{3,2,1,0:T(8,128)S(1)} %get-tuple-element.22.wide_sides, ...), custom_call_target="tpu_custom_call" | custom-call | tf_op jit(solution)/shard_map/adjoint_steps/pallas_call | solution.py:664
  (1 shorter events, 0.0 us)
Async XLA Ops:
  0.6 42.8 %copy-start.2 = (f32[7,2,16,128]{3,2,1,0:T(8,128)S(1)}, f32[7,2,16,128]{3,2,1,0:T(8,128)}, u32[]{:S(2)}) copy-start(f32[7,2,16,128]{3,2,1,0:T(8,128)} %heat.1) | copy-start | bytes 344068
  0.6 42.8 %copy-start = (f32[19,2,16,128]{3,2,1,0:T(8,128)S(1)}, f32[19,2,16,128]{3,2,1,0:T(8,128)}, u32[]{:S(2)}) copy-start(f32[19,2,16,128]{3,2,1,0:T(8,128)} %flow.1) | copy-start | bytes 933892
  2.8 10.5 %collective-permute-start = (f32[2,16,128]{2,1,0:T(8,128)}, f32[2,16,128]{2,1,0:T(8,128)S(1)}, u32[]{:S(2)}, u32[]{:S(2)}) collective-permute-start(f32[2,16,128]{2,1,0:T(8,128)} %get-tuple-element.16), channel_id=1, source_target_pairs={{0,1},{1,2},{2,3},{3,4},{4,5},{5,6},{6,7},{7,0},{8,9},{9,10},{10,1... | collective-permute-start | bytes 49160 | tf_op jit(solution)/shard_map/ppermute | solution.py:616
  10.2 8.0 %collective-permute-start.1 = (f32[2,16,128]{2,1,0:T(8,128)}, f32[2,16,128]{2,1,0:T(8,128)S(1)}, u32[]{:S(2)}, u32[]{:S(2)}) collective-permute-start(f32[2,16,128]{2,1,0:T(8,128)} %get-tuple-element.17), channel_id=1, source_target_pairs={{1,0},{2,1},{3,2},{4,3},{5,4},{6,5},{7,6},{0,7},{9,8},{10,9},{11,1... | collective-permute-start | bytes 49160 | tf_op jit(solution)/shard_map/ppermute | solution.py:617
  12.2 1.0 %copy-start.1 = (f32[64,16,128]{2,1,0:T(8,128)S(1)}, f32[64,16,128]{2,1,0:T(8,128)}, u32[]{:S(2)}) copy-start(f32[64,16,128]{2,1,0:T(8,128)} %get-tuple-element.15.own) | copy-start | bytes 1572868
  18.5 11.0 %collective-permute-start.2 = (f32[29,16,128]{2,1,0:T(8,128)S(1)}, f32[29,16,128]{2,1,0:T(8,128)S(1)}, u32[]{:S(2)}, u32[]{:S(2)}) collective-permute-start(f32[29,16,128]{2,1,0:T(8,128)S(1)} %get-tuple-element.19), channel_id=1, source_target_pairs={{0,504},{8,16},{16,8},{24,32},{32,24},{40,48},{48,40},{56,64},{64,... | collective-permute-start | bytes 712712 | tf_op jit(solution)/shard_map/ppermute | solution.py:578
  24.5 5.1 %collective-permute-start.3 = (f32[29,16,128]{2,1,0:T(8,128)S(1)}, f32[29,16,128]{2,1,0:T(8,128)S(1)}, u32[]{:S(2)}, u32[]{:S(2)}) collective-permute-start(f32[29,16,128]{2,1,0:T(8,128)S(1)} %get-tuple-element.20), channel_id=1, source_target_pairs={{0,8},{8,0},{16,24},{24,16},{32,40},{40,32},{48,56},{56,48},{64,72... | collective-permute-start | bytes 712712 | tf_op jit(solution)/shard_map/ppermute | solution.py:578
  31.2 10.5 %collective-permute-start.4 = (f32[23,16,128]{2,1,0:T(8,128)S(1)}, f32[23,16,128]{2,1,0:T(8,128)S(1)}, u32[]{:S(2)}, u32[]{:S(2)}) collective-permute-start(f32[23,16,128]{2,1,0:T(8,128)S(1)} %get-tuple-element.26), channel_id=1, source_target_pairs={{0,8},{8,16},{16,24},{24,32},{32,40},{40,48},{48,56},{56,64},{64,7... | collective-permute-start | bytes 565256 | tf_op jit(solution)/shard_map/ppermute | solution.py:661
  33.1 10.3 %collective-permute-start.5 = (f32[23,16,128]{2,1,0:T(8,128)S(1)}, f32[23,16,128]{2,1,0:T(8,128)S(1)}, u32[]{:S(2)}, u32[]{:S(2)}) collective-permute-start(f32[23,16,128]{2,1,0:T(8,128)S(1)} %get-tuple-element.27), channel_id=1, source_target_pairs={{8,0},{16,8},{24,16},{32,24},{40,32},{48,40},{56,48},{64,56},{72,6... | collective-permute-start | bytes 565256 | tf_op jit(solution)/shard_map/ppermute | solution.py:662

commit v7 on v6

--- a/solution.py
+++ b/solution.py
@@ -38,6 +38,13 @@
 LEFTWARD = [q for q in range(MEMBERS) if VELOCITY[q][0] == -1]
 LEVEL = [q for q in range(MEMBERS) if VELOCITY[q][0] == 0]
 
+
+def mirrored(q):
+    x, y, z = VELOCITY[q]
+    start = 0 if q < 19 else 19
+    return start + FLOW_VELOCITY.index((-x, y, z))
+
+
 MOBILITY, RATE, WEIGHT = MEMBERS, MEMBERS + 1, MEMBERS + 2
 FIELDS = MEMBERS + 6
 SIDE_FIELDS = list(range(MEMBERS, FIELDS))
@@ -54,11 +61,11 @@
     return {entry: row for row, entry in enumerate(entries)}
 
 
-TO_RIGHT = rows_of([(q, 0) for q in RIGHTWARD] + [(k, 1) for k in RIGHTWARD + SIDE_FIELDS + SUM_FIELDS])
-TO_LEFT = rows_of([(q, 1) for q in LEFTWARD] + [(k, 0) for k in LEFTWARD + SIDE_FIELDS + SUM_FIELDS])
-ADJ_TO_RIGHT = rows_of([(q, 0) for q in LEFTWARD] + [(k, 1) for k in LEFTWARD + SUM_FIELDS])
-ADJ_TO_LEFT = rows_of([(q, 1) for q in RIGHTWARD] + [(k, 0) for k in RIGHTWARD + SUM_FIELDS])
-BULK_ROWS, ADJ_BULK = len(TO_RIGHT), len(ADJ_TO_RIGHT)
+TO_NEAR = rows_of([(q, 0) for q in RIGHTWARD] + [(k, 1) for k in RIGHTWARD + SIDE_FIELDS + SUM_FIELDS])
+TO_FAR = rows_of([(q, 1) for q in LEFTWARD] + [(k, 0) for k in LEFTWARD + SIDE_FIELDS + SUM_FIELDS])
+ADJ_TO_NEAR = rows_of([(q, 0) for q in LEFTWARD] + [(k, 1) for k in LEFTWARD + SUM_FIELDS])
+ADJ_TO_FAR = rows_of([(q, 1) for q in RIGHTWARD] + [(k, 0) for k in RIGHTWARD + SUM_FIELDS])
+BULK_ROWS, ADJ_BULK = len(TO_NEAR), len(ADJ_TO_NEAR)
 
 
 def with_strips(bulk):
@@ -272,10 +279,12 @@
     return lax.broadcasted_iota(jnp.int32, (ZED, LANES), 1) % (2 * EDGE) < EDGE
 
 
-def either_way(move):
-    first = lax.rem(lax.axis_index("gx"), 2) == 0
-    pl.when(first)(lambda: move(True))
-    pl.when(jnp.logical_not(first))(lambda: move(False))
+def second_core():
+    return lax.rem(lax.axis_index("gx"), 2)
+
+
+def framed(q, odd):
+    return q + odd * (mirrored(q) - q)
 
 
 def copy_rows(target, source):
@@ -325,20 +334,11 @@
     return (buffer[place],) + beside(buffer[bulk + place // SLOTS], place % SLOTS)
 
 
-def send_out(far, near, right, left):
-    def send(first):
-        copy_rows(far, left if first else right)
-        copy_rows(near, right if first else left)
-
-    either_way(send)
-
-
-def take_in(from_left, from_right, from_far, from_near):
-    def receive(first):
-        copy_rows(from_left, from_far if first else from_near)
-        copy_rows(from_right, from_near if first else from_far)
-
-    either_way(receive)
+def given_state(flow, heat, odd, c, z):
+    i = c + odd * (1 - 2 * c)
+    return [flow[framed(q, odd), i, z, :] for q in range(19)] + [
+        heat[framed(q, odd) - 19, i, z, :] for q in range(19, MEMBERS)
+    ]
 
 
 def first_kernel(
@@ -360,13 +360,17 @@
         copy.start()
     for copy in copies:
         copy.wait()
+    odd = second_core()
+    sign = (1 - 2 * odd).astype(jnp.float32)
     for c in range(2):
+        i = c + odd * (1 - 2 * c)
         for z in halves():
-            mobility = jnp.where(solid[c, z, :] != 0, 0.0, 1.0 / (1.0 + resistance[c, z, :]))
-            rate = 1.0 / (0.5 + 0.4 * conductivity[c, z, :])
-            p = [flow[q, c, z, :] for q in range(19)] + [heat[q, c, z, :] for q in range(7)]
+            mobility = jnp.where(solid[i, z, :] != 0, 0.0, 1.0 / (1.0 + resistance[i, z, :]))
+            rate = 1.0 / (0.5 + 0.4 * conductivity[i, z, :])
+            p = given_state(flow, heat, odd, c, z)
             after = collide(p, level_sums(p), mobility, rate, range(MEMBERS))
-            more = [mobility, rate] + [flow_weight[k, c, z, :] for k in range(3)] + [heat_weight[c, z, :]]
+            more = [mobility, rate, sign * flow_weight[0, i, z, :]]
+            more += [flow_weight[1, i, z, :], flow_weight[2, i, z, :], heat_weight[i, z, :]]
             for k, value in enumerate([after[q] for q in range(MEMBERS)] + more):
                 own[own_row(k, c), z, :] = value
     copy_own = pltpu.make_async_copy(own, own_out, sent.at[0])
@@ -391,13 +395,13 @@
     copy_rows(staged, own)
 
 
-def halo_kernel(own, from_below, from_above, far, near, strip, right, left):
+def halo_kernel(own, from_below, from_above, far, near, strip):
     low = low_lanes()
     for k in range(HALF_ROWS):
         under, over = from_below[k], from_above[k]
         strip[k] = jnp.where(low, under, turn(over, EDGE, 1))
         strip[k + HALF_ROWS] = jnp.where(low, turn(under, -EDGE, 1), over)
-    for side, rows, c in ((right, TO_RIGHT, 1), (left, TO_LEFT, 0)):
+    for side, rows, c in ((near, TO_NEAR, 1), (far, TO_FAR, 0)):
         level = {q: moved(own_value(own, strip, q, c), VELOCITY[q], 1) for q in LEVEL}
         sums = [level_sums({q: level[q][t] for q in LEVEL}) for t in range(2)]
         parts = []
@@ -415,79 +419,128 @@
                 )
         for k, row in enumerate(pack_rows(parts)):
             side[BULK_ROWS + k] = row
-    send_out(far, near, right, left)
 
 
 def level_of(p, column, sums):
     return sums(p) if 0 <= column <= 1 else [p[q] for q in LEVEL[:SUMS]]
 
 
-def second_kernel(
-    own, strip, from_far, from_near,
-    state, wide_sides, adjoint, by_resistance, by_conductivity, right, left,
-    from_left, from_right, after, later, seed,
+def near_place(rows, k, column):
+    return rows[mirrored(k) if k < MEMBERS else k, 3 - column]
+
+
+def far_place(rows, k, column):
+    return rows[mirrored(k) if k < MEMBERS else k, -1 - column]
+
+
+def own_fed(q, column):
+    return 0 <= column <= 1 and 0 <= column - VELOCITY[q][0] <= 1
+
+
+def state_of(own_state, state, first, column, z, y):
+    return [
+        own_state[q, column, z, y] if own_fed(q, column) else state[q, column - first, z, y]
+        for q in range(MEMBERS)
+    ]
+
+
+def first_state(wide, column, state, sides, i):
+    put(sides, 0, i, moved(wide(MOBILITY, column), STILL, 1))
+    put(sides, 1, i, moved(wide(RATE, column), STILL, 1))
+    for q in range(MEMBERS):
+        if own_fed(q, column):
+            continue
+        if 0 <= column <= 1 or q not in LEVEL:
+            put(state, q, i, moved(wide(q, column - VELOCITY[q][0]), VELOCITY[q], 1))
+        elif q in LEVEL[:SUMS]:
+            put(state, q, i, moved(wide(SUM_FIELDS[LEVEL.index(q)], column), STILL, 1))
+
+
+def first_collision(column, own_state, state, sides, after, first):
+    i = column - first
+    wanted = [q for q in range(MEMBERS) if 0 <= column + VELOCITY[q][0] <= 1]
+    for z, y in tiles(WIDE):
+        p = state_of(own_state, state, first, column, z, y)
+        level = level_of(p, column, level_sums)
+        result = collide(p, level, sides[0, i, z, y], sides[1, i, z, y], wanted)
+        for q in wanted:
+            after[q, i, z, y] = result[q]
+
+
+def seeds(wide, column, seed):
+    weights = [wide(WEIGHT + k, column) for k in range(3)]
+    weights = [(main, turn(extra, by, 1)) for main, extra, by in weights]
+    if not 0 <= column <= 1:
+        weights[0] = tuple(-value for value in weights[0])
+    for q in range(1, MEMBERS):
+        velocity = VELOCITY[q]
+        c = column - velocity[0]
+        if not 0 <= c <= 1:
+            continue
+        if q < 19:
+            parts = [
+                tuple(value if velocity[k] > 0 else -value for value in weights[k]) for k in range(3) if velocity[k]
+            ]
+            pair = parts[0] if len(parts) == 1 else tuple(a + b for a, b in zip(*parts))
+            pair += (0,)
+        else:
+            pair = wide(WEIGHT + 3, column)
+        put(seed, q, c, moved(pair, velocity, -1))
+
+
+def own_step_kernel(own, strip, own_state, own_seed):
+    def wide(k, column):
+        return own_value(own, strip, k, column)
+
+    for column in (0, 1):
+        for q in range(MEMBERS):
+            if own_fed(q, column):
+                put(own_state, q, column, moved(wide(q, column - VELOCITY[q][0]), VELOCITY[q], 1))
+        seeds(wide, column, own_seed)
+
+
+def step_kernel(
+    own, strip, own_state, own_seed, from_far, from_near,
+    far_state, far_sides, near_state, near_sides, adjoint, by_resistance, by_conductivity, far, near,
+    after, near_after, later, halo_seed,
 ):
-    take_in(from_left, from_right, from_far, from_near)
-
     def wide(k, column):
         if column < 0:
-            return halo_value(from_left, BULK_ROWS, TO_RIGHT[k, column + 2])
+            return halo_value(from_far, BULK_ROWS, far_place(TO_FAR, k, column))
         if column > 1:
-            return halo_value(from_right, BULK_ROWS, TO_LEFT[k, column - 2])
+            return halo_value(from_near, BULK_ROWS, near_place(TO_NEAR, k, column))
         return own_value(own, strip, k, column)
 
-    for column in range(-1, 3):
-        i = column + 1
-        put(wide_sides, 0, i, moved(wide(MOBILITY, column), STILL, 1))
-        put(wide_sides, 1, i, moved(wide(RATE, column), STILL, 1))
-        for q in range(MEMBERS):
-            if 0 <= column <= 1 or q not in LEVEL:
-                put(state, q, i, moved(wide(q, column - VELOCITY[q][0]), VELOCITY[q], 1))
-            elif q in LEVEL[:SUMS]:
-                put(state, q, i, moved(wide(SUM_FIELDS[LEVEL.index(q)], column), STILL, 1))
-    for column in range(-1, 3):
-        i = column + 1
-        wanted = [q for q in range(MEMBERS) if 0 <= column + VELOCITY[q][0] <= 1]
-        for z, y in tiles(WIDE):
-            p = [state[q, i, z, y] for q in range(MEMBERS)]
-            level = level_of(p, column, level_sums)
-            result = collide(p, level, wide_sides[0, i, z, y], wide_sides[1, i, z, y], wanted)
-            for q in wanted:
-                after[q, i, z, y] = result[q]
+    for column in (-1, 0):
+        first_state(wide, column, far_state, far_sides, column + 1)
+        first_collision(column, own_state, far_state, far_sides, after, -1)
+    for column in (1, 2):
+        first_state(wide, column, near_state, near_sides, column - 1)
+        first_collision(column, own_state, near_state, near_sides, near_after, 1)
+    for column in (-1, 2):
+        seeds(wide, column, halo_seed)
     for c in range(2):
         for q in range(MEMBERS):
-            put(later, q, c, moved(split(after[q, c + 1 - VELOCITY[q][0]]), VELOCITY[q], 1))
-    for column in range(-1, 3):
-        weights = [wide(WEIGHT + k, column) for k in range(3)]
-        weights = [(main, turn(extra, by, 1)) for main, extra, by in weights]
-        for q in range(1, MEMBERS):
-            velocity = VELOCITY[q]
-            c = column - velocity[0]
-            if not 0 <= c <= 1:
-                continue
-            if q < 19:
-                parts = [
-                    tuple(value if velocity[k] > 0 else -value for value in weights[k]) for k in range(3) if velocity[k]
-                ]
-                pair = parts[0] if len(parts) == 1 else tuple(a + b for a, b in zip(*parts))
-                pair += (0,)
-            else:
-                pair = wide(WEIGHT + 3, column)
-            put(seed, q, c, moved(pair, velocity, -1))
+            column = c - VELOCITY[q][0]
+            source = near_after[q, column - 1] if column >= 1 else after[q, column + 1]
+            put(later, q, c, moved(split(source), VELOCITY[q], 1))
     for c in range(2):
         for z, y in tiles(WIDE):
             p = [later[q, c, z, y] for q in range(MEMBERS)]
-            pa = [jnp.zeros((8, LANES), jnp.float32)] + [seed[q, c, z, y] for q in range(1, MEMBERS)]
+            pa = [jnp.zeros((8, LANES), jnp.float32)]
+            pa += [
+                (own_seed if 0 <= c + VELOCITY[q][0] <= 1 else halo_seed)[q, c, z, y] for q in range(1, MEMBERS)
+            ]
             inner = y.start == 0
+            mobility, rate = [near_sides[k, 0, z, y] if c else far_sides[k, 1, z, y] for k in range(2)]
             result = pull_back(
-                p, level_sums(p), pa, level_adjoint_sums(pa),
-                wide_sides[0, c + 1, z, y], wide_sides[1, c + 1, z, y], range(MEMBERS), inner,
+                p, level_sums(p), pa, level_adjoint_sums(pa), mobility, rate, range(MEMBERS), inner
             )
             if inner:
                 by_resistance[c, z, :], by_conductivity[c, z, :] = result["by"]
             for q in range(MEMBERS):
                 adjoint[q, c, z, y] = result[q]
-    for side, rows, c in ((right, ADJ_TO_RIGHT, 1), (left, ADJ_TO_LEFT, 0)):
+    for side, rows, c in ((near, ADJ_TO_NEAR, 1), (far, ADJ_TO_FAR, 0)):
         level = {q: moved(split(adjoint[q, c]), VELOCITY[q], -1) for q in LEVEL}
         sums = [level_adjoint_sums({q: level[q][t] for q in LEVEL}) for t in range(2)]
         parts = []
@@ -502,65 +555,88 @@
             side[ADJ_BULK + k] = row
 
 
-def third_kernel(
-    flow, heat, state, wide_sides, adjoint, part_resistance, part_conductivity, from_left, from_right,
-    by_resistance, by_conductivity,
-    arrived, earlier, last,
+def adjoint_step(wide, column, own_state, state, sides, arrived, earlier, first, keep):
+    own = 0 <= column <= 1
+    i = column - first
+    for q in range(MEMBERS):
+        if own or q not in LEVEL:
+            put(arrived, q, i, moved(wide(q, column + VELOCITY[q][0]), VELOCITY[q], -1))
+        elif q in LEVEL[:SUMS]:
+            put(arrived, q, i, moved(wide(SUM_FIELDS[LEVEL.index(q)], column), STILL, 1))
+    for z, y in tiles(WIDE):
+        inner = y.start == 0
+        wanted = [
+            q for q in range(MEMBERS) if 0 <= column - VELOCITY[q][0] <= 1 and (inner or VELOCITY[q][1])
+        ]
+        p = state_of(own_state, state, first, column, z, y)
+        pa = [arrived[q, i, z, y] for q in range(MEMBERS)]
+        result = pull_back(
+            p, level_of(p, column, level_sums), pa, level_of(pa, column, level_adjoint_sums),
+            sides[0, i, z, y], sides[1, i, z, y], wanted, inner and own,
+        )
+        for q in wanted:
+            earlier[q, i, z, y] = result[q]
+        if inner and own:
+            keep(z, *result["by"])
+
+
+def far_adjoint_kernel(
+    own_state, state, sides, adjoint, part_resistance, part_conductivity, from_far,
+    earlier, by_resistance, by_conductivity,
+    arrived,
 ):
     def wide(k, column):
         if column < 0:
-            return halo_value(from_left, ADJ_BULK, ADJ_TO_RIGHT[k, column + 2])
+            return halo_value(from_far, ADJ_BULK, far_place(ADJ_TO_FAR, k, column))
+        return split(adjoint[k, column])
+
+    def keep(z, resistance, conductivity):
+        by_resistance[0, z, :] = part_resistance[0, z, :] + resistance
+        by_conductivity[0, z, :] = part_conductivity[0, z, :] + conductivity
+
+    for column in (-1, 0):
+        adjoint_step(wide, column, own_state, state, sides, arrived, earlier, -1, keep)
+    by_resistance[1] = part_resistance[1]
+    by_conductivity[1] = part_conductivity[1]
+
+
+def near_adjoint_kernel(
+    flow, heat, own_state, state, sides, far_sides, adjoint, far_earlier, part_resistance, part_conductivity, from_near,
+    by_resistance, by_conductivity,
+    arrived, earlier, last, sums,
+):
+    def wide(k, column):
         if column > 1:
-            return halo_value(from_right, ADJ_BULK, ADJ_TO_LEFT[k, column - 2])
+            return halo_value(from_near, ADJ_BULK, near_place(ADJ_TO_NEAR, k, column))
         return split(adjoint[k, column])
 
-    for column in range(-1, 3):
-        i = column + 1
-        for q in range(MEMBERS):
-            if 0 <= column <= 1 or q not in LEVEL:
-                put(arrived, q, i, moved(wide(q, column + VELOCITY[q][0]), VELOCITY[q], -1))
-            elif q in LEVEL[:SUMS]:
-                put(arrived, q, i, moved(wide(SUM_FIELDS[LEVEL.index(q)], column), STILL, 1))
-    for column in range(-1, 3):
-        i = column + 1
-        own = 0 <= column <= 1
-        for z, y in tiles(WIDE):
-            inner = y.start == 0
-            wanted = [
-                q
-                for q in range(MEMBERS)
-                if 0 <= column - VELOCITY[q][0] <= 1 and (inner or VELOCITY[q][1])
-            ]
-            p = [state[q, i, z, y] for q in range(MEMBERS)]
-            pa = [arrived[q, i, z, y] for q in range(MEMBERS)]
-            result = pull_back(
-                p, level_of(p, column, level_sums), pa, level_of(pa, column, level_adjoint_sums),
-                wide_sides[0, i, z, y], wide_sides[1, i, z, y], wanted, inner and own,
-            )
-            for q in wanted:
-                earlier[q, i, z, y] = result[q]
-            if inner and own:
-                by_resistance[column, z, :] = part_resistance[column, z, :] + result["by"][0]
-                by_conductivity[column, z, :] = part_conductivity[column, z, :] + result["by"][1]
+    def keep(z, resistance, conductivity):
+        sums[0, z, :] = part_resistance[1, z, :] + resistance
+        sums[1, z, :] = part_conductivity[1, z, :] + conductivity
+
+    for column in (1, 2):
+        adjoint_step(wide, column, own_state, state, sides, arrived, earlier, 1, keep)
     for c in range(2):
         for q in range(MEMBERS):
             velocity = VELOCITY[q]
-            i = c + 1 + velocity[0]
+            column = c + velocity[0]
+            source, i = (earlier, column - 1) if column >= 1 else (far_earlier, column + 1)
             if velocity[1]:
-                last[q, c] = moved(split(earlier[q, i]), velocity, -1)[0]
+                last[q, c] = moved(split(source[q, i]), velocity, -1)[0]
             else:
-                last[q, c] = turn(earlier[q, i, :, :LANES], -velocity[2], 0)
+                last[q, c] = turn(source[q, i, :, :LANES], -velocity[2], 0)
     narrow = pl.ds(0, LANES)
+    odd = second_core()
     for c in range(2):
+        i = c + odd * (1 - 2 * c)
         for z in halves():
-            p = [flow[q, c, z, :] for q in range(19)] + [heat[q, c, z, :] for q in range(7)]
+            p = given_state(flow, heat, odd, c, z)
             pa = [last[q, c, z, :] for q in range(MEMBERS)]
-            result = pull_back(
-                p, level_sums(p), pa, level_adjoint_sums(pa),
-                wide_sides[0, c + 1, z, narrow], wide_sides[1, c + 1, z, narrow], (), True,
-            )
-            by_resistance[c, z, :] += result["by"][0]
-            by_conductivity[c, z, :] += result["by"][1]
+            mobility, rate = [(sides[k, 0, z, narrow] if c else far_sides[k, 1, z, narrow]) for k in range(2)]
+            result = pull_back(p, level_sums(p), pa, level_adjoint_sums(pa), mobility, rate, (), True)
+            resistance, conductivity = result["by"]
+            by_resistance[i, z, :] = resistance + (sums[0, z, :] if c else part_resistance[0, z, :])
+            by_conductivity[i, z, :] = conductivity + (sums[1, z, :] if c else part_conductivity[0, z, :])
 
 
 def floats(*shape):
@@ -627,51 +703,60 @@
     far, near, strip = pl.pallas_call(
         halo_kernel,
         out_shape=(floats(SENT, ZED, LANES), floats(SENT, ZED, LANES), floats(STRIP_ROWS, ZED, LANES)),
-        scratch_shapes=[vmem(SENT, ZED, LANES), vmem(SENT, ZED, LANES)],
         compiler_params=PARAMS,
         name="halo_buffers",
     )(own, from_below, from_above)
 
     from_far, from_near = swap_along_x(far, near)
 
-    state, wide_sides, adjoint, part_resistance, part_conductivity, right, left = pl.pallas_call(
-        second_kernel,
-        out_shape=(
-            floats(MEMBERS, 4, ZED, WIDE),
-            floats(2, 4, ZED, WIDE),
-            floats(MEMBERS, 2, ZED, WIDE),
-            floats(2, ZED, LANES),
-            floats(2, ZED, LANES),
-            floats(ADJ_SENT, ZED, LANES),
-            floats(ADJ_SENT, ZED, LANES),
-        ),
-        scratch_shapes=[
-            vmem(SENT, ZED, LANES),
-            vmem(SENT, ZED, LANES),
-            vmem(MEMBERS, 4, ZED, WIDE),
-            vmem(MEMBERS, 2, ZED, WIDE),
-            vmem(MEMBERS, 2, ZED, WIDE),
-        ],
+    columns = floats(MEMBERS, 2, ZED, WIDE)
+    side_columns = floats(2, 2, ZED, WIDE)
+    cells = floats(2, ZED, LANES)
+    held = vmem(MEMBERS, 2, ZED, WIDE)
+    busy = pl.CostEstimate(flops=10**7, bytes_accessed=10**6, transcendentals=0)
+
+    own_state, own_seed = pl.pallas_call(
+        own_step_kernel,
+        out_shape=(columns, columns),
         compiler_params=PARAMS,
-        name="forward_and_seed",
-    )(own, strip, from_far, from_near)
-
-    count = lax.axis_size("gx")
-    rightward = [(i, (i + 1) % count) for i in range(count)]
-    from_left = lax.ppermute(right, "gx", rightward)
-    from_right = lax.ppermute(left, "gx", [(target, source) for source, target in rightward])
+        cost_estimate=busy,
+        name="own_step",
+    )(own, strip)
+
+    far_state, far_sides, near_state, near_sides, adjoint, part_resistance, part_conductivity, far, near = (
+        pl.pallas_call(
+            step_kernel,
+            out_shape=(
+                columns, side_columns, columns, side_columns, columns, cells, cells,
+                floats(ADJ_SENT, ZED, LANES), floats(ADJ_SENT, ZED, LANES),
+            ),
+            scratch_shapes=[held, held, held, held],
+            compiler_params=PARAMS,
+            name="two_steps",
+        )(own, strip, own_state, own_seed, from_far, from_near)
+    )
+
+    from_far, from_near = swap_along_x(far, near)
+
+    far_earlier, part_resistance, part_conductivity = pl.pallas_call(
+        far_adjoint_kernel,
+        out_shape=(columns, cells, cells),
+        scratch_shapes=[held],
+        compiler_params=PARAMS,
+        cost_estimate=busy,
+        name="far_adjoint",
+    )(own_state, far_state, far_sides, adjoint, part_resistance, part_conductivity, from_far)
 
     return pl.pallas_call(
-        third_kernel,
-        out_shape=(floats(2, ZED, LANES), floats(2, ZED, LANES)),
-        scratch_shapes=[
-            vmem(MEMBERS, 4, ZED, WIDE),
-            vmem(MEMBERS, 4, ZED, WIDE),
-            vmem(MEMBERS, 2, ZED, LANES),
-        ],
+        near_adjoint_kernel,
+        out_shape=(cells, cells),
+        scratch_shapes=[held, held, vmem(MEMBERS, 2, ZED, LANES), vmem(2, ZED, LANES)],
         compiler_params=PARAMS,
-        name="adjoint_steps",
-    )(flow, heat, state, wide_sides, adjoint, part_resistance, part_conductivity, from_left, from_right)
+        name="near_adjoint",
+    )(
+        flow, heat, own_state, near_state, near_sides, far_sides, adjoint, far_earlier,
+        part_resistance, part_conductivity, from_near,
+    )
 
 
 def solution(mesh):

time: 45.2 us -> 43.8 us (0.969)
  starting transfers between devices: 26.4 us -> 25 us
  waiting for transfers between devices: 11.2 us -> 10.4 us
  local copies, waits for them, and re-layouts: 1.04 us -> 1.64 us
    ppermute x2 -> x0, starting transfers between devices: 9.18 us -> none  [the longest x1 7.26 us: on_device(): lax.ppermute(left, 'gx', [(target, source) for source, target in rightward])]
    ppermute x2 -> x4, starting transfers between devices: 7.83 us -> 15.6 us  [swap_along_x(): return (lax.ppermute(far, 'gx', across), lax.ppermute(near, 'gx', within))]
    ppermute x2 -> x0, waiting for transfers between devices: 3.08 us -> none  [the longest x1 1.76 us: on_device(): lax.ppermute(left, 'gx', [(target, source) for source, target in rightward])]
    ppermute x2 -> x4, waiting for transfers between devices: 3.2 us -> 5.48 us  [swap_along_x(): return (lax.ppermute(far, 'gx', across), lax.ppermute(near, 'gx', within))]
    unnamed x6, local copies, waits for them, and re-layouts: 1.04 us -> 1.64 us
    pallas_call x2 -> x4, Pallas kernels: 3.05 us -> 3.18 us  [the longest x1 1.3 us: on_device(): pl.pallas_call(step_kernel, out_shape=(columns, side_columns, columns, si...]
  transfers between devices with their start and end apart: 6 -> 6, of which waited for: 4 -> 3; matrix products, arithmetic and copies ran while one was open for 0% -> 0% of each run, Pallas kernels for 0% -> 2%
where the time goes in v7:
time: 43.8 us; the launch traced here: 43.4 us
  starting transfers between devices  25 us (57%)
  waiting for transfers between devices  10.4 us (24%)
  Pallas kernels  5.6 us (13%)
  local copies, waits for them, and re-layouts  1.64 us (4%)
  between operations  0.74 us (2%)
    ppermute x4, starting transfers between devices, swap_along_x(): return (lax.ppermute(far, 'gx', across), lax.ppermute(near, 'gx', within))  15.6 us
    ppermute x1, starting transfers between devices, on_device(): from_below = lax.ppermute(up, 'gy', upward)  7.48 us
    ppermute x4, waiting for transfers between devices, swap_along_x(): return (lax.ppermute(far, 'gx', across), lax.ppermute(near, 'gx', within))  5.48 us
    ppermute x1, waiting for transfers between devices, on_device(): lax.ppermute(down, 'gy', [(target, source) for source, target in upward])  4.93 us
    pallas_call x1, Pallas kernels, on_device(): pl.pallas_call(first_kernel, in_specs=[in_hbm] * 7, out_specs=[in_hbm] *...  2.06 us
    ppermute x1, starting transfers between devices, on_device(): lax.ppermute(down, 'gy', [(target, source) for source, target in upward])  1.92 us
    unnamed x6, local copies, waits for them, and re-layouts  1.64 us
    pallas_call x1, Pallas kernels, on_device(): pl.pallas_call(step_kernel, out_shape=(columns, side_columns, columns, si...  1.3 us
  transfers between devices with their start and end apart: 6, of which 3 were waited for; matrix products, arithmetic and copies ran while one was open for 0% of the time, Pallas kernels for 2%

profile of v7, /device:TPU:26, one launch (start us, length us, event | category | flops | bytes accessed | tf_op | source)
XLA Modules:
  0.0 43.4 jit_solution(12046106108122164922)
XLA Ops:
  0.6 2.1 %collide_own.1 = (f32[64,16,128]{2,1,0:T(8,128)}, f32[2,16,128]{2,1,0:T(8,128)}, f32[2,16,128]{2,1,0:T(8,128)}) custom-call(f32[19,2,16,128]{3,2,1,0:T(8,128)} %flow.1, f32[7,2,16,128]{3,2,1,0:T(8,128)} %heat.1, f32[3,2,16,128]{3,2,1,0:T(8,128)} %flow_weight_in.1, f32[2,16,128]{2,1,0:T(8,128)} %heat_weight_in.1, f32[2,16,128]{2,1,0:T(8,128)} %resistance_in.1, ...), custom_call_target="tpu_custom_call" | custom-call | tf_op jit(solution)/shard_map/collide_own/pallas_call | solution.py:663
  2.7 7.5 %collective-permute-start = (f32[2,16,128]{2,1,0:T(8,128)}, f32[2,16,128]{2,1,0:T(8,128)S(1)}, u32[]{:S(2)}, u32[]{:S(2)}) collective-permute-start(f32[2,16,128]{2,1,0:T(8,128)} %get-tuple-element.23), channel_id=1, source_target_pairs={{0,1},{1,2},{2,3},{3,4},{4,5},{5,6},{6,7},{7,0},{8,9},{9,10},{10,1... | collective-permute-start | bytes 49160 | tf_op jit(solution)/shard_map/ppermute | solution.py:692
  10.2 1.9 %collective-permute-start.1 = (f32[2,16,128]{2,1,0:T(8,128)}, f32[2,16,128]{2,1,0:T(8,128)S(1)}, u32[]{:S(2)}, u32[]{:S(2)}) collective-permute-start(f32[2,16,128]{2,1,0:T(8,128)} %get-tuple-element.24), channel_id=1, source_target_pairs={{1,0},{2,1},{3,2},{4,3},{5,4},{6,5},{7,6},{0,7},{9,8},{10,9},{11,1... | collective-permute-start | bytes 49160 | tf_op jit(solution)/shard_map/ppermute | solution.py:693
  12.1 0.0 copy-start.1
  12.1 1.0 %copy-done.1 = f32[64,16,128]{2,1,0:T(8,128)S(1)} copy-done((f32[64,16,128]{2,1,0:T(8,128)S(1)}, f32[64,16,128]{2,1,0:T(8,128)}, u32[]{:S(2)}) %copy-start.1) | copy-done | bytes 524312
  13.2 0.0 collective-permute-done.from_below
  13.2 4.9 %collective-permute-done.1.from_above = f32[2,16,128]{2,1,0:T(8,128)S(1)} collective-permute-done((f32[2,16,128]{2,1,0:T(8,128)}, f32[2,16,128]{2,1,0:T(8,128)S(1)}, u32[]{:S(2)}, u32[]{:S(2)}) %collective-permute-start.1) | collective-permute-done | bytes 16416 | tf_op jit(solution)/shard_map/ppermute | solution.py:693
  18.1 0.3 halo_buffers.1
  18.5 5.9 %collective-permute-start.2 = (f32[29,16,128]{2,1,0:T(8,128)S(1)}, f32[29,16,128]{2,1,0:T(8,128)S(1)}, u32[]{:S(2)}, u32[]{:S(2)}) collective-permute-start(f32[29,16,128]{2,1,0:T(8,128)S(1)} %get-tuple-element.28), channel_id=1, source_target_pairs={{0,504},{8,16},{16,8},{24,32},{32,24},{40,48},{48,40},{56,64},{64,... | collective-permute-start | bytes 712712 | tf_op jit(solution)/shard_map/ppermute | solution.py:654
  24.4 1.9 %collective-permute-start.3 = (f32[29,16,128]{2,1,0:T(8,128)S(1)}, f32[29,16,128]{2,1,0:T(8,128)S(1)}, u32[]{:S(2)}, u32[]{:S(2)}) collective-permute-start(f32[29,16,128]{2,1,0:T(8,128)S(1)} %get-tuple-element.29), channel_id=1, source_target_pairs={{0,8},{8,0},{16,24},{24,16},{32,40},{40,32},{48,56},{56,48},{64,72... | collective-permute-start | bytes 712712 | tf_op jit(solution)/shard_map/ppermute | solution.py:654
  26.3 0.4 own_step.1
  26.7 2.8 %collective-permute-done.2.from_far = f32[29,16,128]{2,1,0:T(8,128)S(1)} collective-permute-done((f32[29,16,128]{2,1,0:T(8,128)S(1)}, f32[29,16,128]{2,1,0:T(8,128)S(1)}, u32[]{:S(2)}, u32[]{:S(2)}) %collective-permute-start.2) | collective-permute-done | bytes 237600 | tf_op jit(solution)/shard_map/ppermute | solution.py:654
  29.5 0.0 collective-permute-done.3.from_near
  29.5 1.3 %two_steps.1 = (f32[26,2,16,256]{3,2,1,0:T(8,128)S(1)}, f32[2,2,16,256]{3,2,1,0:T(8,128)S(1)}, f32[26,2,16,256]{3,2,1,0:T(8,128)S(1)}, f32[2,2,16,256]{3,2,1,0:T...) custom-call(f32[64,16,128]{2,1,0:T(8,128)S(1)} %stage_own.1.own, ...), custom_call_target="tpu_custom_call" | custom-call | tf_op jit(solution)/shard_map/two_steps/pallas_call | solution.py:727
  30.8 5.9 %collective-permute-start.4 = (f32[23,16,128]{2,1,0:T(8,128)S(1)}, f32[23,16,128]{2,1,0:T(8,128)S(1)}, u32[]{:S(2)}, u32[]{:S(2)}) collective-permute-start(f32[23,16,128]{2,1,0:T(8,128)S(1)} %get-tuple-element.37), channel_id=1, source_target_pairs={{0,504},{8,16},{16,8},{24,32},{32,24},{40,48},{48,40},{56,64},{64,... | collective-permute-start | bytes 565256 | tf_op jit(solution)/shard_map/ppermute | solution.py:654
  36.7 1.9 %collective-permute-start.5 = (f32[23,16,128]{2,1,0:T(8,128)S(1)}, f32[23,16,128]{2,1,0:T(8,128)S(1)}, u32[]{:S(2)}, u32[]{:S(2)}) collective-permute-start(f32[23,16,128]{2,1,0:T(8,128)S(1)} %get-tuple-element.41), channel_id=1, source_target_pairs={{0,8},{8,0},{16,24},{24,16},{32,40},{40,32},{48,56},{56,48},{64,72... | collective-permute-start | bytes 565256 | tf_op jit(solution)/shard_map/ppermute | solution.py:654
  38.6 2.7 %collective-permute-done.4.from_far = f32[23,16,128]{2,1,0:T(8,128)S(1)} collective-permute-done((f32[23,16,128]{2,1,0:T(8,128)S(1)}, f32[23,16,128]{2,1,0:T(8,128)S(1)}, u32[]{:S(2)}, u32[]{:S(2)}) %collective-permute-start.4) | collective-permute-done | bytes 188448 | tf_op jit(solution)/shard_map/ppermute | solution.py:654
  41.3 0.0 copy-start
  41.3 0.0 copy-start.2
  41.3 0.4 far_adjoint.1
  41.7 0.0 collective-permute-done.5.from_near
  41.7 0.6 %copy-done = f32[19,2,16,128]{3,2,1,0:T(8,128)S(1)} copy-done((f32[19,2,16,128]{3,2,1,0:T(8,128)S(1)}, f32[19,2,16,128]{3,2,1,0:T(8,128)}, u32[]{:S(2)}) %copy-start) | copy-done | bytes 311320
  42.3 0.0 copy-done.2
  42.3 1.1 %near_adjoint.1 = (f32[2,16,128]{2,1,0:T(8,128)}, f32[2,16,128]{2,1,0:T(8,128)}) custom-call(f32[19,2,16,128]{3,2,1,0:T(8,128)S(1)} %copy-done, f32[7,2,16,128]{3,2,1,0:T(8,128)S(1)} %copy-done.2, f32[26,2,16,256]{3,2,1,0:T(8,128)S(1)} %get-tuple-element.26.own_state, f32[26,2,16,256]{3,2,1,0:T(8,128)S(1)} %get-tuple-element.30.state, ...), custom_call_target="tpu_custom_call" | custom-call | tf_op jit(solution)/shard_map/near_adjoint/pallas_call | solution.py:750
  (1 shorter events, 0.0 us)
Async XLA Ops:
  2.7 10.5 %collective-permute-start = (f32[2,16,128]{2,1,0:T(8,128)}, f32[2,16,128]{2,1,0:T(8,128)S(1)}, u32[]{:S(2)}, u32[]{:S(2)}) collective-permute-start(f32[2,16,128]{2,1,0:T(8,128)} %get-tuple-element.23), channel_id=1, source_target_pairs={{0,1},{1,2},{2,3},{3,4},{4,5},{5,6},{6,7},{7,0},{8,9},{9,10},{10,1... | collective-permute-start | bytes 49160 | tf_op jit(solution)/shard_map/ppermute | solution.py:692
  10.2 8.0 %collective-permute-start.1 = (f32[2,16,128]{2,1,0:T(8,128)}, f32[2,16,128]{2,1,0:T(8,128)S(1)}, u32[]{:S(2)}, u32[]{:S(2)}) collective-permute-start(f32[2,16,128]{2,1,0:T(8,128)} %get-tuple-element.24), channel_id=1, source_target_pairs={{1,0},{2,1},{3,2},{4,3},{5,4},{6,5},{7,6},{0,7},{9,8},{10,9},{11,1... | collective-permute-start | bytes 49160 | tf_op jit(solution)/shard_map/ppermute | solution.py:693
  12.1 1.0 %copy-start.1 = (f32[64,16,128]{2,1,0:T(8,128)S(1)}, f32[64,16,128]{2,1,0:T(8,128)}, u32[]{:S(2)}) copy-start(f32[64,16,128]{2,1,0:T(8,128)} %get-tuple-element.22.own) | copy-start | bytes 1572868
  18.5 11.0 %collective-permute-start.2 = (f32[29,16,128]{2,1,0:T(8,128)S(1)}, f32[29,16,128]{2,1,0:T(8,128)S(1)}, u32[]{:S(2)}, u32[]{:S(2)}) collective-permute-start(f32[29,16,128]{2,1,0:T(8,128)S(1)} %get-tuple-element.28), channel_id=1, source_target_pairs={{0,504},{8,16},{16,8},{24,32},{32,24},{40,48},{48,40},{56,64},{64,... | collective-permute-start | bytes 712712 | tf_op jit(solution)/shard_map/ppermute | solution.py:654
  24.4 5.1 %collective-permute-start.3 = (f32[29,16,128]{2,1,0:T(8,128)S(1)}, f32[29,16,128]{2,1,0:T(8,128)S(1)}, u32[]{:S(2)}, u32[]{:S(2)}) collective-permute-start(f32[29,16,128]{2,1,0:T(8,128)S(1)} %get-tuple-element.29), channel_id=1, source_target_pairs={{0,8},{8,0},{16,24},{24,16},{32,40},{40,32},{48,56},{56,48},{64,72... | collective-permute-start | bytes 712712 | tf_op jit(solution)/shard_map/ppermute | solution.py:654
  30.8 10.5 %collective-permute-start.4 = (f32[23,16,128]{2,1,0:T(8,128)S(1)}, f32[23,16,128]{2,1,0:T(8,128)S(1)}, u32[]{:S(2)}, u32[]{:S(2)}) collective-permute-start(f32[23,16,128]{2,1,0:T(8,128)S(1)} %get-tuple-element.37), channel_id=1, source_target_pairs={{0,504},{8,16},{16,8},{24,32},{32,24},{40,48},{48,40},{56,64},{64,... | collective-permute-start | bytes 565256 | tf_op jit(solution)/shard_map/ppermute | solution.py:654
  36.7 5.0 %collective-permute-start.5 = (f32[23,16,128]{2,1,0:T(8,128)S(1)}, f32[23,16,128]{2,1,0:T(8,128)S(1)}, u32[]{:S(2)}, u32[]{:S(2)}) collective-permute-start(f32[23,16,128]{2,1,0:T(8,128)S(1)} %get-tuple-element.41), channel_id=1, source_target_pairs={{0,8},{8,0},{16,24},{24,16},{32,40},{40,32},{48,56},{56,48},{64,72... | collective-permute-start | bytes 565256 | tf_op jit(solution)/shard_map/ppermute | solution.py:654
  41.3 1.0 %copy-start = (f32[19,2,16,128]{3,2,1,0:T(8,128)S(1)}, f32[19,2,16,128]{3,2,1,0:T(8,128)}, u32[]{:S(2)}) copy-start(f32[19,2,16,128]{3,2,1,0:T(8,128)} %flow.1) | copy-start | bytes 933892
  41.3 1.0 %copy-start.2 = (f32[7,2,16,128]{3,2,1,0:T(8,128)S(1)}, f32[7,2,16,128]{3,2,1,0:T(8,128)}, u32[]{:S(2)}) copy-start(f32[7,2,16,128]{3,2,1,0:T(8,128)} %heat.1) | copy-start | bytes 344068

commit v8 on v7

--- a/solution.py
+++ b/solution.py
@@ -246,6 +246,38 @@
     return result
 
 
+BEGIN = 8
+
+
+def begin_terms(p, mobility, rate):
+    _, _, u, _, _, temperature, flux, _, omega = common(p, level_sums(p), mobility)
+    bent = [temperature * u[k] - flux[k] for k in range(3)]
+    return list(u) + bent + [2.4 - 2.0 * (1.2 - omega), (4.0 * rate) * temperature]
+
+
+def end_terms(terms, pa, mobility, rate):
+    u, bent, mix, push = terms[:3], terms[3:6], terms[6], terms[7]
+    level = level_adjoint_sums(pa)
+    s, d = cross_sums(pa)
+    w = 1.0 / 36.0
+    xy, xz = s[1] + s[2], s[3] + s[4]
+    along = (s[0] + s[0]) + xy + xz
+    shift = (1.5 * w) * (level[0] + along)
+    v = 4.5 * w
+    dxx, dyy, dzz = v * along - shift, v * (level[3] + xy) - shift, v * (level[4] + xz) - shift
+    dxy, dxz, dyz = v * (s[1] - s[2]), v * (s[3] - s[4]), v * level[5]
+    px = (d[0] + d[0]) + (d[1] + d[2]) + (d[3] + d[4])
+    py = level[1] + (d[1] - d[2])
+    pz = level[2] + (d[3] - d[4])
+    b = ((pa[20] - pa[21]) * 0.125, level[7], level[8])
+    ux = (3.6 * w) * px + mix * (dxx * u[0] + dxy * u[1] + dxz * u[2]) + push * b[0]
+    uy = (3.6 * w) * py + mix * (dxy * u[0] + dyy * u[1] + dyz * u[2]) + push * b[1]
+    uz = (3.6 * w) * pz + mix * (dxz * u[0] + dyz * u[1] + dzz * u[2]) + push * b[2]
+    by_resistance = -mobility * (ux * u[0] + uy * u[1] + uz * u[2])
+    by_conductivity = (-1.6 * (rate * rate)) * (b[0] * bent[0] + b[1] * bent[1] + b[2] * bent[2])
+    return by_resistance, by_conductivity
+
+
 def turn(value, by, axis):
     count = value.shape[axis]
     by %= count
@@ -281,6 +313,10 @@
 
 def second_core():
     return lax.rem(lax.axis_index("gx"), 2)
+
+
+def odd_along_y():
+    return lax.rem(lax.axis_index("gy"), 2)
 
 
 def framed(q, odd):
@@ -343,8 +379,8 @@
 
 def first_kernel(
     flow_in, heat_in, flow_weight_in, heat_weight_in, resistance_in, conductivity_in, solid_in,
-    own_out, up_out, down_out,
-    own, up, down, flow, heat, flow_weight, heat_weight, resistance, conductivity, solid, arrived, sent,
+    own_out, outer_out, inner_out,
+    own, strips, flow, heat, flow_weight, heat_weight, resistance, conductivity, solid, arrived, sent,
 ):
     pairs = [
         (flow_in, flow),
@@ -378,11 +414,12 @@
     rows = pack_rows([lambda slot, k=k: packed(own[k], slot) for k in range(2 * FIELDS)])
     low = low_lanes()
     for k in range(HALF_ROWS):
-        up[k] = jnp.where(low, rows[k], turn(rows[k + HALF_ROWS], EDGE, 1))
-        down[k] = jnp.where(low, turn(rows[k], -EDGE, 1), rows[k + HALF_ROWS])
+        strips[k] = jnp.where(low, rows[k], turn(rows[k + HALF_ROWS], EDGE, 1))
+        strips[k + HALF_ROWS] = jnp.where(low, turn(rows[k], -EDGE, 1), rows[k + HALF_ROWS])
+    above = HALF_ROWS * (1 - odd_along_y())
     copies = [
-        pltpu.make_async_copy(up, up_out, sent.at[1]),
-        pltpu.make_async_copy(down, down_out, sent.at[2]),
+        pltpu.make_async_copy(strips.at[pl.ds(above, HALF_ROWS)], outer_out, sent.at[1]),
+        pltpu.make_async_copy(strips.at[pl.ds(HALF_ROWS - above, HALF_ROWS)], inner_out, sent.at[2]),
     ]
     for copy in copies:
         copy.start()
@@ -395,10 +432,12 @@
     copy_rows(staged, own)
 
 
-def halo_kernel(own, from_below, from_above, far, near, strip):
+def halo_kernel(own, from_outer, from_inner, far, near, strip):
     low = low_lanes()
+    odd = odd_along_y() == 1
     for k in range(HALF_ROWS):
-        under, over = from_below[k], from_above[k]
+        outer, inner = from_outer[k], from_inner[k]
+        under, over = jnp.where(odd, inner, outer), jnp.where(odd, outer, inner)
         strip[k] = jnp.where(low, under, turn(over, EDGE, 1))
         strip[k + HALF_ROWS] = jnp.where(low, turn(under, -EDGE, 1), over)
     for side, rows, c in ((near, TO_NEAR, 1), (far, TO_FAR, 0)):
@@ -488,7 +527,7 @@
         put(seed, q, c, moved(pair, velocity, -1))
 
 
-def own_step_kernel(own, strip, own_state, own_seed):
+def own_step_kernel(flow, heat, own, strip, own_state, own_seed, begin):
     def wide(k, column):
         return own_value(own, strip, k, column)
 
@@ -497,6 +536,14 @@
             if own_fed(q, column):
                 put(own_state, q, column, moved(wide(q, column - VELOCITY[q][0]), VELOCITY[q], 1))
         seeds(wide, column, own_seed)
+    odd = second_core()
+    for c in range(2):
+        for z in halves():
+            terms = begin_terms(
+                given_state(flow, heat, odd, c, z), own[own_row(MOBILITY, c), z, :], own[own_row(RATE, c), z, :]
+            )
+            for k, value in enumerate(terms):
+                begin[k, c, z, :] = value
 
 
 def step_kernel(
@@ -601,7 +648,7 @@
 
 
 def near_adjoint_kernel(
-    flow, heat, own_state, state, sides, far_sides, adjoint, far_earlier, part_resistance, part_conductivity, from_near,
+    begin, own_state, state, sides, far_sides, adjoint, far_earlier, part_resistance, part_conductivity, from_near,
     by_resistance, by_conductivity,
     arrived, earlier, last, sums,
 ):
@@ -630,11 +677,10 @@
     for c in range(2):
         i = c + odd * (1 - 2 * c)
         for z in halves():
-            p = given_state(flow, heat, odd, c, z)
             pa = [last[q, c, z, :] for q in range(MEMBERS)]
             mobility, rate = [(sides[k, 0, z, narrow] if c else far_sides[k, 1, z, narrow]) for k in range(2)]
-            result = pull_back(p, level_sums(p), pa, level_adjoint_sums(pa), mobility, rate, (), True)
-            resistance, conductivity = result["by"]
+            terms = [begin[k, c, z, :] for k in range(BEGIN)]
+            resistance, conductivity = end_terms(terms, pa, mobility, rate)
             by_resistance[i, z, :] = resistance + (sums[0, z, :] if c else part_resistance[0, z, :])
             by_conductivity[i, z, :] = conductivity + (sums[1, z, :] if c else part_conductivity[0, z, :])
 
@@ -647,11 +693,11 @@
     return pltpu.VMEM(shape, jnp.float32)
 
 
-def swap_along_x(far, near):
-    count = lax.axis_size("gx")
+def swap(outer, inner, axis):
+    count = lax.axis_size(axis)
     across = [(i, (i + (1 if i % 2 else -1)) % count) for i in range(count)]
     within = [(i, i ^ 1) for i in range(count)]
-    return lax.ppermute(far, "gx", across), lax.ppermute(near, "gx", within)
+    return lax.ppermute(outer, axis, across), lax.ppermute(inner, axis, within)
 
 
 FIRST_PARAMS = pltpu.CompilerParams(vmem_limit_bytes=56 * 1024 * 1024)
@@ -660,7 +706,7 @@
 
 def on_device(flow, heat, flow_weight, heat_weight, resistance, conductivity, solid):
     in_hbm = pl.BlockSpec(memory_space=pltpu.HBM)
-    own, up, down = pl.pallas_call(
+    own, outer, inner = pl.pallas_call(
         first_kernel,
         in_specs=[in_hbm] * 7,
         out_specs=[in_hbm] * 3,
@@ -671,8 +717,7 @@
         ),
         scratch_shapes=[
             vmem(2 * FIELDS, ZED, LANES),
-            vmem(HALF_ROWS, ZED, LANES),
-            vmem(HALF_ROWS, ZED, LANES),
+            vmem(STRIP_ROWS, ZED, LANES),
             vmem(19, 2, ZED, LANES),
             vmem(7, 2, ZED, LANES),
             vmem(3, 2, ZED, LANES),
@@ -687,10 +732,7 @@
         name="collide_own",
     )(flow, heat, flow_weight, heat_weight, resistance, conductivity, solid)
 
-    count = lax.axis_size("gy")
-    upward = [(i, (i + 1) % count) for i in range(count)]
-    from_below = lax.ppermute(up, "gy", upward)
-    from_above = lax.ppermute(down, "gy", [(target, source) for source, target in upward])
+    from_outer, from_inner = swap(outer, inner, "gy")
 
     own = pl.pallas_call(
         stage_kernel,
@@ -705,9 +747,9 @@
         out_shape=(floats(SENT, ZED, LANES), floats(SENT, ZED, LANES), floats(STRIP_ROWS, ZED, LANES)),
         compiler_params=PARAMS,
         name="halo_buffers",
-    )(own, from_below, from_above)
-
-    from_far, from_near = swap_along_x(far, near)
+    )(own, from_outer, from_inner)
+
+    from_far, from_near = swap(far, near, "gx")
 
     columns = floats(MEMBERS, 2, ZED, WIDE)
     side_columns = floats(2, 2, ZED, WIDE)
@@ -715,13 +757,13 @@
     held = vmem(MEMBERS, 2, ZED, WIDE)
     busy = pl.CostEstimate(flops=10**7, bytes_accessed=10**6, transcendentals=0)
 
-    own_state, own_seed = pl.pallas_call(
+    own_state, own_seed, begin = pl.pallas_call(
         own_step_kernel,
-        out_shape=(columns, columns),
+        out_shape=(columns, columns, floats(BEGIN, 2, ZED, LANES)),
         compiler_params=PARAMS,
         cost_estimate=busy,
         name="own_step",
-    )(own, strip)
+    )(flow, heat, own, strip)
 
     far_state, far_sides, near_state, near_sides, adjoint, part_resistance, part_conductivity, far, near = (
         pl.pallas_call(
@@ -736,7 +778,7 @@
         )(own, strip, own_state, own_seed, from_far, from_near)
     )
 
-    from_far, from_near = swap_along_x(far, near)
+    from_far, from_near = swap(far, near, "gx")
 
     far_earlier, part_resistance, part_conductivity = pl.pallas_call(
         far_adjoint_kernel,
@@ -754,7 +796,7 @@
         compiler_params=PARAMS,
         name="near_adjoint",
     )(
-        flow, heat, own_state, near_state, near_sides, far_sides, adjoint, far_earlier,
+        begin, own_state, near_state, near_sides, far_sides, adjoint, far_earlier,
         part_resistance, part_conductivity, from_near,
     )
 

time: 43.8 us -> 44.5 us (1.016)
  the two profiles are of different devices: /device:TPU:26 before, /device:TPU:1 now
where the time goes in v8:
time: 44.5 us; the launch traced here: 44.2 us
  starting transfers between devices  33.8 us (76%)
  Pallas kernels  5.56 us (12%)
  waiting for transfers between devices  2.97 us (7%)
  local copies, waits for them, and re-layouts  1.05 us (2%)
  between operations  0.78 us (2%)
    ppermute x3, starting transfers between devices, swap(): lax.ppermute(inner, axis, within)  20 us
    ppermute x3, starting transfers between devices, swap(): lax.ppermute(outer, axis, across)  13.9 us
    ppermute x3, waiting for transfers between devices, swap(): lax.ppermute(inner, axis, within)  2.96 us
    pallas_call x1, Pallas kernels, on_device(): pl.pallas_call(first_kernel, in_specs=[in_hbm] * 7, out_specs=[in_hbm] *...  2.06 us
    pallas_call x1, Pallas kernels, on_device(): pl.pallas_call(step_kernel, out_shape=(columns, side_columns, columns, si...  1.3 us
    pallas_call x1, Pallas kernels, on_device(): pl.pallas_call(near_adjoint_kernel, out_shape=(cells, cells), scratch_sha...  1.06 us
    unnamed x6, local copies, waits for them, and re-layouts  1.05 us
  transfers between devices with their start and end apart: 6, of which 3 were waited for; matrix products, arithmetic and copies ran while one was open for 0% of the time, Pallas kernels for 2%

profile of v8, /device:TPU:1, one launch (start us, length us, event | category | flops | bytes accessed | tf_op | source)
XLA Modules:
  0.0 44.2 jit_solution(4244699116505879512)
XLA Ops:
  0.6 2.1 %collide_own.1 = (f32[64,16,128]{2,1,0:T(8,128)}, f32[2,16,128]{2,1,0:T(8,128)}, f32[2,16,128]{2,1,0:T(8,128)}) custom-call(f32[19,2,16,128]{3,2,1,0:T(8,128)} %flow.1, f32[7,2,16,128]{3,2,1,0:T(8,128)} %heat.1, f32[3,2,16,128]{3,2,1,0:T(8,128)} %flow_weight_in.1, f32[2,16,128]{2,1,0:T(8,128)} %heat_weight_in.1, f32[2,16,128]{2,1,0:T(8,128)} %resistance_in.1, ...), custom_call_target="tpu_custom_call" | custom-call | tf_op jit(solution)/shard_map/collide_own/pallas_call | solution.py:709
  2.7 6.4 %collective-permute-start = (f32[2,16,128]{2,1,0:T(8,128)}, f32[2,16,128]{2,1,0:T(8,128)S(1)}, u32[]{:S(2)}, u32[]{:S(2)}) collective-permute-start(f32[2,16,128]{2,1,0:T(8,128)} %get-tuple-element.24), channel_id=1, source_target_pairs={{0,7},{1,2},{2,1},{3,4},{4,3},{5,6},{6,5},{7,0},{8,15},{9,10},{10,... | collective-permute-start | bytes 49160 | tf_op jit(solution)/shard_map/ppermute | solution.py:700
  9.1 1.9 %collective-permute-start.1 = (f32[2,16,128]{2,1,0:T(8,128)}, f32[2,16,128]{2,1,0:T(8,128)S(1)}, u32[]{:S(2)}, u32[]{:S(2)}) collective-permute-start(f32[2,16,128]{2,1,0:T(8,128)} %get-tuple-element.25), channel_id=1, source_target_pairs={{0,1},{1,0},{2,3},{3,2},{4,5},{5,4},{6,7},{7,6},{8,9},{9,8},{10,11... | collective-permute-start | bytes 49160 | tf_op jit(solution)/shard_map/ppermute | solution.py:700
  11.0 0.0 copy-start.1
  11.0 1.0 %copy-done.1 = f32[64,16,128]{2,1,0:T(8,128)S(1)} copy-done((f32[64,16,128]{2,1,0:T(8,128)S(1)}, f32[64,16,128]{2,1,0:T(8,128)}, u32[]{:S(2)}) %copy-start.1) | copy-done | bytes 524312
  12.1 0.0 copy-start
  12.1 0.0 copy-start.2
  12.1 0.0 collective-permute-done.from_outer
  12.2 1.6 %collective-permute-done.1.from_inner = f32[2,16,128]{2,1,0:T(8,128)S(1)} collective-permute-done((f32[2,16,128]{2,1,0:T(8,128)}, f32[2,16,128]{2,1,0:T(8,128)S(1)}, u32[]{:S(2)}, u32[]{:S(2)}) %collective-permute-start.1) | collective-permute-done | bytes 16416 | tf_op jit(solution)/shard_map/ppermute | solution.py:700
  13.8 0.3 halo_buffers.1
  14.1 5.5 %collective-permute-start.2 = (f32[29,16,128]{2,1,0:T(8,128)S(1)}, f32[29,16,128]{2,1,0:T(8,128)S(1)}, u32[]{:S(2)}, u32[]{:S(2)}) collective-permute-start(f32[29,16,128]{2,1,0:T(8,128)S(1)} %get-tuple-element.30), channel_id=1, source_target_pairs={{0,504},{8,16},{16,8},{24,32},{32,24},{40,48},{48,40},{56,64},{64,... | collective-permute-start | bytes 712712 | tf_op jit(solution)/shard_map/ppermute | solution.py:700
  19.7 10.1 %collective-permute-start.3 = (f32[29,16,128]{2,1,0:T(8,128)S(1)}, f32[29,16,128]{2,1,0:T(8,128)S(1)}, u32[]{:S(2)}, u32[]{:S(2)}) collective-permute-start(f32[29,16,128]{2,1,0:T(8,128)S(1)} %get-tuple-element.31), channel_id=1, source_target_pairs={{0,8},{8,0},{16,24},{24,16},{32,40},{40,32},{48,56},{56,48},{64,72... | collective-permute-start | bytes 712712 | tf_op jit(solution)/shard_map/ppermute | solution.py:700
  29.7 0.0 copy-done
  29.7 0.0 copy-done.2
  29.8 0.4 own_step.1
  30.2 0.0 collective-permute-done.2.from_far
  30.2 0.7 %collective-permute-done.3.from_near = f32[29,16,128]{2,1,0:T(8,128)S(1)} collective-permute-done((f32[29,16,128]{2,1,0:T(8,128)S(1)}, f32[29,16,128]{2,1,0:T(8,128)S(1)}, u32[]{:S(2)}, u32[]{:S(2)}) %collective-permute-start.3) | collective-permute-done | bytes 237600 | tf_op jit(solution)/shard_map/ppermute | solution.py:700
  30.8 1.3 %two_steps.1 = (f32[26,2,16,256]{3,2,1,0:T(8,128)S(1)}, f32[2,2,16,256]{3,2,1,0:T(8,128)S(1)}, f32[26,2,16,256]{3,2,1,0:T(8,128)S(1)}, f32[2,2,16,256]{3,2,1,0:T...) custom-call(f32[64,16,128]{2,1,0:T(8,128)S(1)} %stage_own.1.own, ...), custom_call_target="tpu_custom_call" | custom-call | tf_op jit(solution)/shard_map/two_steps/pallas_call | solution.py:769
  32.1 1.9 %collective-permute-start.4 = (f32[23,16,128]{2,1,0:T(8,128)S(1)}, f32[23,16,128]{2,1,0:T(8,128)S(1)}, u32[]{:S(2)}, u32[]{:S(2)}) collective-permute-start(f32[23,16,128]{2,1,0:T(8,128)S(1)} %get-tuple-element.39), channel_id=1, source_target_pairs={{0,504},{8,16},{16,8},{24,32},{32,24},{40,48},{48,40},{56,64},{64,... | collective-permute-start | bytes 565256 | tf_op jit(solution)/shard_map/ppermute | solution.py:700
  34.1 8.0 %collective-permute-start.5 = (f32[23,16,128]{2,1,0:T(8,128)S(1)}, f32[23,16,128]{2,1,0:T(8,128)S(1)}, u32[]{:S(2)}, u32[]{:S(2)}) collective-permute-start(f32[23,16,128]{2,1,0:T(8,128)S(1)} %get-tuple-element.43), channel_id=1, source_target_pairs={{0,8},{8,0},{16,24},{24,16},{32,40},{40,32},{48,56},{56,48},{64,72... | collective-permute-start | bytes 565256 | tf_op jit(solution)/shard_map/ppermute | solution.py:700
  42.1 0.0 collective-permute-done.4.from_far
  42.1 0.4 far_adjoint.1
  42.5 0.7 %collective-permute-done.5.from_near = f32[23,16,128]{2,1,0:T(8,128)S(1)} collective-permute-done((f32[23,16,128]{2,1,0:T(8,128)S(1)}, f32[23,16,128]{2,1,0:T(8,128)S(1)}, u32[]{:S(2)}, u32[]{:S(2)}) %collective-permute-start.5) | collective-permute-done | bytes 188448 | tf_op jit(solution)/shard_map/ppermute | solution.py:700
  43.1 1.1 %near_adjoint.1 = (f32[2,16,128]{2,1,0:T(8,128)}, f32[2,16,128]{2,1,0:T(8,128)}) custom-call(f32[8,2,16,128]{3,2,1,0:T(8,128)S(1)} %get-tuple-element.27.begin, f32[26,2,16,256]{3,2,1,0:T(8,128)S(1)} %get-tuple-element.28.own_state, f32[26,2,16,256]{3,2,1,0:T(8,128)S(1)} %get-tuple-element.32.state, f32[2,2,16,256]{3,2,1,0:T(8,128)S(1)} %get-tuple-element.33.sides, ...), custom_call_target="tpu_custom_call" | custom-call | tf_op jit(solution)/shard_map/near_adjoint/pallas_call | solution.py:792
  (1 shorter events, 0.0 us)
Async XLA Ops:
  2.7 9.4 %collective-permute-start = (f32[2,16,128]{2,1,0:T(8,128)}, f32[2,16,128]{2,1,0:T(8,128)S(1)}, u32[]{:S(2)}, u32[]{:S(2)}) collective-permute-start(f32[2,16,128]{2,1,0:T(8,128)} %get-tuple-element.24), channel_id=1, source_target_pairs={{0,7},{1,2},{2,1},{3,4},{4,3},{5,6},{6,5},{7,0},{8,15},{9,10},{10,... | collective-permute-start | bytes 49160 | tf_op jit(solution)/shard_map/ppermute | solution.py:700
  9.1 4.7 %collective-permute-start.1 = (f32[2,16,128]{2,1,0:T(8,128)}, f32[2,16,128]{2,1,0:T(8,128)S(1)}, u32[]{:S(2)}, u32[]{:S(2)}) collective-permute-start(f32[2,16,128]{2,1,0:T(8,128)} %get-tuple-element.25), channel_id=1, source_target_pairs={{0,1},{1,0},{2,3},{3,2},{4,5},{5,4},{6,7},{7,6},{8,9},{9,8},{10,11... | collective-permute-start | bytes 49160 | tf_op jit(solution)/shard_map/ppermute | solution.py:700
  11.0 1.0 %copy-start.1 = (f32[64,16,128]{2,1,0:T(8,128)S(1)}, f32[64,16,128]{2,1,0:T(8,128)}, u32[]{:S(2)}) copy-start(f32[64,16,128]{2,1,0:T(8,128)} %get-tuple-element.23.own) | copy-start | bytes 1572868
  12.1 17.6 %copy-start = (f32[19,2,16,128]{3,2,1,0:T(8,128)S(1)}, f32[19,2,16,128]{3,2,1,0:T(8,128)}, u32[]{:S(2)}) copy-start(f32[19,2,16,128]{3,2,1,0:T(8,128)} %flow.1) | copy-start | bytes 933892
  12.1 17.6 %copy-start.2 = (f32[7,2,16,128]{3,2,1,0:T(8,128)S(1)}, f32[7,2,16,128]{3,2,1,0:T(8,128)}, u32[]{:S(2)}) copy-start(f32[7,2,16,128]{3,2,1,0:T(8,128)} %heat.1) | copy-start | bytes 344068
  14.1 16.0 %collective-permute-start.2 = (f32[29,16,128]{2,1,0:T(8,128)S(1)}, f32[29,16,128]{2,1,0:T(8,128)S(1)}, u32[]{:S(2)}, u32[]{:S(2)}) collective-permute-start(f32[29,16,128]{2,1,0:T(8,128)S(1)} %get-tuple-element.30), channel_id=1, source_target_pairs={{0,504},{8,16},{16,8},{24,32},{32,24},{40,48},{48,40},{56,64},{64,... | collective-permute-start | bytes 712712 | tf_op jit(solution)/shard_map/ppermute | solution.py:700
  19.7 11.2 %collective-permute-start.3 = (f32[29,16,128]{2,1,0:T(8,128)S(1)}, f32[29,16,128]{2,1,0:T(8,128)S(1)}, u32[]{:S(2)}, u32[]{:S(2)}) collective-permute-start(f32[29,16,128]{2,1,0:T(8,128)S(1)} %get-tuple-element.31), channel_id=1, source_target_pairs={{0,8},{8,0},{16,24},{24,16},{32,40},{40,32},{48,56},{56,48},{64,72... | collective-permute-start | bytes 712712 | tf_op jit(solution)/shard_map/ppermute | solution.py:700
  32.1 9.9 %collective-permute-start.4 = (f32[23,16,128]{2,1,0:T(8,128)S(1)}, f32[23,16,128]{2,1,0:T(8,128)S(1)}, u32[]{:S(2)}, u32[]{:S(2)}) collective-permute-start(f32[23,16,128]{2,1,0:T(8,128)S(1)} %get-tuple-element.39), channel_id=1, source_target_pairs={{0,504},{8,16},{16,8},{24,32},{32,24},{40,48},{48,40},{56,64},{64,... | collective-permute-start | bytes 565256 | tf_op jit(solution)/shard_map/ppermute | solution.py:700
  34.1 9.1 %collective-permute-start.5 = (f32[23,16,128]{2,1,0:T(8,128)S(1)}, f32[23,16,128]{2,1,0:T(8,128)S(1)}, u32[]{:S(2)}, u32[]{:S(2)}) collective-permute-start(f32[23,16,128]{2,1,0:T(8,128)S(1)} %get-tuple-element.43), channel_id=1, source_target_pairs={{0,8},{8,0},{16,24},{24,16},{32,40},{40,32},{48,56},{56,48},{64,72... | collective-permute-start | bytes 565256 | tf_op jit(solution)/shard_map/ppermute | solution.py:700

commit v9 on v8

--- a/solution.py
+++ b/solution.py
@@ -315,10 +315,6 @@
     return lax.rem(lax.axis_index("gx"), 2)
 
 
-def odd_along_y():
-    return lax.rem(lax.axis_index("gy"), 2)
-
-
 def framed(q, odd):
     return q + odd * (mirrored(q) - q)
 
@@ -379,7 +375,7 @@
 
 def first_kernel(
     flow_in, heat_in, flow_weight_in, heat_weight_in, resistance_in, conductivity_in, solid_in,
-    own_out, outer_out, inner_out,
+    own_out, up_out, down_out,
     own, strips, flow, heat, flow_weight, heat_weight, resistance, conductivity, solid, arrived, sent,
 ):
     pairs = [
@@ -416,10 +412,9 @@
     for k in range(HALF_ROWS):
         strips[k] = jnp.where(low, rows[k], turn(rows[k + HALF_ROWS], EDGE, 1))
         strips[k + HALF_ROWS] = jnp.where(low, turn(rows[k], -EDGE, 1), rows[k + HALF_ROWS])
-    above = HALF_ROWS * (1 - odd_along_y())
     copies = [
-        pltpu.make_async_copy(strips.at[pl.ds(above, HALF_ROWS)], outer_out, sent.at[1]),
-        pltpu.make_async_copy(strips.at[pl.ds(HALF_ROWS - above, HALF_ROWS)], inner_out, sent.at[2]),
+        pltpu.make_async_copy(strips.at[pl.ds(0, HALF_ROWS)], up_out, sent.at[1]),
+        pltpu.make_async_copy(strips.at[pl.ds(HALF_ROWS, HALF_ROWS)], down_out, sent.at[2]),
     ]
     for copy in copies:
         copy.start()
@@ -432,12 +427,10 @@
     copy_rows(staged, own)
 
 
-def halo_kernel(own, from_outer, from_inner, far, near, strip):
+def halo_kernel(own, from_below, from_above, far, near, strip):
     low = low_lanes()
-    odd = odd_along_y() == 1
     for k in range(HALF_ROWS):
-        outer, inner = from_outer[k], from_inner[k]
-        under, over = jnp.where(odd, inner, outer), jnp.where(odd, outer, inner)
+        under, over = from_below[k], from_above[k]
         strip[k] = jnp.where(low, under, turn(over, EDGE, 1))
         strip[k + HALF_ROWS] = jnp.where(low, turn(under, -EDGE, 1), over)
     for side, rows, c in ((near, TO_NEAR, 1), (far, TO_FAR, 0)):
@@ -693,11 +686,11 @@
     return pltpu.VMEM(shape, jnp.float32)
 
 
-def swap(outer, inner, axis):
-    count = lax.axis_size(axis)
+def swap_along_x(far, near):
+    count = lax.axis_size("gx")
     across = [(i, (i + (1 if i % 2 else -1)) % count) for i in range(count)]
     within = [(i, i ^ 1) for i in range(count)]
-    return lax.ppermute(outer, axis, across), lax.ppermute(inner, axis, within)
+    return lax.ppermute(far, "gx", across), lax.ppermute(near, "gx", within)
 
 
 FIRST_PARAMS = pltpu.CompilerParams(vmem_limit_bytes=56 * 1024 * 1024)
@@ -706,7 +699,7 @@
 
 def on_device(flow, heat, flow_weight, heat_weight, resistance, conductivity, solid):
     in_hbm = pl.BlockSpec(memory_space=pltpu.HBM)
-    own, outer, inner = pl.pallas_call(
+    own, up, down = pl.pallas_call(
         first_kernel,
         in_specs=[in_hbm] * 7,
         out_specs=[in_hbm] * 3,
@@ -732,7 +725,10 @@
         name="collide_own",
     )(flow, heat, flow_weight, heat_weight, resistance, conductivity, solid)
 
-    from_outer, from_inner = swap(outer, inner, "gy")
+    count = lax.axis_size("gy")
+    upward = [(i, (i + 1) % count) for i in range(count)]
+    from_below = lax.ppermute(up, "gy", upward)
+    from_above = lax.ppermute(down, "gy", [(target, source) for source, target in upward])
 
     own = pl.pallas_call(
         stage_kernel,
@@ -747,9 +743,9 @@
         out_shape=(floats(SENT, ZED, LANES), floats(SENT, ZED, LANES), floats(STRIP_ROWS, ZED, LANES)),
         compiler_params=PARAMS,
         name="halo_buffers",
-    )(own, from_outer, from_inner)
-
-    from_far, from_near = swap(far, near, "gx")
+    )(own, from_below, from_above)
+
+    from_far, from_near = swap_along_x(far, near)
 
     columns = floats(MEMBERS, 2, ZED, WIDE)
     side_columns = floats(2, 2, ZED, WIDE)
@@ -778,7 +774,7 @@
         )(own, strip, own_state, own_seed, from_far, from_near)
     )
 
-    from_far, from_near = swap(far, near, "gx")
+    from_far, from_near = swap_along_x(far, near)
 
     far_earlier, part_resistance, part_conductivity = pl.pallas_call(
         far_adjoint_kernel,

time: 44.5 us -> 43.1 us (0.969)
  waiting for transfers between devices: 2.97 us -> 1.32 us
    ppermute x6, waiting for transfers between devices: 2.97 us -> 1.32 us  [the longest x4 1.32 us: swap_along_x(): return (lax.ppermute(far, 'gx', across), lax.ppermute(near, 'gx', within))]
  transfers between devices with their start and end apart: 6 -> 6, of which waited for: 3 -> 2; matrix products, arithmetic and copies ran while one was open for 0% -> 0% of each run, Pallas kernels for 2% -> 2%
where the time goes in v9:
time: 43.1 us; the launch traced here: 42.8 us
  starting transfers between devices  34 us (79%)
  Pallas kernels  5.57 us (13%)
  waiting for transfers between devices  1.32 us (3%)
  local copies, waits for them, and re-layouts  1.05 us (2%)
  between operations  0.78 us (2%)
    ppermute x4, starting transfers between devices, swap_along_x(): return (lax.ppermute(far, 'gx', across), lax.ppermute(near, 'gx', within))  25.7 us
    ppermute x1, starting transfers between devices, on_device(): lax.ppermute(down, 'gy', [(target, source) for source, target in upward])  4.37 us
    ppermute x1, starting transfers between devices, on_device(): from_below = lax.ppermute(up, 'gy', upward)  3.95 us
    pallas_call x1, Pallas kernels, on_device(): pl.pallas_call(first_kernel, in_specs=[in_hbm] * 7, out_specs=[in_hbm] *...  2.08 us
    ppermute x4, waiting for transfers between devices, swap_along_x(): return (lax.ppermute(far, 'gx', across), lax.ppermute(near, 'gx', within))  1.32 us
    pallas_call x1, Pallas kernels, on_device(): pl.pallas_call(step_kernel, out_shape=(columns, side_columns, columns, si...  1.3 us
    pallas_call x1, Pallas kernels, on_device(): pl.pallas_call(near_adjoint_kernel, out_shape=(cells, cells), scratch_sha...  1.06 us
    unnamed x6, local copies, waits for them, and re-layouts  1.05 us
  transfers between devices with their start and end apart: 6, of which 2 were waited for; matrix products, arithmetic and copies ran while one was open for 0% of the time, Pallas kernels for 2%

profile of v9, /device:TPU:1, one launch (start us, length us, event | category | flops | bytes accessed | tf_op | source)
XLA Modules:
  0.0 42.8 jit_solution(18318808893329929202)
XLA Ops:
  0.6 2.1 %collide_own.1 = (f32[64,16,128]{2,1,0:T(8,128)}, f32[2,16,128]{2,1,0:T(8,128)}, f32[2,16,128]{2,1,0:T(8,128)}) custom-call(f32[19,2,16,128]{3,2,1,0:T(8,128)} %flow.1, f32[7,2,16,128]{3,2,1,0:T(8,128)} %heat.1, f32[3,2,16,128]{3,2,1,0:T(8,128)} %flow_weight_in.1, f32[2,16,128]{2,1,0:T(8,128)} %heat_weight_in.1, f32[2,16,128]{2,1,0:T(8,128)} %resistance_in.1, ...), custom_call_target="tpu_custom_call" | custom-call | tf_op jit(solution)/shard_map/collide_own/pallas_call | solution.py:702
  2.7 3.9 %collective-permute-start = (f32[2,16,128]{2,1,0:T(8,128)}, f32[2,16,128]{2,1,0:T(8,128)S(1)}, u32[]{:S(2)}, u32[]{:S(2)}) collective-permute-start(f32[2,16,128]{2,1,0:T(8,128)} %get-tuple-element.24), channel_id=1, source_target_pairs={{0,1},{1,2},{2,3},{3,4},{4,5},{5,6},{6,7},{7,0},{8,9},{9,10},{10,1... | collective-permute-start | bytes 49160 | tf_op jit(solution)/shard_map/ppermute | solution.py:730
  6.7 4.4 %collective-permute-start.1 = (f32[2,16,128]{2,1,0:T(8,128)}, f32[2,16,128]{2,1,0:T(8,128)S(1)}, u32[]{:S(2)}, u32[]{:S(2)}) collective-permute-start(f32[2,16,128]{2,1,0:T(8,128)} %get-tuple-element.25), channel_id=1, source_target_pairs={{1,0},{2,1},{3,2},{4,3},{5,4},{6,5},{7,6},{0,7},{9,8},{10,9},{11,1... | collective-permute-start | bytes 49160 | tf_op jit(solution)/shard_map/ppermute | solution.py:731
  11.1 0.0 copy-start.1
  11.1 1.0 %copy-done.1 = f32[64,16,128]{2,1,0:T(8,128)S(1)} copy-done((f32[64,16,128]{2,1,0:T(8,128)S(1)}, f32[64,16,128]{2,1,0:T(8,128)}, u32[]{:S(2)}) %copy-start.1) | copy-done | bytes 524312
  12.1 0.0 copy-start
  12.1 0.0 copy-start.2
  12.2 0.0 collective-permute-done.from_below
  12.2 0.0 collective-permute-done.1.from_above
  12.2 0.3 halo_buffers.1
  12.5 5.1 %collective-permute-start.2 = (f32[29,16,128]{2,1,0:T(8,128)S(1)}, f32[29,16,128]{2,1,0:T(8,128)S(1)}, u32[]{:S(2)}, u32[]{:S(2)}) collective-permute-start(f32[29,16,128]{2,1,0:T(8,128)S(1)} %get-tuple-element.30), channel_id=1, source_target_pairs={{0,504},{8,16},{16,8},{24,32},{32,24},{40,48},{48,40},{56,64},{64,... | collective-permute-start | bytes 712712 | tf_op jit(solution)/shard_map/ppermute | solution.py:693
  17.6 10.7 %collective-permute-start.3 = (f32[29,16,128]{2,1,0:T(8,128)S(1)}, f32[29,16,128]{2,1,0:T(8,128)S(1)}, u32[]{:S(2)}, u32[]{:S(2)}) collective-permute-start(f32[29,16,128]{2,1,0:T(8,128)S(1)} %get-tuple-element.31), channel_id=1, source_target_pairs={{0,8},{8,0},{16,24},{24,16},{32,40},{40,32},{48,56},{56,48},{64,72... | collective-permute-start | bytes 712712 | tf_op jit(solution)/shard_map/ppermute | solution.py:693
  28.3 0.0 copy-done
  28.3 0.0 copy-done.2
  28.3 0.4 own_step.1
  28.7 0.0 collective-permute-done.2.from_far
  28.8 0.7 %collective-permute-done.3.from_near = f32[29,16,128]{2,1,0:T(8,128)S(1)} collective-permute-done((f32[29,16,128]{2,1,0:T(8,128)S(1)}, f32[29,16,128]{2,1,0:T(8,128)S(1)}, u32[]{:S(2)}, u32[]{:S(2)}) %collective-permute-start.3) | collective-permute-done | bytes 237600 | tf_op jit(solution)/shard_map/ppermute | solution.py:693
  29.4 1.3 %two_steps.1 = (f32[26,2,16,256]{3,2,1,0:T(8,128)S(1)}, f32[2,2,16,256]{3,2,1,0:T(8,128)S(1)}, f32[26,2,16,256]{3,2,1,0:T(8,128)S(1)}, f32[2,2,16,256]{3,2,1,0:T...) custom-call(f32[64,16,128]{2,1,0:T(8,128)S(1)} %stage_own.1.own, ...), custom_call_target="tpu_custom_call" | custom-call | tf_op jit(solution)/shard_map/two_steps/pallas_call | solution.py:765
  30.7 1.9 %collective-permute-start.4 = (f32[23,16,128]{2,1,0:T(8,128)S(1)}, f32[23,16,128]{2,1,0:T(8,128)S(1)}, u32[]{:S(2)}, u32[]{:S(2)}) collective-permute-start(f32[23,16,128]{2,1,0:T(8,128)S(1)} %get-tuple-element.39), channel_id=1, source_target_pairs={{0,504},{8,16},{16,8},{24,32},{32,24},{40,48},{48,40},{56,64},{64,... | collective-permute-start | bytes 565256 | tf_op jit(solution)/shard_map/ppermute | solution.py:693
  32.6 8.0 %collective-permute-start.5 = (f32[23,16,128]{2,1,0:T(8,128)S(1)}, f32[23,16,128]{2,1,0:T(8,128)S(1)}, u32[]{:S(2)}, u32[]{:S(2)}) collective-permute-start(f32[23,16,128]{2,1,0:T(8,128)S(1)} %get-tuple-element.43), channel_id=1, source_target_pairs={{0,8},{8,0},{16,24},{24,16},{32,40},{40,32},{48,56},{56,48},{64,72... | collective-permute-start | bytes 565256 | tf_op jit(solution)/shard_map/ppermute | solution.py:693
  40.7 0.0 collective-permute-done.4.from_far
  40.7 0.4 far_adjoint.1
  41.0 0.7 %collective-permute-done.5.from_near = f32[23,16,128]{2,1,0:T(8,128)S(1)} collective-permute-done((f32[23,16,128]{2,1,0:T(8,128)S(1)}, f32[23,16,128]{2,1,0:T(8,128)S(1)}, u32[]{:S(2)}, u32[]{:S(2)}) %collective-permute-start.5) | collective-permute-done | bytes 188448 | tf_op jit(solution)/shard_map/ppermute | solution.py:693
  41.7 1.1 %near_adjoint.1 = (f32[2,16,128]{2,1,0:T(8,128)}, f32[2,16,128]{2,1,0:T(8,128)}) custom-call(f32[8,2,16,128]{3,2,1,0:T(8,128)S(1)} %get-tuple-element.27.begin, f32[26,2,16,256]{3,2,1,0:T(8,128)S(1)} %get-tuple-element.28.own_state, f32[26,2,16,256]{3,2,1,0:T(8,128)S(1)} %get-tuple-element.32.state, f32[2,2,16,256]{3,2,1,0:T(8,128)S(1)} %get-tuple-element.33.sides, ...), custom_call_target="tpu_custom_call" | custom-call | tf_op jit(solution)/shard_map/near_adjoint/pallas_call | solution.py:788
  (1 shorter events, 0.0 us)
Async XLA Ops:
  2.7 9.4 %collective-permute-start = (f32[2,16,128]{2,1,0:T(8,128)}, f32[2,16,128]{2,1,0:T(8,128)S(1)}, u32[]{:S(2)}, u32[]{:S(2)}) collective-permute-start(f32[2,16,128]{2,1,0:T(8,128)} %get-tuple-element.24), channel_id=1, source_target_pairs={{0,1},{1,2},{2,3},{3,4},{4,5},{5,6},{6,7},{7,0},{8,9},{9,10},{10,1... | collective-permute-start | bytes 49160 | tf_op jit(solution)/shard_map/ppermute | solution.py:730
  6.7 5.5 %collective-permute-start.1 = (f32[2,16,128]{2,1,0:T(8,128)}, f32[2,16,128]{2,1,0:T(8,128)S(1)}, u32[]{:S(2)}, u32[]{:S(2)}) collective-permute-start(f32[2,16,128]{2,1,0:T(8,128)} %get-tuple-element.25), channel_id=1, source_target_pairs={{1,0},{2,1},{3,2},{4,3},{5,4},{6,5},{7,6},{0,7},{9,8},{10,9},{11,1... | collective-permute-start | bytes 49160 | tf_op jit(solution)/shard_map/ppermute | solution.py:731
  11.1 1.0 %copy-start.1 = (f32[64,16,128]{2,1,0:T(8,128)S(1)}, f32[64,16,128]{2,1,0:T(8,128)}, u32[]{:S(2)}) copy-start(f32[64,16,128]{2,1,0:T(8,128)} %get-tuple-element.23.own) | copy-start | bytes 1572868
  12.1 16.2 %copy-start = (f32[19,2,16,128]{3,2,1,0:T(8,128)S(1)}, f32[19,2,16,128]{3,2,1,0:T(8,128)}, u32[]{:S(2)}) copy-start(f32[19,2,16,128]{3,2,1,0:T(8,128)} %flow.1) | copy-start | bytes 933892
  12.1 16.2 %copy-start.2 = (f32[7,2,16,128]{3,2,1,0:T(8,128)S(1)}, f32[7,2,16,128]{3,2,1,0:T(8,128)}, u32[]{:S(2)}) copy-start(f32[7,2,16,128]{3,2,1,0:T(8,128)} %heat.1) | copy-start | bytes 344068
  12.5 16.2 %collective-permute-start.2 = (f32[29,16,128]{2,1,0:T(8,128)S(1)}, f32[29,16,128]{2,1,0:T(8,128)S(1)}, u32[]{:S(2)}, u32[]{:S(2)}) collective-permute-start(f32[29,16,128]{2,1,0:T(8,128)S(1)} %get-tuple-element.30), channel_id=1, source_target_pairs={{0,504},{8,16},{16,8},{24,32},{32,24},{40,48},{48,40},{56,64},{64,... | collective-permute-start | bytes 712712 | tf_op jit(solution)/shard_map/ppermute | solution.py:693
  17.6 11.8 %collective-permute-start.3 = (f32[29,16,128]{2,1,0:T(8,128)S(1)}, f32[29,16,128]{2,1,0:T(8,128)S(1)}, u32[]{:S(2)}, u32[]{:S(2)}) collective-permute-start(f32[29,16,128]{2,1,0:T(8,128)S(1)} %get-tuple-element.31), channel_id=1, source_target_pairs={{0,8},{8,0},{16,24},{24,16},{32,40},{40,32},{48,56},{56,48},{64,72... | collective-permute-start | bytes 712712 | tf_op jit(solution)/shard_map/ppermute | solution.py:693
  30.7 9.9 %collective-permute-start.4 = (f32[23,16,128]{2,1,0:T(8,128)S(1)}, f32[23,16,128]{2,1,0:T(8,128)S(1)}, u32[]{:S(2)}, u32[]{:S(2)}) collective-permute-start(f32[23,16,128]{2,1,0:T(8,128)S(1)} %get-tuple-element.39), channel_id=1, source_target_pairs={{0,504},{8,16},{16,8},{24,32},{32,24},{40,48},{48,40},{56,64},{64,... | collective-permute-start | bytes 565256 | tf_op jit(solution)/shard_map/ppermute | solution.py:693
  32.6 9.1 %collective-permute-start.5 = (f32[23,16,128]{2,1,0:T(8,128)S(1)}, f32[23,16,128]{2,1,0:T(8,128)S(1)}, u32[]{:S(2)}, u32[]{:S(2)}) collective-permute-start(f32[23,16,128]{2,1,0:T(8,128)S(1)} %get-tuple-element.43), channel_id=1, source_target_pairs={{0,8},{8,0},{16,24},{24,16},{32,40},{40,32},{48,56},{56,48},{64,72... | collective-permute-start | bytes 565256 | tf_op jit(solution)/shard_map/ppermute | solution.py:693

commit v10 on v9

--- a/solution.py
+++ b/solution.py
@@ -171,10 +171,16 @@
     return result
 
 
-def pull_back(p, level, pa, adjoint_level, mobility, rate, wanted, sensitivity):
-    rho, j, u, square, stress, temperature, flux, decay, omega = common(p, level, mobility)
+def state_terms(p, level, mobility, rate, full):
+    _, _, u, _, stress, temperature, flux, decay, omega = common(p, level, mobility)
+    slope = jnp.where(mobility == 0.0, 0.0, (0.6 * decay) * (omega * omega))
+    terms = list(u) + list(stress) + [1.2 - omega, (4.0 * rate) * temperature, slope]
+    return terms + [temperature * u[k] - flux[k] for k in range(3)] if full else terms
+
+
+def pull_back(terms, pa, adjoint_level, mobility, rate, wanted, sensitivity):
+    u, stress, lam, push, slope, bent = terms[:3], terms[3:9], terms[9], terms[10], terms[11], terms[12:]
     solid = mobility == 0.0
-    lam = 1.2 - omega
     s, d = cross_sums(pa)
     w = 1.0 / 36.0
     xy, xz = s[1] + s[2], s[3] + s[4]
@@ -190,7 +196,6 @@
     dxy, dxz, dyz = 4.5 * rxy, 4.5 * rxz, 4.5 * ryz
     mix = 2.4 - 2.0 * lam
     b = ((pa[20] - pa[21]) * 0.125, adjoint_level[7], adjoint_level[8])
-    push = (4.0 * rate) * temperature
     ux = 3.6 * px + mix * (dxx * u[0] + dxy * u[1] + dxz * u[2]) + push * b[0]
     uy = 3.6 * py + mix * (dxy * u[0] + dyy * u[1] + dyz * u[2]) + push * b[1]
     uz = 3.6 * pz + mix * (dxz * u[0] + dyz * u[1] + dzz * u[2]) + push * b[2]
@@ -222,7 +227,7 @@
             adjoint_level[6]
             + 0.175 * (pa[20] + pa[21])
             + (4.0 * rate) * (b[0] * u[0] + b[1] * u[1] + b[2] * u[2])
-            - jnp.where(solid, 0.0, lam_bar * (0.6 * decay) * (omega * omega))
+            - lam_bar * slope
         )
         keep = 5.6 - 4.0 * rate
         if 19 in wanted:
@@ -235,13 +240,8 @@
             if m in wanted:
                 result[m] = (warm - along) - 0.4 * pa[m]
     if sensitivity:
-        by_resistance = -(mobility * mobility) * (ux * j[0] + uy * j[1] + uz * j[2])
-        bent = (
-            b[0] * (temperature * u[0] - flux[0])
-            + b[1] * (temperature * u[1] - flux[1])
-            + b[2] * (temperature * u[2] - flux[2])
-        )
-        by_conductivity = (-1.6 * (rate * rate)) * bent
+        by_resistance = -mobility * (ux * u[0] + uy * u[1] + uz * u[2])
+        by_conductivity = (-1.6 * (rate * rate)) * (b[0] * bent[0] + b[1] * bent[1] + b[2] * bent[2])
         result["by"] = (by_resistance, by_conductivity)
     return result
 
@@ -573,9 +573,8 @@
             ]
             inner = y.start == 0
             mobility, rate = [near_sides[k, 0, z, y] if c else far_sides[k, 1, z, y] for k in range(2)]
-            result = pull_back(
-                p, level_sums(p), pa, level_adjoint_sums(pa), mobility, rate, range(MEMBERS), inner
-            )
+            terms = state_terms(p, level_sums(p), mobility, rate, inner)
+            result = pull_back(terms, pa, level_adjoint_sums(pa), mobility, rate, range(MEMBERS), inner)
             if inner:
                 by_resistance[c, z, :], by_conductivity[c, z, :] = result["by"]
             for q in range(MEMBERS):
@@ -595,24 +594,62 @@
             side[ADJ_BULK + k] = row
 
 
-def adjoint_step(wide, column, own_state, state, sides, arrived, earlier, first, keep):
+TERMS = 15
+
+
+def prepare_kernel(
+    own_state, far_state, far_sides, near_state, near_sides, adjoint,
+    terms, own_arrived, own_sums,
+):
+    for column in range(-1, 3):
+        first, state, sides = (1, near_state, near_sides) if column >= 1 else (-1, far_state, far_sides)
+        for z, y in tiles(WIDE):
+            p = state_of(own_state, state, first, column, z, y)
+            mobility, rate = sides[0, column - first, z, y], sides[1, column - first, z, y]
+            full = y.start == 0 and 0 <= column <= 1
+            values = state_terms(p, level_of(p, column, level_sums), mobility, rate, full)
+            for k, value in enumerate(values):
+                terms[k, column + 1, z, y] = value
+    for column in range(-1, 3):
+        level = {}
+        for q in range(MEMBERS):
+            if 0 <= column + VELOCITY[q][0] <= 1:
+                pair = moved(split(adjoint[q, column + VELOCITY[q][0]]), VELOCITY[q], -1)
+                put(own_arrived, q, column + 1, pair)
+                if q in LEVEL:
+                    level[q] = pair
+        if 0 <= column <= 1:
+            sums = [level_adjoint_sums({q: level[q][t] for q in LEVEL}) for t in range(2)]
+            for k in range(SUMS):
+                put(own_sums, k, column, (sums[0][k], sums[1][k]))
+
+
+def adjoint_step(halo, column, terms, own_arrived, own_sums, sides, arrived, earlier, first, keep):
     own = 0 <= column <= 1
     i = column - first
     for q in range(MEMBERS):
-        if own or q not in LEVEL:
-            put(arrived, q, i, moved(wide(q, column + VELOCITY[q][0]), VELOCITY[q], -1))
+        if 0 <= column + VELOCITY[q][0] <= 1:
+            continue
+        if q not in LEVEL:
+            put(arrived, q, i, moved(halo(q, column + VELOCITY[q][0]), VELOCITY[q], -1))
         elif q in LEVEL[:SUMS]:
-            put(arrived, q, i, moved(wide(SUM_FIELDS[LEVEL.index(q)], column), STILL, 1))
+            put(arrived, q, i, moved(halo(SUM_FIELDS[LEVEL.index(q)], column), STILL, 1))
     for z, y in tiles(WIDE):
         inner = y.start == 0
         wanted = [
             q for q in range(MEMBERS) if 0 <= column - VELOCITY[q][0] <= 1 and (inner or VELOCITY[q][1])
         ]
-        p = state_of(own_state, state, first, column, z, y)
-        pa = [arrived[q, i, z, y] for q in range(MEMBERS)]
+        pa = [
+            own_arrived[q, column + 1, z, y] if 0 <= column + VELOCITY[q][0] <= 1 else arrived[q, i, z, y]
+            for q in range(MEMBERS)
+        ]
+        if own:
+            level = [own_sums[k, column, z, y] for k in range(SUMS)]
+        else:
+            level = [pa[q] for q in LEVEL[:SUMS]]
+        held_terms = [terms[k, column + 1, z, y] for k in range(TERMS if inner and own else TERMS - 3)]
         result = pull_back(
-            p, level_of(p, column, level_sums), pa, level_of(pa, column, level_adjoint_sums),
-            sides[0, i, z, y], sides[1, i, z, y], wanted, inner and own,
+            held_terms, pa, level, sides[0, i, z, y], sides[1, i, z, y], wanted, inner and own
         )
         for q in wanted:
             earlier[q, i, z, y] = result[q]
@@ -621,41 +658,38 @@
 
 
 def far_adjoint_kernel(
-    own_state, state, sides, adjoint, part_resistance, part_conductivity, from_far,
+    terms, own_arrived, own_sums, sides, part_resistance, part_conductivity, from_far,
     earlier, by_resistance, by_conductivity,
     arrived,
 ):
-    def wide(k, column):
-        if column < 0:
-            return halo_value(from_far, ADJ_BULK, far_place(ADJ_TO_FAR, k, column))
-        return split(adjoint[k, column])
+    def halo(k, column):
+        return halo_value(from_far, ADJ_BULK, far_place(ADJ_TO_FAR, k, column))
 
     def keep(z, resistance, conductivity):
         by_resistance[0, z, :] = part_resistance[0, z, :] + resistance
         by_conductivity[0, z, :] = part_conductivity[0, z, :] + conductivity
 
     for column in (-1, 0):
-        adjoint_step(wide, column, own_state, state, sides, arrived, earlier, -1, keep)
+        adjoint_step(halo, column, terms, own_arrived, own_sums, sides, arrived, earlier, -1, keep)
     by_resistance[1] = part_resistance[1]
     by_conductivity[1] = part_conductivity[1]
 
 
 def near_adjoint_kernel(
-    begin, own_state, state, sides, far_sides, adjoint, far_earlier, part_resistance, part_conductivity, from_near,
+    begin, terms, own_arrived, own_sums, sides, far_sides, far_earlier,
+    part_resistance, part_conductivity, from_near,
     by_resistance, by_conductivity,
     arrived, earlier, last, sums,
 ):
-    def wide(k, column):
-        if column > 1:
-            return halo_value(from_near, ADJ_BULK, near_place(ADJ_TO_NEAR, k, column))
-        return split(adjoint[k, column])
+    def halo(k, column):
+        return halo_value(from_near, ADJ_BULK, near_place(ADJ_TO_NEAR, k, column))
 
     def keep(z, resistance, conductivity):
         sums[0, z, :] = part_resistance[1, z, :] + resistance
         sums[1, z, :] = part_conductivity[1, z, :] + conductivity
 
     for column in (1, 2):
-        adjoint_step(wide, column, own_state, state, sides, arrived, earlier, 1, keep)
+        adjoint_step(halo, column, terms, own_arrived, own_sums, sides, arrived, earlier, 1, keep)
     for c in range(2):
         for q in range(MEMBERS):
             velocity = VELOCITY[q]
@@ -776,6 +810,16 @@
 
     from_far, from_near = swap_along_x(far, near)
 
+    terms, own_arrived, own_sums = pl.pallas_call(
+        prepare_kernel,
+        out_shape=(
+            floats(TERMS, 4, ZED, WIDE), floats(MEMBERS, 4, ZED, WIDE), floats(SUMS, 2, ZED, WIDE),
+        ),
+        compiler_params=PARAMS,
+        cost_estimate=busy,
+        name="prepare",
+    )(own_state, far_state, far_sides, near_state, near_sides, adjoint)
+
     far_earlier, part_resistance, part_conductivity = pl.pallas_call(
         far_adjoint_kernel,
         out_shape=(columns, cells, cells),
@@ -783,7 +827,7 @@
         compiler_params=PARAMS,
         cost_estimate=busy,
         name="far_adjoint",
-    )(own_state, far_state, far_sides, adjoint, part_resistance, part_conductivity, from_far)
+    )(terms, own_arrived, own_sums, far_sides, part_resistance, part_conductivity, from_far)
 
     return pl.pallas_call(
         near_adjoint_kernel,
@@ -792,7 +836,7 @@
         compiler_params=PARAMS,
         name="near_adjoint",
     )(
-        begin, own_state, near_state, near_sides, far_sides, adjoint, far_earlier,
+        begin, terms, own_arrived, own_sums, near_sides, far_sides, far_earlier,
         part_resistance, part_conductivity, from_near,
     )
 

time: 43.1 us -> 43.1 us (level)
  no operation moved by 1% of the time
where the time goes in v10:
time: 43.1 us; the launch traced here: 42.7 us
  starting transfers between devices  34 us (79%)
  Pallas kernels  5.73 us (13%)
  waiting for transfers between devices  1.11 us (3%)
  local copies, waits for them, and re-layouts  1.04 us (2%)
  between operations  0.79 us (2%)
    ppermute x4, starting transfers between devices, swap_along_x(): return (lax.ppermute(far, 'gx', across), lax.ppermute(near, 'gx', within))  25.7 us
    ppermute x1, starting transfers between devices, on_device(): lax.ppermute(down, 'gy', [(target, source) for source, target in upward])  4.37 us
    ppermute x1, starting transfers between devices, on_device(): from_below = lax.ppermute(up, 'gy', upward)  3.95 us
    pallas_call x1, Pallas kernels, on_device(): pl.pallas_call(first_kernel, in_specs=[in_hbm] * 7, out_specs=[in_hbm] *...  2.13 us
    pallas_call x1, Pallas kernels, on_device(): pl.pallas_call(step_kernel, out_shape=(columns, side_columns, columns, si...  1.3 us
    ppermute x4, waiting for transfers between devices, swap_along_x(): return (lax.ppermute(far, 'gx', across), lax.ppermute(near, 'gx', within))  1.1 us
    unnamed x6, local copies, waits for them, and re-layouts  1.04 us
    pallas_call x1, Pallas kernels, on_device(): pl.pallas_call(near_adjoint_kernel, out_shape=(cells, cells), scratch_sha...  0.96 us
  transfers between devices with their start and end apart: 6, of which 2 were waited for; matrix products, arithmetic and copies ran while one was open for 0% of the time, Pallas kernels for 2%

profile of v10, /device:TPU:1, one launch (start us, length us, event | category | flops | bytes accessed | tf_op | source)
XLA Modules:
  0.0 42.7 jit_solution(16084528314988071191)
XLA Ops:
  0.6 0.0 copy-start.2
  0.6 0.0 copy-start
  0.7 2.1 %collide_own.1 = (f32[64,16,128]{2,1,0:T(8,128)}, f32[2,16,128]{2,1,0:T(8,128)}, f32[2,16,128]{2,1,0:T(8,128)}) custom-call(f32[19,2,16,128]{3,2,1,0:T(8,128)} %flow.1, f32[7,2,16,128]{3,2,1,0:T(8,128)} %heat.1, f32[3,2,16,128]{3,2,1,0:T(8,128)} %flow_weight_in.1, f32[2,16,128]{2,1,0:T(8,128)} %heat_weight_in.1, f32[2,16,128]{2,1,0:T(8,128)} %resistance_in.1, ...), custom_call_target="tpu_custom_call" | custom-call | tf_op jit(solution)/shard_map/collide_own/pallas_call | solution.py:736
  2.8 3.9 %collective-permute-start = (f32[2,16,128]{2,1,0:T(8,128)}, f32[2,16,128]{2,1,0:T(8,128)S(1)}, u32[]{:S(2)}, u32[]{:S(2)}) collective-permute-start(f32[2,16,128]{2,1,0:T(8,128)} %get-tuple-element.27), channel_id=1, source_target_pairs={{0,1},{1,2},{2,3},{3,4},{4,5},{5,6},{6,7},{7,0},{8,9},{9,10},{10,1... | collective-permute-start | bytes 49160 | tf_op jit(solution)/shard_map/ppermute | solution.py:764
  6.7 4.4 %collective-permute-start.1 = (f32[2,16,128]{2,1,0:T(8,128)}, f32[2,16,128]{2,1,0:T(8,128)S(1)}, u32[]{:S(2)}, u32[]{:S(2)}) collective-permute-start(f32[2,16,128]{2,1,0:T(8,128)} %get-tuple-element.28), channel_id=1, source_target_pairs={{1,0},{2,1},{3,2},{4,3},{5,4},{6,5},{7,6},{0,7},{9,8},{10,9},{11,1... | collective-permute-start | bytes 49160 | tf_op jit(solution)/shard_map/ppermute | solution.py:765
  11.1 0.0 copy-start.1
  11.1 1.0 %copy-done.1 = f32[64,16,128]{2,1,0:T(8,128)S(1)} copy-done((f32[64,16,128]{2,1,0:T(8,128)S(1)}, f32[64,16,128]{2,1,0:T(8,128)}, u32[]{:S(2)}) %copy-start.1) | copy-done | bytes 524312
  12.2 0.0 collective-permute-done.from_below
  12.2 0.0 collective-permute-done.1.from_above
  12.2 0.3 halo_buffers.1
  12.5 5.1 %collective-permute-start.2 = (f32[29,16,128]{2,1,0:T(8,128)S(1)}, f32[29,16,128]{2,1,0:T(8,128)S(1)}, u32[]{:S(2)}, u32[]{:S(2)}) collective-permute-start(f32[29,16,128]{2,1,0:T(8,128)S(1)} %get-tuple-element.33), channel_id=1, source_target_pairs={{0,504},{8,16},{16,8},{24,32},{32,24},{40,48},{48,40},{56,64},{64,... | collective-permute-start | bytes 712712 | tf_op jit(solution)/shard_map/ppermute | solution.py:727
  17.7 10.7 %collective-permute-start.3 = (f32[29,16,128]{2,1,0:T(8,128)S(1)}, f32[29,16,128]{2,1,0:T(8,128)S(1)}, u32[]{:S(2)}, u32[]{:S(2)}) collective-permute-start(f32[29,16,128]{2,1,0:T(8,128)S(1)} %get-tuple-element.34), channel_id=1, source_target_pairs={{0,8},{8,0},{16,24},{24,16},{32,40},{40,32},{48,56},{56,48},{64,72... | collective-permute-start | bytes 712712 | tf_op jit(solution)/shard_map/ppermute | solution.py:727
  28.4 0.0 copy-done.2
  28.4 0.0 copy-done
  28.4 0.4 own_step.1
  28.8 0.0 collective-permute-done.2.from_far
  28.8 0.7 %collective-permute-done.3.from_near = f32[29,16,128]{2,1,0:T(8,128)S(1)} collective-permute-done((f32[29,16,128]{2,1,0:T(8,128)S(1)}, f32[29,16,128]{2,1,0:T(8,128)S(1)}, u32[]{:S(2)}, u32[]{:S(2)}) %collective-permute-start.3) | collective-permute-done | bytes 237600 | tf_op jit(solution)/shard_map/ppermute | solution.py:727
  29.5 1.3 %two_steps.1 = (f32[26,2,16,256]{3,2,1,0:T(8,128)S(1)}, f32[2,2,16,256]{3,2,1,0:T(8,128)S(1)}, f32[26,2,16,256]{3,2,1,0:T(8,128)S(1)}, f32[2,2,16,256]{3,2,1,0:T...) custom-call(f32[64,16,128]{2,1,0:T(8,128)S(1)} %stage_own.1.own, ...), custom_call_target="tpu_custom_call" | custom-call | tf_op jit(solution)/shard_map/two_steps/pallas_call | solution.py:799
  30.8 1.9 %collective-permute-start.4 = (f32[23,16,128]{2,1,0:T(8,128)S(1)}, f32[23,16,128]{2,1,0:T(8,128)S(1)}, u32[]{:S(2)}, u32[]{:S(2)}) collective-permute-start(f32[23,16,128]{2,1,0:T(8,128)S(1)} %get-tuple-element.45), channel_id=1, source_target_pairs={{0,504},{8,16},{16,8},{24,32},{32,24},{40,48},{48,40},{56,64},{64,... | collective-permute-start | bytes 565256 | tf_op jit(solution)/shard_map/ppermute | solution.py:727
  32.7 8.0 %collective-permute-start.5 = (f32[23,16,128]{2,1,0:T(8,128)S(1)}, f32[23,16,128]{2,1,0:T(8,128)S(1)}, u32[]{:S(2)}, u32[]{:S(2)}) collective-permute-start(f32[23,16,128]{2,1,0:T(8,128)S(1)} %get-tuple-element.49), channel_id=1, source_target_pairs={{0,8},{8,0},{16,24},{24,16},{32,40},{40,32},{48,56},{56,48},{64,72... | collective-permute-start | bytes 565256 | tf_op jit(solution)/shard_map/ppermute | solution.py:727
  40.7 0.3 prepare.1
  41.0 0.0 collective-permute-done.4.from_far
  41.0 0.2 far_adjoint.1
  41.3 0.4 %collective-permute-done.5.from_near = f32[23,16,128]{2,1,0:T(8,128)S(1)} collective-permute-done((f32[23,16,128]{2,1,0:T(8,128)S(1)}, f32[23,16,128]{2,1,0:T(8,128)S(1)}, u32[]{:S(2)}, u32[]{:S(2)}) %collective-permute-start.5) | collective-permute-done | bytes 188448 | tf_op jit(solution)/shard_map/ppermute | solution.py:727
  41.7 1.0 %near_adjoint.1 = (f32[2,16,128]{2,1,0:T(8,128)}, f32[2,16,128]{2,1,0:T(8,128)}) custom-call(f32[8,2,16,128]{3,2,1,0:T(8,128)S(1)} %get-tuple-element.30.begin, f32[15,4,16,256]{3,2,1,0:T(8,128)S(1)} %get-tuple-element.40.terms, f32[26,4,16,256]{3,2,1,0:T(8,128)S(1)} %get-tuple-element.41.own_arrived, f32[9,2,16,256]{3,2,1,0:T(8,128)S(1)} %get-tuple-element.42.own_sums, ...), custom_call_target="tpu_custom_call" | custom-call | tf_op jit(solution)/shard_map/near_adjoint/pallas_call | solution.py:832
  (1 shorter events, 0.0 us)
Async XLA Ops:
  0.6 27.7 %copy-start.2 = (f32[7,2,16,128]{3,2,1,0:T(8,128)S(1)}, f32[7,2,16,128]{3,2,1,0:T(8,128)}, u32[]{:S(2)}) copy-start(f32[7,2,16,128]{3,2,1,0:T(8,128)} %heat.1) | copy-start | bytes 344068
  0.6 27.7 %copy-start = (f32[19,2,16,128]{3,2,1,0:T(8,128)S(1)}, f32[19,2,16,128]{3,2,1,0:T(8,128)}, u32[]{:S(2)}) copy-start(f32[19,2,16,128]{3,2,1,0:T(8,128)} %flow.1) | copy-start | bytes 933892
  2.8 9.4 %collective-permute-start = (f32[2,16,128]{2,1,0:T(8,128)}, f32[2,16,128]{2,1,0:T(8,128)S(1)}, u32[]{:S(2)}, u32[]{:S(2)}) collective-permute-start(f32[2,16,128]{2,1,0:T(8,128)} %get-tuple-element.27), channel_id=1, source_target_pairs={{0,1},{1,2},{2,3},{3,4},{4,5},{5,6},{6,7},{7,0},{8,9},{9,10},{10,1... | collective-permute-start | bytes 49160 | tf_op jit(solution)/shard_map/ppermute | solution.py:764
  6.7 5.5 %collective-permute-start.1 = (f32[2,16,128]{2,1,0:T(8,128)}, f32[2,16,128]{2,1,0:T(8,128)S(1)}, u32[]{:S(2)}, u32[]{:S(2)}) collective-permute-start(f32[2,16,128]{2,1,0:T(8,128)} %get-tuple-element.28), channel_id=1, source_target_pairs={{1,0},{2,1},{3,2},{4,3},{5,4},{6,5},{7,6},{0,7},{9,8},{10,9},{11,1... | collective-permute-start | bytes 49160 | tf_op jit(solution)/shard_map/ppermute | solution.py:765
  11.1 1.0 %copy-start.1 = (f32[64,16,128]{2,1,0:T(8,128)S(1)}, f32[64,16,128]{2,1,0:T(8,128)}, u32[]{:S(2)}) copy-start(f32[64,16,128]{2,1,0:T(8,128)} %get-tuple-element.26.own) | copy-start | bytes 1572868
  12.5 16.2 %collective-permute-start.2 = (f32[29,16,128]{2,1,0:T(8,128)S(1)}, f32[29,16,128]{2,1,0:T(8,128)S(1)}, u32[]{:S(2)}, u32[]{:S(2)}) collective-permute-start(f32[29,16,128]{2,1,0:T(8,128)S(1)} %get-tuple-element.33), channel_id=1, source_target_pairs={{0,504},{8,16},{16,8},{24,32},{32,24},{40,48},{48,40},{56,64},{64,... | collective-permute-start | bytes 712712 | tf_op jit(solution)/shard_map/ppermute | solution.py:727
  17.7 11.8 %collective-permute-start.3 = (f32[29,16,128]{2,1,0:T(8,128)S(1)}, f32[29,16,128]{2,1,0:T(8,128)S(1)}, u32[]{:S(2)}, u32[]{:S(2)}) collective-permute-start(f32[29,16,128]{2,1,0:T(8,128)S(1)} %get-tuple-element.34), channel_id=1, source_target_pairs={{0,8},{8,0},{16,24},{24,16},{32,40},{40,32},{48,56},{56,48},{64,72... | collective-permute-start | bytes 712712 | tf_op jit(solution)/shard_map/ppermute | solution.py:727
  30.8 10.3 %collective-permute-start.4 = (f32[23,16,128]{2,1,0:T(8,128)S(1)}, f32[23,16,128]{2,1,0:T(8,128)S(1)}, u32[]{:S(2)}, u32[]{:S(2)}) collective-permute-start(f32[23,16,128]{2,1,0:T(8,128)S(1)} %get-tuple-element.45), channel_id=1, source_target_pairs={{0,504},{8,16},{16,8},{24,32},{32,24},{40,48},{48,40},{56,64},{64,... | collective-permute-start | bytes 565256 | tf_op jit(solution)/shard_map/ppermute | solution.py:727
  32.7 9.1 %collective-permute-start.5 = (f32[23,16,128]{2,1,0:T(8,128)S(1)}, f32[23,16,128]{2,1,0:T(8,128)S(1)}, u32[]{:S(2)}, u32[]{:S(2)}) collective-permute-start(f32[23,16,128]{2,1,0:T(8,128)S(1)} %get-tuple-element.49), channel_id=1, source_target_pairs={{0,8},{8,0},{16,24},{24,16},{32,40},{40,32},{48,56},{56,48},{64,72... | collective-permute-start | bytes 565256 | tf_op jit(solution)/shard_map/ppermute | solution.py:727

commit v11 on v10

--- a/solution.py
+++ b/solution.py
@@ -52,6 +52,7 @@
 SUMS = 9
 SUM_FIELDS = [FIELDS + k for k in range(SUMS)]
 
+ADJ_EDGE = 2
 SLOTS = LANES // (2 * EDGE)
 STRIP_ROWS = 2 * FIELDS // SLOTS
 HALF_ROWS = STRIP_ROWS // 2
@@ -68,11 +69,11 @@
 BULK_ROWS, ADJ_BULK = len(TO_NEAR), len(ADJ_TO_NEAR)
 
 
-def with_strips(bulk):
-    return bulk + -(-bulk // SLOTS)
-
-
-SENT, ADJ_SENT = with_strips(BULK_ROWS), with_strips(ADJ_BULK)
+def with_strips(bulk, edge):
+    return bulk + -(-bulk * 2 * edge // LANES)
+
+
+SENT, ADJ_SENT = with_strips(BULK_ROWS, EDGE), with_strips(ADJ_BULK, ADJ_EDGE)
 
 
 def level_sums(p):
@@ -284,22 +285,23 @@
     return pltpu.roll(value, by, axis) if by else value
 
 
-def side_by_side(parts):
+def side_by_side(parts, edge):
     lane = lax.broadcasted_iota(jnp.int32, (ZED, LANES), 1)
     row = None
     for slot, part in enumerate(parts):
-        row = part if row is None else jnp.where(lane >= 2 * EDGE * slot, part, row)
+        row = part if row is None else jnp.where(lane >= 2 * edge * slot, part, row)
     return row
 
 
-def packed(value, slot):
-    return turn(value, 2 * EDGE * slot + EDGE, 1)
-
-
-def pack_rows(parts):
+def packed(value, slot, edge=EDGE):
+    return turn(value, 2 * edge * slot + edge, 1)
+
+
+def pack_rows(parts, edge=EDGE):
+    slots = LANES // (2 * edge)
     return [
-        side_by_side([part(slot) for slot, part in enumerate(parts[start : start + SLOTS])])
-        for start in range(0, len(parts), SLOTS)
+        side_by_side([part(slot) for slot, part in enumerate(parts[start : start + slots])], edge)
+        for start in range(0, len(parts), slots)
     ]
 
 
@@ -328,8 +330,8 @@
     return value[:, :LANES], value[:, LANES:], 0
 
 
-def beside(row, slot):
-    return row, -EDGE - 2 * EDGE * slot
+def beside(row, slot, edge=EDGE):
+    return row, -edge - 2 * edge * slot
 
 
 def moved(triple, velocity, way):
@@ -362,8 +364,9 @@
     return (own[place],) + beside(strip[place // SLOTS], place % SLOTS)
 
 
-def halo_value(buffer, bulk, place):
-    return (buffer[place],) + beside(buffer[bulk + place // SLOTS], place % SLOTS)
+def halo_value(buffer, bulk, place, edge=EDGE):
+    slots = LANES // (2 * edge)
+    return (buffer[place],) + beside(buffer[bulk + place // slots], place % slots, edge)
 
 
 def given_state(flow, heat, odd, c, z):
@@ -586,11 +589,11 @@
         for (k, column), row in rows.items():
             if k >= FIELDS:
                 side[row] = sums[0][k - FIELDS]
-                parts.append(lambda slot, k=k: packed(sums[1][k - FIELDS], slot))
+                parts.append(lambda slot, k=k: packed(sums[1][k - FIELDS], slot, ADJ_EDGE))
             else:
                 side[row] = adjoint[k, column, :, :LANES]
-                parts.append(lambda slot, k=k, column=column: packed(adjoint[k, column, :, LANES:], slot))
-        for k, row in enumerate(pack_rows(parts)):
+                parts.append(lambda slot, k=k, column=column: packed(adjoint[k, column, :, LANES:], slot, ADJ_EDGE))
+        for k, row in enumerate(pack_rows(parts, ADJ_EDGE)):
             side[ADJ_BULK + k] = row
 
 
@@ -663,7 +666,7 @@
     arrived,
 ):
     def halo(k, column):
-        return halo_value(from_far, ADJ_BULK, far_place(ADJ_TO_FAR, k, column))
+        return halo_value(from_far, ADJ_BULK, far_place(ADJ_TO_FAR, k, column), ADJ_EDGE)
 
     def keep(z, resistance, conductivity):
         by_resistance[0, z, :] = part_resistance[0, z, :] + resistance
@@ -682,7 +685,7 @@
     arrived, earlier, last, sums,
 ):
     def halo(k, column):
-        return halo_value(from_near, ADJ_BULK, near_place(ADJ_TO_NEAR, k, column))
+        return halo_value(from_near, ADJ_BULK, near_place(ADJ_TO_NEAR, k, column), ADJ_EDGE)
 
     def keep(z, resistance, conductivity):
         sums[0, z, :] = part_resistance[1, z, :] + resistance

time: 43.1 us -> 43 us (level)
  no operation moved by 1% of the time
where the time goes in v11:
time: 43 us; the launch traced here: 42.7 us
  starting transfers between devices  34 us (79%)
  Pallas kernels  5.72 us (13%)
  waiting for transfers between devices  1.1 us (3%)
  local copies, waits for them, and re-layouts  1.04 us (2%)
  between operations  0.79 us (2%)
    ppermute x4, starting transfers between devices, swap_along_x(): return (lax.ppermute(far, 'gx', across), lax.ppermute(near, 'gx', within))  25.7 us
    ppermute x1, starting transfers between devices, on_device(): lax.ppermute(down, 'gy', [(target, source) for source, target in upward])  4.37 us
    ppermute x1, starting transfers between devices, on_device(): from_below = lax.ppermute(up, 'gy', upward)  3.95 us
    pallas_call x1, Pallas kernels, on_device(): pl.pallas_call(first_kernel, in_specs=[in_hbm] * 7, out_specs=[in_hbm] *...  2.13 us
    pallas_call x1, Pallas kernels, on_device(): pl.pallas_call(step_kernel, out_shape=(columns, side_columns, columns, si...  1.3 us
    ppermute x4, waiting for transfers between devices, swap_along_x(): return (lax.ppermute(far, 'gx', across), lax.ppermute(near, 'gx', within))  1.1 us
    unnamed x6, local copies, waits for them, and re-layouts  1.04 us
    pallas_call x1, Pallas kernels, on_device(): pl.pallas_call(near_adjoint_kernel, out_shape=(cells, cells), scratch_sha...  0.96 us
  transfers between devices with their start and end apart: 6, of which 2 were waited for; matrix products, arithmetic and copies ran while one was open for 0% of the time, Pallas kernels for 2%

profile of v11, /device:TPU:1, one launch (start us, length us, event | category | flops | bytes accessed | tf_op | source)
XLA Modules:
  0.0 42.7 jit_solution(15599494755277756172)
XLA Ops:
  0.6 0.0 copy-start.2
  0.6 0.0 copy-start
  0.7 2.1 %collide_own.1 = (f32[64,16,128]{2,1,0:T(8,128)}, f32[2,16,128]{2,1,0:T(8,128)}, f32[2,16,128]{2,1,0:T(8,128)}) custom-call(f32[19,2,16,128]{3,2,1,0:T(8,128)} %flow.1, f32[7,2,16,128]{3,2,1,0:T(8,128)} %heat.1, f32[3,2,16,128]{3,2,1,0:T(8,128)} %flow_weight_in.1, f32[2,16,128]{2,1,0:T(8,128)} %heat_weight_in.1, f32[2,16,128]{2,1,0:T(8,128)} %resistance_in.1, ...), custom_call_target="tpu_custom_call" | custom-call | tf_op jit(solution)/shard_map/collide_own/pallas_call | solution.py:739
  2.8 3.9 %collective-permute-start = (f32[2,16,128]{2,1,0:T(8,128)}, f32[2,16,128]{2,1,0:T(8,128)S(1)}, u32[]{:S(2)}, u32[]{:S(2)}) collective-permute-start(f32[2,16,128]{2,1,0:T(8,128)} %get-tuple-element.27), channel_id=1, source_target_pairs={{0,1},{1,2},{2,3},{3,4},{4,5},{5,6},{6,7},{7,0},{8,9},{9,10},{10,1... | collective-permute-start | bytes 49160 | tf_op jit(solution)/shard_map/ppermute | solution.py:767
  6.7 4.4 %collective-permute-start.1 = (f32[2,16,128]{2,1,0:T(8,128)}, f32[2,16,128]{2,1,0:T(8,128)S(1)}, u32[]{:S(2)}, u32[]{:S(2)}) collective-permute-start(f32[2,16,128]{2,1,0:T(8,128)} %get-tuple-element.28), channel_id=1, source_target_pairs={{1,0},{2,1},{3,2},{4,3},{5,4},{6,5},{7,6},{0,7},{9,8},{10,9},{11,1... | collective-permute-start | bytes 49160 | tf_op jit(solution)/shard_map/ppermute | solution.py:768
  11.1 0.0 copy-start.1
  11.1 1.0 %copy-done.1 = f32[64,16,128]{2,1,0:T(8,128)S(1)} copy-done((f32[64,16,128]{2,1,0:T(8,128)S(1)}, f32[64,16,128]{2,1,0:T(8,128)}, u32[]{:S(2)}) %copy-start.1) | copy-done | bytes 524312
  12.2 0.0 collective-permute-done.from_below
  12.2 0.0 collective-permute-done.1.from_above
  12.2 0.3 halo_buffers.1
  12.5 5.1 %collective-permute-start.2 = (f32[29,16,128]{2,1,0:T(8,128)S(1)}, f32[29,16,128]{2,1,0:T(8,128)S(1)}, u32[]{:S(2)}, u32[]{:S(2)}) collective-permute-start(f32[29,16,128]{2,1,0:T(8,128)S(1)} %get-tuple-element.33), channel_id=1, source_target_pairs={{0,504},{8,16},{16,8},{24,32},{32,24},{40,48},{48,40},{56,64},{64,... | collective-permute-start | bytes 712712 | tf_op jit(solution)/shard_map/ppermute | solution.py:730
  17.7 10.7 %collective-permute-start.3 = (f32[29,16,128]{2,1,0:T(8,128)S(1)}, f32[29,16,128]{2,1,0:T(8,128)S(1)}, u32[]{:S(2)}, u32[]{:S(2)}) collective-permute-start(f32[29,16,128]{2,1,0:T(8,128)S(1)} %get-tuple-element.34), channel_id=1, source_target_pairs={{0,8},{8,0},{16,24},{24,16},{32,40},{40,32},{48,56},{56,48},{64,72... | collective-permute-start | bytes 712712 | tf_op jit(solution)/shard_map/ppermute | solution.py:730
  28.4 0.0 copy-done.2
  28.4 0.0 copy-done
  28.4 0.4 own_step.1
  28.8 0.0 collective-permute-done.2.from_far
  28.8 0.7 %collective-permute-done.3.from_near = f32[29,16,128]{2,1,0:T(8,128)S(1)} collective-permute-done((f32[29,16,128]{2,1,0:T(8,128)S(1)}, f32[29,16,128]{2,1,0:T(8,128)S(1)}, u32[]{:S(2)}, u32[]{:S(2)}) %collective-permute-start.3) | collective-permute-done | bytes 237600 | tf_op jit(solution)/shard_map/ppermute | solution.py:730
  29.5 1.3 %two_steps.1 = (f32[26,2,16,256]{3,2,1,0:T(8,128)S(1)}, f32[2,2,16,256]{3,2,1,0:T(8,128)S(1)}, f32[26,2,16,256]{3,2,1,0:T(8,128)S(1)}, f32[2,2,16,256]{3,2,1,0:T...) custom-call(f32[64,16,128]{2,1,0:T(8,128)S(1)} %stage_own.1.own, ...), custom_call_target="tpu_custom_call" | custom-call | tf_op jit(solution)/shard_map/two_steps/pallas_call | solution.py:802
  30.8 1.9 %collective-permute-start.4 = (f32[22,16,128]{2,1,0:T(8,128)S(1)}, f32[22,16,128]{2,1,0:T(8,128)S(1)}, u32[]{:S(2)}, u32[]{:S(2)}) collective-permute-start(f32[22,16,128]{2,1,0:T(8,128)S(1)} %get-tuple-element.45), channel_id=1, source_target_pairs={{0,504},{8,16},{16,8},{24,32},{32,24},{40,48},{48,40},{56,64},{64,... | collective-permute-start | bytes 540680 | tf_op jit(solution)/shard_map/ppermute | solution.py:730
  32.7 8.0 %collective-permute-start.5 = (f32[22,16,128]{2,1,0:T(8,128)S(1)}, f32[22,16,128]{2,1,0:T(8,128)S(1)}, u32[]{:S(2)}, u32[]{:S(2)}) collective-permute-start(f32[22,16,128]{2,1,0:T(8,128)S(1)} %get-tuple-element.49), channel_id=1, source_target_pairs={{0,8},{8,0},{16,24},{24,16},{32,40},{40,32},{48,56},{56,48},{64,72... | collective-permute-start | bytes 540680 | tf_op jit(solution)/shard_map/ppermute | solution.py:730
  40.7 0.3 prepare.1
  41.0 0.0 collective-permute-done.4.from_far
  41.0 0.2 far_adjoint.1
  41.3 0.4 %collective-permute-done.5.from_near = f32[22,16,128]{2,1,0:T(8,128)S(1)} collective-permute-done((f32[22,16,128]{2,1,0:T(8,128)S(1)}, f32[22,16,128]{2,1,0:T(8,128)S(1)}, u32[]{:S(2)}, u32[]{:S(2)}) %collective-permute-start.5) | collective-permute-done | bytes 180256 | tf_op jit(solution)/shard_map/ppermute | solution.py:730
  41.7 1.0 %near_adjoint.1 = (f32[2,16,128]{2,1,0:T(8,128)}, f32[2,16,128]{2,1,0:T(8,128)}) custom-call(f32[8,2,16,128]{3,2,1,0:T(8,128)S(1)} %get-tuple-element.30.begin, f32[15,4,16,256]{3,2,1,0:T(8,128)S(1)} %get-tuple-element.40.terms, f32[26,4,16,256]{3,2,1,0:T(8,128)S(1)} %get-tuple-element.41.own_arrived, f32[9,2,16,256]{3,2,1,0:T(8,128)S(1)} %get-tuple-element.42.own_sums, ...), custom_call_target="tpu_custom_call" | custom-call | tf_op jit(solution)/shard_map/near_adjoint/pallas_call | solution.py:835
  (1 shorter events, 0.0 us)
Async XLA Ops:
  0.6 27.7 %copy-start.2 = (f32[7,2,16,128]{3,2,1,0:T(8,128)S(1)}, f32[7,2,16,128]{3,2,1,0:T(8,128)}, u32[]{:S(2)}) copy-start(f32[7,2,16,128]{3,2,1,0:T(8,128)} %heat.1) | copy-start | bytes 344068
  0.6 27.7 %copy-start = (f32[19,2,16,128]{3,2,1,0:T(8,128)S(1)}, f32[19,2,16,128]{3,2,1,0:T(8,128)}, u32[]{:S(2)}) copy-start(f32[19,2,16,128]{3,2,1,0:T(8,128)} %flow.1) | copy-start | bytes 933892
  2.8 9.4 %collective-permute-start = (f32[2,16,128]{2,1,0:T(8,128)}, f32[2,16,128]{2,1,0:T(8,128)S(1)}, u32[]{:S(2)}, u32[]{:S(2)}) collective-permute-start(f32[2,16,128]{2,1,0:T(8,128)} %get-tuple-element.27), channel_id=1, source_target_pairs={{0,1},{1,2},{2,3},{3,4},{4,5},{5,6},{6,7},{7,0},{8,9},{9,10},{10,1... | collective-permute-start | bytes 49160 | tf_op jit(solution)/shard_map/ppermute | solution.py:767
  6.7 5.5 %collective-permute-start.1 = (f32[2,16,128]{2,1,0:T(8,128)}, f32[2,16,128]{2,1,0:T(8,128)S(1)}, u32[]{:S(2)}, u32[]{:S(2)}) collective-permute-start(f32[2,16,128]{2,1,0:T(8,128)} %get-tuple-element.28), channel_id=1, source_target_pairs={{1,0},{2,1},{3,2},{4,3},{5,4},{6,5},{7,6},{0,7},{9,8},{10,9},{11,1... | collective-permute-start | bytes 49160 | tf_op jit(solution)/shard_map/ppermute | solution.py:768
  11.1 1.0 %copy-start.1 = (f32[64,16,128]{2,1,0:T(8,128)S(1)}, f32[64,16,128]{2,1,0:T(8,128)}, u32[]{:S(2)}) copy-start(f32[64,16,128]{2,1,0:T(8,128)} %get-tuple-element.26.own) | copy-start | bytes 1572868
  12.5 16.2 %collective-permute-start.2 = (f32[29,16,128]{2,1,0:T(8,128)S(1)}, f32[29,16,128]{2,1,0:T(8,128)S(1)}, u32[]{:S(2)}, u32[]{:S(2)}) collective-permute-start(f32[29,16,128]{2,1,0:T(8,128)S(1)} %get-tuple-element.33), channel_id=1, source_target_pairs={{0,504},{8,16},{16,8},{24,32},{32,24},{40,48},{48,40},{56,64},{64,... | collective-permute-start | bytes 712712 | tf_op jit(solution)/shard_map/ppermute | solution.py:730
  17.7 11.8 %collective-permute-start.3 = (f32[29,16,128]{2,1,0:T(8,128)S(1)}, f32[29,16,128]{2,1,0:T(8,128)S(1)}, u32[]{:S(2)}, u32[]{:S(2)}) collective-permute-start(f32[29,16,128]{2,1,0:T(8,128)S(1)} %get-tuple-element.34), channel_id=1, source_target_pairs={{0,8},{8,0},{16,24},{24,16},{32,40},{40,32},{48,56},{56,48},{64,72... | collective-permute-start | bytes 712712 | tf_op jit(solution)/shard_map/ppermute | solution.py:730
  30.8 10.3 %collective-permute-start.4 = (f32[22,16,128]{2,1,0:T(8,128)S(1)}, f32[22,16,128]{2,1,0:T(8,128)S(1)}, u32[]{:S(2)}, u32[]{:S(2)}) collective-permute-start(f32[22,16,128]{2,1,0:T(8,128)S(1)} %get-tuple-element.45), channel_id=1, source_target_pairs={{0,504},{8,16},{16,8},{24,32},{32,24},{40,48},{48,40},{56,64},{64,... | collective-permute-start | bytes 540680 | tf_op jit(solution)/shard_map/ppermute | solution.py:730
  32.7 9.0 %collective-permute-start.5 = (f32[22,16,128]{2,1,0:T(8,128)S(1)}, f32[22,16,128]{2,1,0:T(8,128)S(1)}, u32[]{:S(2)}, u32[]{:S(2)}) collective-permute-start(f32[22,16,128]{2,1,0:T(8,128)S(1)} %get-tuple-element.49), channel_id=1, source_target_pairs={{0,8},{8,0},{16,24},{24,16},{32,40},{40,32},{48,56},{56,48},{64,72... | collective-permute-start | bytes 540680 | tf_op jit(solution)/shard_map/ppermute | solution.py:730

commit v12 on v11

--- a/solution.py
+++ b/solution.py
@@ -430,30 +430,37 @@
     copy_rows(staged, own)
 
 
-def halo_kernel(own, from_below, from_above, far, near, strip):
+def halo_buffer(own, strip, side, rows, c):
+    level = {q: moved(own_value(own, strip, q, c), VELOCITY[q], 1) for q in LEVEL}
+    sums = [level_sums({q: level[q][t] for q in LEVEL}) for t in range(2)]
+    parts = []
+    for (k, column), row in rows.items():
+        if k >= FIELDS:
+            side[row] = sums[0][k - FIELDS]
+            parts.append(lambda slot, k=k: packed(sums[1][k - FIELDS], slot))
+        else:
+            place = own_row(k, column)
+            side[row] = own[place]
+            parts.append(
+                lambda slot, place=place: turn(
+                    strip[place // SLOTS], 2 * EDGE * (slot - place % SLOTS), 1
+                )
+            )
+    for k, row in enumerate(pack_rows(parts)):
+        side[BULK_ROWS + k] = row
+
+
+def far_halo_kernel(own, from_below, from_above, far, strip):
     low = low_lanes()
     for k in range(HALF_ROWS):
         under, over = from_below[k], from_above[k]
         strip[k] = jnp.where(low, under, turn(over, EDGE, 1))
         strip[k + HALF_ROWS] = jnp.where(low, turn(under, -EDGE, 1), over)
-    for side, rows, c in ((near, TO_NEAR, 1), (far, TO_FAR, 0)):
-        level = {q: moved(own_value(own, strip, q, c), VELOCITY[q], 1) for q in LEVEL}
-        sums = [level_sums({q: level[q][t] for q in LEVEL}) for t in range(2)]
-        parts = []
-        for (k, column), row in rows.items():
-            if k >= FIELDS:
-                side[row] = sums[0][k - FIELDS]
-                parts.append(lambda slot, k=k: packed(sums[1][k - FIELDS], slot))
-            else:
-                place = own_row(k, column)
-                side[row] = own[place]
-                parts.append(
-                    lambda slot, place=place: turn(
-                        strip[place // SLOTS], 2 * EDGE * (slot - place % SLOTS), 1
-                    )
-                )
-        for k, row in enumerate(pack_rows(parts)):
-            side[BULK_ROWS + k] = row
+    halo_buffer(own, strip, far, TO_FAR, 0)
+
+
+def near_halo_kernel(own, strip, near):
+    halo_buffer(own, strip, near, TO_NEAR, 1)
 
 
 def level_of(p, column, sums):
@@ -544,7 +551,7 @@
 
 def step_kernel(
     own, strip, own_state, own_seed, from_far, from_near,
-    far_state, far_sides, near_state, near_sides, adjoint, by_resistance, by_conductivity, far, near,
+    far_state, far_sides, near_state, near_sides, adjoint, by_resistance, by_conductivity, far,
     after, near_after, later, halo_seed,
 ):
     def wide(k, column):
@@ -582,19 +589,26 @@
                 by_resistance[c, z, :], by_conductivity[c, z, :] = result["by"]
             for q in range(MEMBERS):
                 adjoint[q, c, z, y] = result[q]
-    for side, rows, c in ((near, ADJ_TO_NEAR, 1), (far, ADJ_TO_FAR, 0)):
-        level = {q: moved(split(adjoint[q, c]), VELOCITY[q], -1) for q in LEVEL}
-        sums = [level_adjoint_sums({q: level[q][t] for q in LEVEL}) for t in range(2)]
-        parts = []
-        for (k, column), row in rows.items():
-            if k >= FIELDS:
-                side[row] = sums[0][k - FIELDS]
-                parts.append(lambda slot, k=k: packed(sums[1][k - FIELDS], slot, ADJ_EDGE))
-            else:
-                side[row] = adjoint[k, column, :, :LANES]
-                parts.append(lambda slot, k=k, column=column: packed(adjoint[k, column, :, LANES:], slot, ADJ_EDGE))
-        for k, row in enumerate(pack_rows(parts, ADJ_EDGE)):
-            side[ADJ_BULK + k] = row
+    adjoint_buffer(adjoint, far, ADJ_TO_FAR, 0)
+
+
+def adjoint_buffer(adjoint, side, rows, c):
+    level = {q: moved(split(adjoint[q, c]), VELOCITY[q], -1) for q in LEVEL}
+    sums = [level_adjoint_sums({q: level[q][t] for q in LEVEL}) for t in range(2)]
+    parts = []
+    for (k, column), row in rows.items():
+        if k >= FIELDS:
+            side[row] = sums[0][k - FIELDS]
+            parts.append(lambda slot, k=k: packed(sums[1][k - FIELDS], slot, ADJ_EDGE))
+        else:
+            side[row] = adjoint[k, column, :, :LANES]
+            parts.append(lambda slot, k=k, column=column: packed(adjoint[k, column, :, LANES:], slot, ADJ_EDGE))
+    for k, row in enumerate(pack_rows(parts, ADJ_EDGE)):
+        side[ADJ_BULK + k] = row
+
+
+def near_buffer_kernel(adjoint, near):
+    adjoint_buffer(adjoint, near, ADJ_TO_NEAR, 1)
 
 
 TERMS = 15
@@ -775,12 +789,18 @@
         name="stage_own",
     )(own)
 
-    far, near, strip = pl.pallas_call(
-        halo_kernel,
-        out_shape=(floats(SENT, ZED, LANES), floats(SENT, ZED, LANES), floats(STRIP_ROWS, ZED, LANES)),
+    far, strip = pl.pallas_call(
+        far_halo_kernel,
+        out_shape=(floats(SENT, ZED, LANES), floats(STRIP_ROWS, ZED, LANES)),
         compiler_params=PARAMS,
-        name="halo_buffers",
+        name="far_halo",
     )(own, from_below, from_above)
+    near = pl.pallas_call(
+        near_halo_kernel,
+        out_shape=floats(SENT, ZED, LANES),
+        compiler_params=PARAMS,
+        name="near_halo",
+    )(own, strip)
 
     from_far, from_near = swap_along_x(far, near)
 
@@ -798,18 +818,25 @@
         name="own_step",
     )(flow, heat, own, strip)
 
-    far_state, far_sides, near_state, near_sides, adjoint, part_resistance, part_conductivity, far, near = (
+    far_state, far_sides, near_state, near_sides, adjoint, part_resistance, part_conductivity, far = (
         pl.pallas_call(
             step_kernel,
             out_shape=(
                 columns, side_columns, columns, side_columns, columns, cells, cells,
-                floats(ADJ_SENT, ZED, LANES), floats(ADJ_SENT, ZED, LANES),
+                floats(ADJ_SENT, ZED, LANES),
             ),
             scratch_shapes=[held, held, held, held],
             compiler_params=PARAMS,
             name="two_steps",
         )(own, strip, own_state, own_seed, from_far, from_near)
     )
+
+    near = pl.pallas_call(
+        near_buffer_kernel,
+        out_shape=floats(ADJ_SENT, ZED, LANES),
+        compiler_params=PARAMS,
+        name="near_buffer",
+    )(adjoint)
 
     from_far, from_near = swap_along_x(far, near)
 

time: 43 us -> 43 us (level)
  transfers between devices with their start and end apart: 6 -> 6, of which waited for: 2 -> 2; matrix products, arithmetic and copies ran while one was open for 0% -> 0% of each run, Pallas kernels for 2% -> 3%
where the time goes in v12:
time: 43 us; the launch traced here: 42.7 us
  starting transfers between devices  33.8 us (79%)
  Pallas kernels  5.9 us (14%)
  waiting for transfers between devices  1.11 us (3%)
  local copies, waits for them, and re-layouts  1.04 us (2%)
  between operations  0.8 us (2%)
    ppermute x4, starting transfers between devices, swap_along_x(): return (lax.ppermute(far, 'gx', across), lax.ppermute(near, 'gx', within))  25.5 us
    ppermute x1, starting transfers between devices, on_device(): lax.ppermute(down, 'gy', [(target, source) for source, target in upward])  4.37 us
    ppermute x1, starting transfers between devices, on_device(): from_below = lax.ppermute(up, 'gy', upward)  3.95 us
    pallas_call x1, Pallas kernels, on_device(): pl.pallas_call(first_kernel, in_specs=[in_hbm] * 7, out_specs=[in_hbm] *...  2.12 us
    pallas_call x1, Pallas kernels, on_device(): pl.pallas_call(step_kernel, out_shape=(columns, side_columns, columns, si...  1.18 us
    ppermute x4, waiting for transfers between devices, swap_along_x(): return (lax.ppermute(far, 'gx', across), lax.ppermute(near, 'gx', within))  1.1 us
    unnamed x6, local copies, waits for them, and re-layouts  1.04 us
    pallas_call x1, Pallas kernels, on_device(): pl.pallas_call(near_adjoint_kernel, out_shape=(cells, cells), scratch_sha...  0.96 us
  transfers between devices with their start and end apart: 6, of which 2 were waited for; matrix products, arithmetic and copies ran while one was open for 0% of the time, Pallas kernels for 3%

profile of v12, /device:TPU:1, one launch (start us, length us, event | category | flops | bytes accessed | tf_op | source)
XLA Modules:
  0.0 42.7 jit_solution(10027930077623944014)
XLA Ops:
  0.6 0.0 copy-start
  0.6 0.0 copy-start.2
  0.7 2.1 %collide_own.1 = (f32[64,16,128]{2,1,0:T(8,128)}, f32[2,16,128]{2,1,0:T(8,128)}, f32[2,16,128]{2,1,0:T(8,128)}) custom-call(f32[19,2,16,128]{3,2,1,0:T(8,128)} %flow.1, f32[7,2,16,128]{3,2,1,0:T(8,128)} %heat.1, f32[3,2,16,128]{3,2,1,0:T(8,128)} %flow_weight_in.1, f32[2,16,128]{2,1,0:T(8,128)} %heat_weight_in.1, f32[2,16,128]{2,1,0:T(8,128)} %resistance_in.1, ...), custom_call_target="tpu_custom_call" | custom-call | tf_op jit(solution)/shard_map/collide_own/pallas_call | solution.py:753
  2.8 3.9 %collective-permute-start = (f32[2,16,128]{2,1,0:T(8,128)}, f32[2,16,128]{2,1,0:T(8,128)S(1)}, u32[]{:S(2)}, u32[]{:S(2)}) collective-permute-start(f32[2,16,128]{2,1,0:T(8,128)} %get-tuple-element.25), channel_id=1, source_target_pairs={{0,1},{1,2},{2,3},{3,4},{4,5},{5,6},{6,7},{7,0},{8,9},{9,10},{10,1... | collective-permute-start | bytes 49160 | tf_op jit(solution)/shard_map/ppermute | solution.py:781
  6.7 4.4 %collective-permute-start.1 = (f32[2,16,128]{2,1,0:T(8,128)}, f32[2,16,128]{2,1,0:T(8,128)S(1)}, u32[]{:S(2)}, u32[]{:S(2)}) collective-permute-start(f32[2,16,128]{2,1,0:T(8,128)} %get-tuple-element.26), channel_id=1, source_target_pairs={{1,0},{2,1},{3,2},{4,3},{5,4},{6,5},{7,6},{0,7},{9,8},{10,9},{11,1... | collective-permute-start | bytes 49160 | tf_op jit(solution)/shard_map/ppermute | solution.py:782
  11.1 0.0 copy-start.1
  11.1 1.0 %copy-done.1 = f32[64,16,128]{2,1,0:T(8,128)S(1)} copy-done((f32[64,16,128]{2,1,0:T(8,128)S(1)}, f32[64,16,128]{2,1,0:T(8,128)}, u32[]{:S(2)}) %copy-start.1) | copy-done | bytes 524312
  12.2 0.0 collective-permute-done.from_below
  12.2 0.0 collective-permute-done.1.from_above
  12.2 0.3 far_halo.1
  12.5 5.1 %collective-permute-start.2 = (f32[29,16,128]{2,1,0:T(8,128)S(1)}, f32[29,16,128]{2,1,0:T(8,128)S(1)}, u32[]{:S(2)}, u32[]{:S(2)}) collective-permute-start(f32[29,16,128]{2,1,0:T(8,128)S(1)} %get-tuple-element.31), channel_id=1, source_target_pairs={{0,504},{8,16},{16,8},{24,32},{32,24},{40,48},{48,40},{56,64},{64,... | collective-permute-start | bytes 712712 | tf_op jit(solution)/shard_map/ppermute | solution.py:744
  17.6 0.2 near_halo.1
  17.8 10.7 %collective-permute-start.3 = (f32[29,16,128]{2,1,0:T(8,128)S(1)}, f32[29,16,128]{2,1,0:T(8,128)S(1)}, u32[]{:S(2)}, u32[]{:S(2)}) collective-permute-start(f32[29,16,128]{2,1,0:T(8,128)S(1)} %near_halo.1), channel_id=1, source_target_pairs={{0,8},{8,0},{16,24},{24,16},{32,40},{40,32},{48,56},{56,48},{64,72... | collective-permute-start | bytes 712712 | tf_op jit(solution)/shard_map/ppermute | solution.py:744
  28.5 0.0 copy-done
  28.5 0.0 copy-done.2
  28.5 0.4 own_step.1
  28.9 0.0 collective-permute-done.2.from_far
  28.9 0.7 %collective-permute-done.3.from_near = f32[29,16,128]{2,1,0:T(8,128)S(1)} collective-permute-done((f32[29,16,128]{2,1,0:T(8,128)S(1)}, f32[29,16,128]{2,1,0:T(8,128)S(1)}, u32[]{:S(2)}, u32[]{:S(2)}) %collective-permute-start.3) | collective-permute-done | bytes 237600 | tf_op jit(solution)/shard_map/ppermute | solution.py:744
  29.6 1.2 %two_steps.1 = (f32[26,2,16,256]{3,2,1,0:T(8,128)S(1)}, f32[2,2,16,256]{3,2,1,0:T(8,128)S(1)}, f32[26,2,16,256]{3,2,1,0:T(8,128)S(1)}, f32[2,2,16,256]{3,2,1,0:T...) custom-call(f32[64,16,128]{2,1,0:T(8,128)S(1)} %stage_own.1.own, ...), custom_call_target="tpu_custom_call" | custom-call | tf_op jit(solution)/shard_map/two_steps/pallas_call | solution.py:822
  30.8 1.9 %collective-permute-start.4 = (f32[22,16,128]{2,1,0:T(8,128)S(1)}, f32[22,16,128]{2,1,0:T(8,128)S(1)}, u32[]{:S(2)}, u32[]{:S(2)}) collective-permute-start(f32[22,16,128]{2,1,0:T(8,128)S(1)} %get-tuple-element.42), channel_id=1, source_target_pairs={{0,504},{8,16},{16,8},{24,32},{32,24},{40,48},{48,40},{56,64},{64,... | collective-permute-start | bytes 540680 | tf_op jit(solution)/shard_map/ppermute | solution.py:744
  32.7 0.2 near_buffer.1
  32.9 7.8 %collective-permute-start.5 = (f32[22,16,128]{2,1,0:T(8,128)S(1)}, f32[22,16,128]{2,1,0:T(8,128)S(1)}, u32[]{:S(2)}, u32[]{:S(2)}) collective-permute-start(f32[22,16,128]{2,1,0:T(8,128)S(1)} %near_buffer.1), channel_id=1, source_target_pairs={{0,8},{8,0},{16,24},{24,16},{32,40},{40,32},{48,56},{56,48},{64,72... | collective-permute-start | bytes 540680 | tf_op jit(solution)/shard_map/ppermute | solution.py:744
  40.7 0.3 prepare.1
  41.0 0.0 collective-permute-done.4.from_far
  41.0 0.2 far_adjoint.1
  41.3 0.4 %collective-permute-done.5.from_near = f32[22,16,128]{2,1,0:T(8,128)S(1)} collective-permute-done((f32[22,16,128]{2,1,0:T(8,128)S(1)}, f32[22,16,128]{2,1,0:T(8,128)S(1)}, u32[]{:S(2)}, u32[]{:S(2)}) %collective-permute-start.5) | collective-permute-done | bytes 180256 | tf_op jit(solution)/shard_map/ppermute | solution.py:744
  41.7 1.0 %near_adjoint.1 = (f32[2,16,128]{2,1,0:T(8,128)}, f32[2,16,128]{2,1,0:T(8,128)}) custom-call(f32[8,2,16,128]{3,2,1,0:T(8,128)S(1)} %get-tuple-element.28.begin, f32[15,4,16,256]{3,2,1,0:T(8,128)S(1)} %get-tuple-element.37.terms, f32[26,4,16,256]{3,2,1,0:T(8,128)S(1)} %get-tuple-element.38.own_arrived, f32[9,2,16,256]{3,2,1,0:T(8,128)S(1)} %get-tuple-element.39.own_sums, ...), custom_call_target="tpu_custom_call" | custom-call | tf_op jit(solution)/shard_map/near_adjoint/pallas_call | solution.py:862
  (1 shorter events, 0.0 us)
Async XLA Ops:
  0.6 27.9 %copy-start = (f32[19,2,16,128]{3,2,1,0:T(8,128)S(1)}, f32[19,2,16,128]{3,2,1,0:T(8,128)}, u32[]{:S(2)}) copy-start(f32[19,2,16,128]{3,2,1,0:T(8,128)} %flow.1) | copy-start | bytes 933892
  0.6 27.9 %copy-start.2 = (f32[7,2,16,128]{3,2,1,0:T(8,128)S(1)}, f32[7,2,16,128]{3,2,1,0:T(8,128)}, u32[]{:S(2)}) copy-start(f32[7,2,16,128]{3,2,1,0:T(8,128)} %heat.1) | copy-start | bytes 344068
  2.8 9.4 %collective-permute-start = (f32[2,16,128]{2,1,0:T(8,128)}, f32[2,16,128]{2,1,0:T(8,128)S(1)}, u32[]{:S(2)}, u32[]{:S(2)}) collective-permute-start(f32[2,16,128]{2,1,0:T(8,128)} %get-tuple-element.25), channel_id=1, source_target_pairs={{0,1},{1,2},{2,3},{3,4},{4,5},{5,6},{6,7},{7,0},{8,9},{9,10},{10,1... | collective-permute-start | bytes 49160 | tf_op jit(solution)/shard_map/ppermute | solution.py:781
  6.7 5.5 %collective-permute-start.1 = (f32[2,16,128]{2,1,0:T(8,128)}, f32[2,16,128]{2,1,0:T(8,128)S(1)}, u32[]{:S(2)}, u32[]{:S(2)}) collective-permute-start(f32[2,16,128]{2,1,0:T(8,128)} %get-tuple-element.26), channel_id=1, source_target_pairs={{1,0},{2,1},{3,2},{4,3},{5,4},{6,5},{7,6},{0,7},{9,8},{10,9},{11,1... | collective-permute-start | bytes 49160 | tf_op jit(solution)/shard_map/ppermute | solution.py:782
  11.1 1.0 %copy-start.1 = (f32[64,16,128]{2,1,0:T(8,128)S(1)}, f32[64,16,128]{2,1,0:T(8,128)}, u32[]{:S(2)}) copy-start(f32[64,16,128]{2,1,0:T(8,128)} %get-tuple-element.24.own) | copy-start | bytes 1572868
  12.5 16.4 %collective-permute-start.2 = (f32[29,16,128]{2,1,0:T(8,128)S(1)}, f32[29,16,128]{2,1,0:T(8,128)S(1)}, u32[]{:S(2)}, u32[]{:S(2)}) collective-permute-start(f32[29,16,128]{2,1,0:T(8,128)S(1)} %get-tuple-element.31), channel_id=1, source_target_pairs={{0,504},{8,16},{16,8},{24,32},{32,24},{40,48},{48,40},{56,64},{64,... | collective-permute-start | bytes 712712 | tf_op jit(solution)/shard_map/ppermute | solution.py:744
  17.8 11.8 %collective-permute-start.3 = (f32[29,16,128]{2,1,0:T(8,128)S(1)}, f32[29,16,128]{2,1,0:T(8,128)S(1)}, u32[]{:S(2)}, u32[]{:S(2)}) collective-permute-start(f32[29,16,128]{2,1,0:T(8,128)S(1)} %near_halo.1), channel_id=1, source_target_pairs={{0,8},{8,0},{16,24},{24,16},{32,40},{40,32},{48,56},{56,48},{64,72... | collective-permute-start | bytes 712712 | tf_op jit(solution)/shard_map/ppermute | solution.py:744
  30.8 10.3 %collective-permute-start.4 = (f32[22,16,128]{2,1,0:T(8,128)S(1)}, f32[22,16,128]{2,1,0:T(8,128)S(1)}, u32[]{:S(2)}, u32[]{:S(2)}) collective-permute-start(f32[22,16,128]{2,1,0:T(8,128)S(1)} %get-tuple-element.42), channel_id=1, source_target_pairs={{0,504},{8,16},{16,8},{24,32},{32,24},{40,48},{48,40},{56,64},{64,... | collective-permute-start | bytes 540680 | tf_op jit(solution)/shard_map/ppermute | solution.py:744
  32.9 8.8 %collective-permute-start.5 = (f32[22,16,128]{2,1,0:T(8,128)S(1)}, f32[22,16,128]{2,1,0:T(8,128)S(1)}, u32[]{:S(2)}, u32[]{:S(2)}) collective-permute-start(f32[22,16,128]{2,1,0:T(8,128)S(1)} %near_buffer.1), channel_id=1, source_target_pairs={{0,8},{8,0},{16,24},{24,16},{32,40},{40,32},{48,56},{56,48},{64,72... | collective-permute-start | bytes 540680 | tf_op jit(solution)/shard_map/ppermute | solution.py:744

commit v13 on v12

--- a/solution.py
+++ b/solution.py
@@ -778,8 +778,8 @@
 
     count = lax.axis_size("gy")
     upward = [(i, (i + 1) % count) for i in range(count)]
+    from_above = lax.ppermute(down, "gy", [(target, source) for source, target in upward])
     from_below = lax.ppermute(up, "gy", upward)
-    from_above = lax.ppermute(down, "gy", [(target, source) for source, target in upward])
 
     own = pl.pallas_call(
         stage_kernel,

time: 43 us -> 43 us (level)
  no operation moved by 1% of the time
where the time goes in v13:
time: 43 us; the launch traced here: 42.7 us
  starting transfers between devices  33.8 us (79%)
  Pallas kernels  5.9 us (14%)
  waiting for transfers between devices  1.11 us (3%)
  local copies, waits for them, and re-layouts  1.04 us (2%)
  between operations  0.8 us (2%)
    ppermute x4, starting transfers between devices, swap_along_x(): return (lax.ppermute(far, 'gx', across), lax.ppermute(near, 'gx', within))  25.5 us
    ppermute x1, starting transfers between devices, on_device(): lax.ppermute(down, 'gy', [(target, source) for source, target in upward])  4.37 us
    ppermute x1, starting transfers between devices, on_device(): from_below = lax.ppermute(up, 'gy', upward)  3.95 us
    pallas_call x1, Pallas kernels, on_device(): pl.pallas_call(first_kernel, in_specs=[in_hbm] * 7, out_specs=[in_hbm] *...  2.12 us
    pallas_call x1, Pallas kernels, on_device(): pl.pallas_call(step_kernel, out_shape=(columns, side_columns, columns, si...  1.18 us
    ppermute x4, waiting for transfers between devices, swap_along_x(): return (lax.ppermute(far, 'gx', across), lax.ppermute(near, 'gx', within))  1.1 us
    unnamed x6, local copies, waits for them, and re-layouts  1.04 us
    pallas_call x1, Pallas kernels, on_device(): pl.pallas_call(near_adjoint_kernel, out_shape=(cells, cells), scratch_sha...  0.96 us
  transfers between devices with their start and end apart: 6, of which 2 were waited for; matrix products, arithmetic and copies ran while one was open for 0% of the time, Pallas kernels for 3%

profile of v13, /device:TPU:1, one launch (start us, length us, event | category | flops | bytes accessed | tf_op | source)
XLA Modules:
  0.0 42.7 jit_solution(10027930077623944014)
XLA Ops:
  0.6 0.0 copy-start
  0.6 0.0 copy-start.2
  0.7 2.1 %collide_own.1 = (f32[64,16,128]{2,1,0:T(8,128)}, f32[2,16,128]{2,1,0:T(8,128)}, f32[2,16,128]{2,1,0:T(8,128)}) custom-call(f32[19,2,16,128]{3,2,1,0:T(8,128)} %flow.1, f32[7,2,16,128]{3,2,1,0:T(8,128)} %heat.1, f32[3,2,16,128]{3,2,1,0:T(8,128)} %flow_weight_in.1, f32[2,16,128]{2,1,0:T(8,128)} %heat_weight_in.1, f32[2,16,128]{2,1,0:T(8,128)} %resistance_in.1, ...), custom_call_target="tpu_custom_call" | custom-call | tf_op jit(solution)/shard_map/collide_own/pallas_call | solution.py:753
  2.8 3.9 %collective-permute-start = (f32[2,16,128]{2,1,0:T(8,128)}, f32[2,16,128]{2,1,0:T(8,128)S(1)}, u32[]{:S(2)}, u32[]{:S(2)}) collective-permute-start(f32[2,16,128]{2,1,0:T(8,128)} %get-tuple-element.25), channel_id=1, source_target_pairs={{0,1},{1,2},{2,3},{3,4},{4,5},{5,6},{6,7},{7,0},{8,9},{9,10},{10,1... | collective-permute-start | bytes 49160 | tf_op jit(solution)/shard_map/ppermute | solution.py:782
  6.7 4.4 %collective-permute-start.1 = (f32[2,16,128]{2,1,0:T(8,128)}, f32[2,16,128]{2,1,0:T(8,128)S(1)}, u32[]{:S(2)}, u32[]{:S(2)}) collective-permute-start(f32[2,16,128]{2,1,0:T(8,128)} %get-tuple-element.26), channel_id=1, source_target_pairs={{1,0},{2,1},{3,2},{4,3},{5,4},{6,5},{7,6},{0,7},{9,8},{10,9},{11,1... | collective-permute-start | bytes 49160 | tf_op jit(solution)/shard_map/ppermute | solution.py:781
  11.1 0.0 copy-start.1
  11.1 1.0 %copy-done.1 = f32[64,16,128]{2,1,0:T(8,128)S(1)} copy-done((f32[64,16,128]{2,1,0:T(8,128)S(1)}, f32[64,16,128]{2,1,0:T(8,128)}, u32[]{:S(2)}) %copy-start.1) | copy-done | bytes 524312
  12.2 0.0 collective-permute-done.from_below
  12.2 0.0 collective-permute-done.1.from_above
  12.2 0.3 far_halo.1
  12.5 5.1 %collective-permute-start.2 = (f32[29,16,128]{2,1,0:T(8,128)S(1)}, f32[29,16,128]{2,1,0:T(8,128)S(1)}, u32[]{:S(2)}, u32[]{:S(2)}) collective-permute-start(f32[29,16,128]{2,1,0:T(8,128)S(1)} %get-tuple-element.31), channel_id=1, source_target_pairs={{0,504},{8,16},{16,8},{24,32},{32,24},{40,48},{48,40},{56,64},{64,... | collective-permute-start | bytes 712712 | tf_op jit(solution)/shard_map/ppermute | solution.py:744
  17.6 0.2 near_halo.1
  17.8 10.7 %collective-permute-start.3 = (f32[29,16,128]{2,1,0:T(8,128)S(1)}, f32[29,16,128]{2,1,0:T(8,128)S(1)}, u32[]{:S(2)}, u32[]{:S(2)}) collective-permute-start(f32[29,16,128]{2,1,0:T(8,128)S(1)} %near_halo.1), channel_id=1, source_target_pairs={{0,8},{8,0},{16,24},{24,16},{32,40},{40,32},{48,56},{56,48},{64,72... | collective-permute-start | bytes 712712 | tf_op jit(solution)/shard_map/ppermute | solution.py:744
  28.5 0.0 copy-done
  28.5 0.0 copy-done.2
  28.5 0.4 own_step.1
  28.9 0.0 collective-permute-done.2.from_far
  28.9 0.7 %collective-permute-done.3.from_near = f32[29,16,128]{2,1,0:T(8,128)S(1)} collective-permute-done((f32[29,16,128]{2,1,0:T(8,128)S(1)}, f32[29,16,128]{2,1,0:T(8,128)S(1)}, u32[]{:S(2)}, u32[]{:S(2)}) %collective-permute-start.3) | collective-permute-done | bytes 237600 | tf_op jit(solution)/shard_map/ppermute | solution.py:744
  29.6 1.2 %two_steps.1 = (f32[26,2,16,256]{3,2,1,0:T(8,128)S(1)}, f32[2,2,16,256]{3,2,1,0:T(8,128)S(1)}, f32[26,2,16,256]{3,2,1,0:T(8,128)S(1)}, f32[2,2,16,256]{3,2,1,0:T...) custom-call(f32[64,16,128]{2,1,0:T(8,128)S(1)} %stage_own.1.own, ...), custom_call_target="tpu_custom_call" | custom-call | tf_op jit(solution)/shard_map/two_steps/pallas_call | solution.py:822
  30.8 1.9 %collective-permute-start.4 = (f32[22,16,128]{2,1,0:T(8,128)S(1)}, f32[22,16,128]{2,1,0:T(8,128)S(1)}, u32[]{:S(2)}, u32[]{:S(2)}) collective-permute-start(f32[22,16,128]{2,1,0:T(8,128)S(1)} %get-tuple-element.42), channel_id=1, source_target_pairs={{0,504},{8,16},{16,8},{24,32},{32,24},{40,48},{48,40},{56,64},{64,... | collective-permute-start | bytes 540680 | tf_op jit(solution)/shard_map/ppermute | solution.py:744
  32.7 0.2 near_buffer.1
  32.9 7.8 %collective-permute-start.5 = (f32[22,16,128]{2,1,0:T(8,128)S(1)}, f32[22,16,128]{2,1,0:T(8,128)S(1)}, u32[]{:S(2)}, u32[]{:S(2)}) collective-permute-start(f32[22,16,128]{2,1,0:T(8,128)S(1)} %near_buffer.1), channel_id=1, source_target_pairs={{0,8},{8,0},{16,24},{24,16},{32,40},{40,32},{48,56},{56,48},{64,72... | collective-permute-start | bytes 540680 | tf_op jit(solution)/shard_map/ppermute | solution.py:744
  40.7 0.3 prepare.1
  41.0 0.0 collective-permute-done.4.from_far
  41.0 0.2 far_adjoint.1
  41.3 0.4 %collective-permute-done.5.from_near = f32[22,16,128]{2,1,0:T(8,128)S(1)} collective-permute-done((f32[22,16,128]{2,1,0:T(8,128)S(1)}, f32[22,16,128]{2,1,0:T(8,128)S(1)}, u32[]{:S(2)}, u32[]{:S(2)}) %collective-permute-start.5) | collective-permute-done | bytes 180256 | tf_op jit(solution)/shard_map/ppermute | solution.py:744
  41.7 1.0 %near_adjoint.1 = (f32[2,16,128]{2,1,0:T(8,128)}, f32[2,16,128]{2,1,0:T(8,128)}) custom-call(f32[8,2,16,128]{3,2,1,0:T(8,128)S(1)} %get-tuple-element.28.begin, f32[15,4,16,256]{3,2,1,0:T(8,128)S(1)} %get-tuple-element.37.terms, f32[26,4,16,256]{3,2,1,0:T(8,128)S(1)} %get-tuple-element.38.own_arrived, f32[9,2,16,256]{3,2,1,0:T(8,128)S(1)} %get-tuple-element.39.own_sums, ...), custom_call_target="tpu_custom_call" | custom-call | tf_op jit(solution)/shard_map/near_adjoint/pallas_call | solution.py:862
  (1 shorter events, 0.0 us)
Async XLA Ops:
  0.6 27.9 %copy-start = (f32[19,2,16,128]{3,2,1,0:T(8,128)S(1)}, f32[19,2,16,128]{3,2,1,0:T(8,128)}, u32[]{:S(2)}) copy-start(f32[19,2,16,128]{3,2,1,0:T(8,128)} %flow.1) | copy-start | bytes 933892
  0.6 27.9 %copy-start.2 = (f32[7,2,16,128]{3,2,1,0:T(8,128)S(1)}, f32[7,2,16,128]{3,2,1,0:T(8,128)}, u32[]{:S(2)}) copy-start(f32[7,2,16,128]{3,2,1,0:T(8,128)} %heat.1) | copy-start | bytes 344068
  2.8 9.4 %collective-permute-start = (f32[2,16,128]{2,1,0:T(8,128)}, f32[2,16,128]{2,1,0:T(8,128)S(1)}, u32[]{:S(2)}, u32[]{:S(2)}) collective-permute-start(f32[2,16,128]{2,1,0:T(8,128)} %get-tuple-element.25), channel_id=1, source_target_pairs={{0,1},{1,2},{2,3},{3,4},{4,5},{5,6},{6,7},{7,0},{8,9},{9,10},{10,1... | collective-permute-start | bytes 49160 | tf_op jit(solution)/shard_map/ppermute | solution.py:782
  6.7 5.5 %collective-permute-start.1 = (f32[2,16,128]{2,1,0:T(8,128)}, f32[2,16,128]{2,1,0:T(8,128)S(1)}, u32[]{:S(2)}, u32[]{:S(2)}) collective-permute-start(f32[2,16,128]{2,1,0:T(8,128)} %get-tuple-element.26), channel_id=1, source_target_pairs={{1,0},{2,1},{3,2},{4,3},{5,4},{6,5},{7,6},{0,7},{9,8},{10,9},{11,1... | collective-permute-start | bytes 49160 | tf_op jit(solution)/shard_map/ppermute | solution.py:781
  11.1 1.0 %copy-start.1 = (f32[64,16,128]{2,1,0:T(8,128)S(1)}, f32[64,16,128]{2,1,0:T(8,128)}, u32[]{:S(2)}) copy-start(f32[64,16,128]{2,1,0:T(8,128)} %get-tuple-element.24.own) | copy-start | bytes 1572868
  12.5 16.4 %collective-permute-start.2 = (f32[29,16,128]{2,1,0:T(8,128)S(1)}, f32[29,16,128]{2,1,0:T(8,128)S(1)}, u32[]{:S(2)}, u32[]{:S(2)}) collective-permute-start(f32[29,16,128]{2,1,0:T(8,128)S(1)} %get-tuple-element.31), channel_id=1, source_target_pairs={{0,504},{8,16},{16,8},{24,32},{32,24},{40,48},{48,40},{56,64},{64,... | collective-permute-start | bytes 712712 | tf_op jit(solution)/shard_map/ppermute | solution.py:744
  17.8 11.8 %collective-permute-start.3 = (f32[29,16,128]{2,1,0:T(8,128)S(1)}, f32[29,16,128]{2,1,0:T(8,128)S(1)}, u32[]{:S(2)}, u32[]{:S(2)}) collective-permute-start(f32[29,16,128]{2,1,0:T(8,128)S(1)} %near_halo.1), channel_id=1, source_target_pairs={{0,8},{8,0},{16,24},{24,16},{32,40},{40,32},{48,56},{56,48},{64,72... | collective-permute-start | bytes 712712 | tf_op jit(solution)/shard_map/ppermute | solution.py:744
  30.8 10.3 %collective-permute-start.4 = (f32[22,16,128]{2,1,0:T(8,128)S(1)}, f32[22,16,128]{2,1,0:T(8,128)S(1)}, u32[]{:S(2)}, u32[]{:S(2)}) collective-permute-start(f32[22,16,128]{2,1,0:T(8,128)S(1)} %get-tuple-element.42), channel_id=1, source_target_pairs={{0,504},{8,16},{16,8},{24,32},{32,24},{40,48},{48,40},{56,64},{64,... | collective-permute-start | bytes 540680 | tf_op jit(solution)/shard_map/ppermute | solution.py:744
  32.9 8.8 %collective-permute-start.5 = (f32[22,16,128]{2,1,0:T(8,128)S(1)}, f32[22,16,128]{2,1,0:T(8,128)S(1)}, u32[]{:S(2)}, u32[]{:S(2)}) collective-permute-start(f32[22,16,128]{2,1,0:T(8,128)S(1)} %near_buffer.1), channel_id=1, source_target_pairs={{0,8},{8,0},{16,24},{24,16},{32,40},{40,32},{48,56},{56,48},{64,72... | collective-permute-start | bytes 540680 | tf_op jit(solution)/shard_map/ppermute | solution.py:744
